TPU v7x, 128 devices: a whole 4x4x4 slice. The times are simulated.
128 devices in a mesh: ep: 32 (over y, x, core), tp: 4 (over z).
Axes of the slice: x: 4, y: 4, z: 4, core: 2. Of those that a mesh axis runs over, the one named last changes fastest.
Arguments:
- queries: bfloat16 [512, 128, 576], P(('ep', 'tp')), may hold values from -45 to 45
- kv_cache: bfloat16 [512, 512, 576], P(('ep', 'tp')), may hold values from -5 to 5
- new_latent: bfloat16 [512, 576], P(('ep', 'tp')), may hold values from -5 to 5
- lengths: int32 [512], P(('ep', 'tp')), may hold values from 2 to 512, as said below
- residual: bfloat16 [512, 7168], P('ep', 'tp'), may hold values from -6 to 6
- gain_first: bfloat16 [7168], P('tp'), may hold values from 0.099609375 to 1.8984375
- gain_second: bfloat16 [7168], P('tp'), may hold values from 0.099609375 to 1.8984375
- value_proj: bfloat16 [128, 512, 128], P('ep'), may hold values from -0.25 to 0.25
- out_proj: bfloat16 [16384, 7168], P('ep', 'tp'), may hold values from -0.046875 to 0.046875
- dense_gate: bfloat16 [7168, 12288], P('tp', 'ep'), may hold values from -0.0625 to 0.0625
- dense_up: bfloat16 [7168, 12288], P('tp', 'ep'), may hold values from -0.0625 to 0.0625
- dense_down: bfloat16 [12288, 7168], P('ep', 'tp'), may hold values from -0.0546875 to 0.0546875
- route_ids: int32 [512, 8], P('ep'), may hold values from 0 to 31, all different within a row; in each aligned block of 16 rows (0 to 15, 16 to 31, ...) at most 6 rows name the same one
- route_gates: float32 [512, 8], P('ep'), may hold values from 0.1 to 0.6
- expert_gate: bfloat16 [32, 7168, 1024], P('ep', None, 'tp'), may hold values from -0.0625 to 0.0625
- expert_up: bfloat16 [32, 7168, 1024], P('ep', None, 'tp'), may hold values from -0.0625 to 0.0625
- expert_down: bfloat16 [32, 1024, 7168], P('ep', 'tp'), may hold values from -0.1875 to 0.1875
Outputs:
- hidden_out: bfloat16 [512, 7168], P('ep', 'tp')
Inputs may be any that keep to these rules, and one draw needn't show every extreme that they name: `lengths`: each device's first request has all 512 slots live. `route_ids`: in each aligned block of 16 rows no expert is named by more than 6 rows.
All inputs are finite; a program needn't handle non-finite values.
Results may differ from a plain program's by a relative error of at most 0.024.
Values may be sent and summed in bfloat16 or wider, within the bound.
No kernel may reach another device: no remote copies, remote signals or barrier semaphores. Data moves between devices by JAX's collectives and lax.ppermute only.
A program may use at most 128 MiB of HBM per device.

v0:
```python
import jax
import jax.numpy as jnp
from jax import lax
from jax.sharding import PartitionSpec as P

D = 7168
ROPE = 64
VD = 128


EPS = 1e-06


def norm_apply(values, total, gain):
    scale_rows = lax.rsqrt(total / D + EPS)
    return (values * scale_rows[:, None] * gain.astype(jnp.float32)).astype(jnp.bfloat16)


def shards(
    queries,
    kv_cache,
    new_latent,
    lengths,
    residual,
    gain_first,
    gain_second,
    value_proj,
    out_proj,
    dense_gate,
    dense_up,
    dense_down,
    route_ids,
    route_gates,
    expert_gate,
    expert_up,
    expert_down,
):
    group_count = lax.axis_size("ep")
    score_scale = (VD + ROPE) ** (-0.5)
    latent_dim = value_proj.shape[1]
    slot_count = kv_cache.shape[1]
    req_dev = queries.shape[0]
    scores = (
        jnp.einsum("rhc,rjc->rhj", queries, kv_cache, preferred_element_type=jnp.float32)
        * score_scale
    )
    self_score = (
        jnp.einsum("rhc,rc->rh", queries, new_latent, preferred_element_type=jnp.float32)
        * score_scale
    )
    live_mask = lax.broadcasted_iota(jnp.int32, (1, slot_count), 1) < lengths[:, None]
    scores = jnp.where(live_mask[:, None, :], scores, -jnp.inf)
    top_score = jnp.maximum(jnp.max(scores, axis=-1), self_score)
    expo = jnp.exp(scores - top_score[..., None])
    self_expo = jnp.exp(self_score - top_score)
    total = jnp.sum(expo, axis=-1) + self_expo
    weights = (expo / total[..., None]).astype(jnp.bfloat16)
    self_weight = (self_expo / total).astype(jnp.bfloat16)
    latent = jnp.einsum(
        "rhj,rjc->rhc", weights, kv_cache[:, :, :latent_dim], preferred_element_type=jnp.float32
    )
    latent = latent + self_weight.astype(jnp.float32)[..., None] * new_latent[
        :, None, :latent_dim
    ].astype(jnp.float32)
    latent = latent.astype(jnp.bfloat16)
    moved = lax.all_to_all(latent, "ep", split_axis=1, concat_axis=0, tiled=True)
    head_vals = jnp.einsum(
        "rhc,hcv->rhv", moved, value_proj, preferred_element_type=jnp.float32
    ).astype(jnp.bfloat16)
    head_vals = head_vals.reshape(group_count, req_dev, -1)
    all_vals = lax.all_gather(head_vals, "tp", axis=1, tiled=True)
    all_vals = all_vals.reshape(-1, all_vals.shape[2])
    tok_group = residual.shape[0]
    rows = all_vals
    attn_out = lax.psum_scatter(
        jnp.dot(rows, out_proj, preferred_element_type=jnp.float32).astype(jnp.bfloat16),
        "ep",
        scatter_dimension=0,
        tiled=True,
    ).astype(jnp.float32)
    first = residual.astype(jnp.float32) + attn_out
    first_total = lax.psum(jnp.sum(first * first, axis=-1), "tp")
    normed = norm_apply(first, first_total, gain_first)
    piece = lax.all_gather(normed, "ep", axis=0, tiled=True)
    partial_sums = jnp.concatenate(
        [
            jnp.dot(piece, dense_gate, preferred_element_type=jnp.float32),
            jnp.dot(piece, dense_up, preferred_element_type=jnp.float32),
        ],
        axis=1,
    )
    width = dense_gate.shape[1]
    summed = lax.psum(partial_sums.astype(jnp.bfloat16), "tp").astype(jnp.float32)
    hidden = (jax.nn.silu(summed[:, :width]) * summed[:, width:]).astype(jnp.bfloat16)
    rows = hidden
    second = first + lax.psum_scatter(
        jnp.dot(rows, dense_down, preferred_element_type=jnp.float32).astype(jnp.bfloat16),
        "ep",
        scatter_dimension=0,
        tiled=True,
    ).astype(jnp.float32)
    second_total = lax.psum(jnp.sum(second * second, axis=-1), "tp")
    normed_b = norm_apply(second, second_total, gain_second)
    top_count = route_ids.shape[1]
    capacity = min(tok_group, 3 * tok_group * top_count // (2 * group_count))
    flat_ids = route_ids.reshape(-1)
    onehot = (flat_ids[:, None] == lax.broadcasted_iota(jnp.int32, (1, group_count), 1)).astype(
        jnp.int32
    )
    before = jnp.cumsum(onehot, axis=0) - onehot
    slot = jnp.sum(before * onehot, axis=1)
    position = (flat_ids * capacity + slot).reshape(tok_group, top_count)
    columns = lax.broadcasted_iota(jnp.int32, (1, 1, group_count * capacity), 2)
    matches = position[:, :, None] == columns
    pick_matrix = jnp.sum(matches.astype(jnp.int32), axis=1).astype(jnp.bfloat16)
    combine_matrix = jnp.sum(jnp.where(matches, route_gates[:, :, None], 0.0), axis=1)
    full_rows = lax.all_gather(normed_b, "tp", axis=1, tiled=True)
    sendbuf = jnp.einsum(
        "tp,td->pd", pick_matrix, full_rows, preferred_element_type=jnp.float32
    ).astype(jnp.bfloat16)
    sendbuf = sendbuf.reshape(group_count, capacity, -1)
    arrived = lax.all_to_all(sendbuf, "ep", split_axis=0, concat_axis=0, tiled=True)
    expert_rows = arrived.reshape(-1, arrived.shape[2])
    gate_act = jnp.dot(expert_rows, expert_gate[0], preferred_element_type=jnp.float32)
    up_act = jnp.dot(expert_rows, expert_up[0], preferred_element_type=jnp.float32)
    expert_hidden = (jax.nn.silu(gate_act) * up_act).astype(jnp.bfloat16)
    expert_partial = jnp.dot(expert_hidden, expert_down[0], preferred_element_type=jnp.float32)
    expert_result = lax.psum_scatter(
        expert_partial.astype(jnp.bfloat16), "tp", scatter_dimension=1, tiled=True
    )
    returned = lax.all_to_all(
        expert_result.reshape(group_count, capacity, -1),
        "ep",
        split_axis=0,
        concat_axis=0,
        tiled=True,
    )
    returned = returned.reshape(group_count * capacity, -1).astype(jnp.float32)
    moe_out = jnp.dot(combine_matrix, returned, precision=lax.Precision.HIGHEST)
    return (second + moe_out).astype(jnp.bfloat16)


def solution(mesh):
    return jax.shard_map(
        shards,
        mesh=mesh,
        in_specs=(
            P(("ep", "tp"), None, None),
            P(("ep", "tp"), None, None),
            P(("ep", "tp"), None),
            P(("ep", "tp")),
            P("ep", "tp"),
            P("tp"),
            P("tp"),
            P("ep", None, None),
            P("ep", "tp"),
            P("tp", "ep"),
            P("tp", "ep"),
            P("ep", "tp"),
            P("ep", None),
            P("ep", None),
            P("ep", None, "tp"),
            P("ep", None, "tp"),
            P("ep", "tp", None),
        ),
        out_specs=P("ep", "tp"),
        check_vma=False,
    )
```

profile of v0, /device:TPU:1, one launch (start us, length us, event | category | flops | bytes accessed | tf_op | source)
XLA Modules:
  0.0 479.8 jit_solution(10325917153971746656)
XLA Ops:
  9.4 2.7 fusion.44
  13.7 19.9 %all_to_all.28 = bf16[4,128,512]{2,0,1:T(4,128)(2,1)S(1)} all-to-all(bf16[4,128,512]{2,0,1:T(4,128)(2,1)S(1)} %copy.47), channel_id=1, replica_groups=mesh['ep'=32,'tp'=4] {'ep'}, dimensions={1} | all-to-all | bytes 1048576 | tf_op jit(solution)/shard_map/all_to_all | solution.py:66
  34.5 12.6 %all_gather.9 = bf16[32,16,512]{2,0,1:T(8,128)(2,1)S(1)} all-gather(bf16[32,4,512]{2,0,1:T(8,128)(2,1)S(1)} %copy.50), channel_id=1, replica_groups=mesh['ep'=32,'tp'=4] {'tp'}, dimensions={1}, use_global_device_ids=true | all-gather | bytes 655360 | tf_op jit(solution)/shard_map/all_gather | solution.py:71
  47.4 2.4 convolution_convert_fusion.3
  49.9 76.2 %reduce-scatter.4.cloned.1.call-done = bf16[16,1792]{1,0:T(8,128)(2,1)} async-done(((bf16[512,1792]{1,0:T(8,128)(2,1)}), bf16[16,1792]{1,0:T(8,128)(2,1)}) %reduce-scatter.4.cloned.1.call-update) | async-done | bytes 57360 | tf_op jit(solution)/shard_map/reduce_scatter | solution.py:75
  127.0 8.7 %psum.21 = f32[16]{0:T(128)S(1)} all-reduce(f32[16]{0:T(128)S(1)} %multiply_reduce_fusion.1), channel_id=1, replica_groups=mesh['ep'=32,'tp'=4] {'tp'}, use_global_device_ids=true, to_apply=%region_4.5 | all-reduce | flops 16 | bytes 128 | tf_op jit(solution)/shard_map/psum | solution.py:82
  137.3 44.6 %all-gather.2.cloned.1.call-done = bf16[512,1792]{1,0:T(8,128)(2,1)} async-done(((bf16[16,1792]{1,0:T(8,128)(2,1)}), bf16[512,1792]{1,0:T(8,128)(2,1)}) %all-gather.2.cloned.1.call-update) | async-done | bytes 1835024 | tf_op jit(solution)/shard_map/all_gather | solution.py:84
  182.0 2.6 convolution_convert_fusion.4
  186.5 42.0 %all-reduce.2.cloned.1.call-done = bf16[512,768]{0,1:T(8,128)(2,1)} async-done(((bf16[512,768]{0,1:T(8,128)(2,1)}), bf16[512,768]{0,1:T(8,128)(2,1)}) %all-reduce.2.cloned.1.call-update) | async-done | bytes 786448 | tf_op jit(solution)/shard_map/psum | solution.py:93
  229.9 3.8 convolution_convert_fusion.2
  234.6 78.4 %reduce-scatter.6.cloned.1.call-done = bf16[16,1792]{1,0:T(8,128)(2,1)} async-done(((bf16[512,1792]{1,0:T(8,128)(2,1)}), bf16[16,1792]{1,0:T(8,128)(2,1)}) %reduce-scatter.6.cloned.1.call-update) | async-done | bytes 57360 | tf_op jit(solution)/shard_map/reduce_scatter | solution.py:96
  314.0 8.7 %psum.23 = f32[16]{0:T(128)S(1)} all-reduce(f32[16]{0:T(128)S(1)} %multiply_reduce_fusion), channel_id=1, replica_groups=mesh['ep'=32,'tp'=4] {'tp'}, use_global_device_ids=true, to_apply=%region_12.13 | all-reduce | flops 16 | bytes 128 | tf_op jit(solution)/shard_map/psum | solution.py:102
  323.6 9.9 %all_gather.11 = bf16[16,7168]{1,0:T(8,128)(2,1)S(1)} all-gather(bf16[16,1792]{1,0:T(8,128)(2,1)S(1)} %multiply_convert_fusion), channel_id=1, replica_groups=mesh['ep'=32,'tp'=4] {'tp'}, dimensions={1}, use_global_device_ids=true | all-gather | bytes 286720 | tf_op jit(solution)/shard_map/all_gather | solution.py:117
  333.5 2.4 convolution_convert_fusion.1
  335.9 4.6 reshape.55
  340.5 56.9 %all_to_all.29 = bf16[32,6,7168]{2,1,0:T(8,128)(2,1)} all-to-all(bf16[32,6,7168]{2,1,0:T(8,128)(2,1)} %reshape.55), channel_id=1, replica_groups=mesh['ep'=32,'tp'=4] {'ep'}, dimensions={0} | all-to-all | bytes 5505024 | tf_op jit(solution)/shard_map/all_to_all | solution.py:122
  397.5 4.6 reshape.56
  402.1 3.8 fusion.3
  405.9 8.6 %convolution_convert_fusion = bf16[192,7168]{1,0:T(8,128)(2,1)} fusion(bf16[1,256,7168]{2,1,0:T(8,128)(2,1)} %param.33, bf16[192,7168]{1,0:T(8,128)(2,1)} %reshape.56, bf16[1,7168,256]{2,1,0:T(8,128)(2,1)} %param.32, f32[192,256]{1,0:T(8,128)S(1)} %fusion.3), kind=kOutput, calls=%fused_computation | convolution fusion | flops 1410957312 | bytes 13041664 | tf_op jit(solution)/shard_map/dot_general | solution.py:127
  414.5 31.3 %reduce-scatter.8.cloned.1.call-done = bf16[192,1792]{1,0:T(8,128)(2,1)} async-done(((bf16[192,7168]{1,0:T(8,128)(2,1)}), bf16[192,1792]{1,0:T(8,128)(2,1)}) %reduce-scatter.8.cloned.1.call-update) | async-done | bytes 688144 | tf_op jit(solution)/shard_map/reduce_scatter | solution.py:128
  445.8 2.1 reshape.57
  447.9 7.5 %all-to-all-start.2 = ((bf16[32,6,1792]{2,1,0:T(8,128)(2,1)}), bf16[32,6,1792]{2,1,0:T(8,128)(2,1)S(1)}, u32[]{:S(2)}, u32[]{:S(2)}) async-start(bf16[32,6,1792]{2,1,0:T(8,128)(2,1)} %reshape.57), calls=%async_computation.5 | async-start | bytes 1835008 | tf_op jit(solution)/shard_map/all_to_all | solution.py:131
  456.2 15.0 %all-to-all-done.2 = bf16[32,6,1792]{2,1,0:T(8,128)(2,1)S(1)} async-done(((bf16[32,6,1792]{2,1,0:T(8,128)(2,1)}), bf16[32,6,1792]{2,1,0:T(8,128)(2,1)S(1)}, u32[]{:S(2)}, u32[]{:S(2)}) %all-to-all-start.2) | async-done | bytes 688160 | tf_op jit(solution)/shard_map/all_to_all | solution.py:131
  471.4 1.9 fusion.5
  (71 shorter events, 15.2 us)
Async XLA Ops:
  6.5 40.8 %copy-start = (bf16[512,1792]{1,0:T(8,128)(2,1)S(1)}, bf16[512,1792]{1,0:T(8,128)(2,1)}, u32[]{:S(2)}) copy-start(bf16[512,1792]{1,0:T(8,128)(2,1)} %param.25) | copy-start | bytes 5505028
  6.5 119.6 %reduce-scatter.4.cloned.1.call-start = ((), (), s32[]{:S(2)}) async-start(), calls=%async_computation.6 | async-start | bytes 1892352 | tf_op jit(solution)/shard_map/reduce_scatter | solution.py:75
  9.3 3.1 copy-start.1
  13.3 20.7 %copy-start.4 = (bf16[4,512,128]{2,1,0:T(8,128)(2,1)S(1)}, bf16[4,512,128]{2,1,0:T(8,128)(2,1)}, u32[]{:S(2)}) copy-start(bf16[4,512,128]{2,1,0:T(8,128)(2,1)} %param.24) | copy-start | bytes 1572868
  47.4 2.5 copy-start.5
  47.4 78.7 %copy-start.2 = (bf16[16,1792]{1,0:T(8,128)(2,1)S(1)}, bf16[16,1792]{1,0:T(8,128)(2,1)}, u32[]{:S(2)}) copy-start(bf16[16,1792]{1,0:T(8,128)(2,1)} %param.21) | copy-start | bytes 172036
  47.4 134.6 %copy-start.10 = (bf16[1792,384]{1,0:T(8,128)(2,1)S(1)}, bf16[1792,384]{1,0:T(8,128)(2,1)}, u32[]{:S(2)}) copy-start(bf16[1792,384]{1,0:T(8,128)(2,1)} %param.27) | copy-start | bytes 4128772
  49.8 132.2 %all-gather.2.cloned.1.call-start = ((), (), s32[]{:S(2)}) async-start(), calls=%async_computation.7 | async-start | bytes 1892352 | tf_op jit(solution)/shard_map/all_gather | solution.py:84
  137.3 91.2 %all-reduce.2.cloned.1.call-start = ((), (), s32[]{:S(2)}) async-start(), calls=%async_computation.8 | async-start | bytes 1572864 | tf_op jit(solution)/shard_map/psum | solution.py:93
  182.0 2.6 copy-start.9
  182.0 2.6 copy-start.11
  186.5 126.5 %reduce-scatter.6.cloned.1.call-start = ((), (), s32[]{:S(2)}) async-start(), calls=%async_computation.9 | async-start | bytes 1892352 | tf_op jit(solution)/shard_map/reduce_scatter | solution.py:96
  229.8 3.9 copy-start.6
  229.8 3.9 copy-start.7
  229.8 83.2 %copy-start.3 = (bf16[16,1792]{1,0:T(8,128)(2,1)S(1)}, bf16[16,1792]{1,0:T(8,128)(2,1)}, u32[]{:S(2)}) copy-start(bf16[16,1792]{1,0:T(8,128)(2,1)} %reduce-scatter.4.cloned.1.call-done) | copy-start | bytes 172036
  233.7 212.1 %reduce-scatter.8.cloned.1.call-start = ((), (), s32[]{:S(2)}) async-start(), calls=%async_computation.10 | async-start | bytes 3440640 | tf_op jit(solution)/shard_map/reduce_scatter | solution.py:128
  414.5 40.9 %copy-start.8 = (f32[16,8]{0,1:T(8,128)S(1)}, f32[16,8]{0,1:T(8,128)}, u32[]{:S(2)}) copy-start(f32[16,8]{0,1:T(8,128)} %param.30) | copy-start | bytes 1540
  447.9 23.2 %all-to-all-start.2 = ((bf16[32,6,1792]{2,1,0:T(8,128)(2,1)}), bf16[32,6,1792]{2,1,0:T(8,128)(2,1)S(1)}, u32[]{:S(2)}, u32[]{:S(2)}) async-start(bf16[32,6,1792]{2,1,0:T(8,128)(2,1)} %reshape.57), calls=%async_computation.5 | async-start | bytes 1835008 | tf_op jit(solution)/shard_map/all_to_all | solution.py:131
Sparse Core Ops, SparseCore 0:
  49.9 76.1 reduce-scatter.3
  137.4 44.5 all-gather.1
  186.6 41.8 all-reduce.1
  233.8 79.1 reduce-scatter.5
  414.6 31.1 reduce-scatter.7
where the time goes:
time: 481 us; the launch traced here: 480 us
  waiting for transfers between devices  288 us (60%)
  blocking collectives  117 us (24%)
  matrix products  31.4 us (7%)
  between operations  13.5 us (3%)
  local copies, waits for them, and re-layouts  13.2 us (3%)
  other arithmetic  9.85 us (2%)
  starting transfers between devices  7.63 us (2%)
    reduce_scatter x1, waiting for transfers between devices, shards(): lax.psum_scatter(jnp.dot(rows, dense_down, preferred_element_type=jnp.flo...  78.4 us
    reduce_scatter x1, waiting for transfers between devices, shards(): lax.psum_scatter(jnp.dot(rows, out_proj, preferred_element_type=jnp.float...  76.2 us
    all_to_all x1, blocking collectives, shards(): lax.all_to_all(sendbuf, 'ep', split_axis=0, concat_axis=0, tiled=True)  56.9 us
    all_gather x1, waiting for transfers between devices, shards(): piece = lax.all_gather(normed, 'ep', axis=0, tiled=True)  44.6 us
    psum x1, waiting for transfers between devices, shards(): lax.psum(partial_sums.astype(jnp.bfloat16), 'tp').astype(jnp.float32)  42 us
    reduce_scatter x1, waiting for transfers between devices, shards(): lax.psum_scatter(expert_partial.astype(jnp.bfloat16), 'tp', scatter_dimen...  31.3 us
    all_to_all x1, blocking collectives, shards(): lax.all_to_all(latent, 'ep', split_axis=1, concat_axis=0, tiled=True)  19.9 us
    all_to_all x1, waiting for transfers between devices, shards(): lax.all_to_all(expert_result.reshape(group_count, capacity, -1), 'ep', sp...  15 us
  transfers between devices with their start and end apart: 6, of which 6 were waited for; matrix products, arithmetic and copies ran while one was open for 0% of the time, Pallas kernels for 0%

commit v1 on v0

v1 whole, which is shorter than its diff:
```python
import jax
import jax.numpy as jnp
from jax import lax
from jax.sharding import Mesh, PartitionSpec as P

D = 7168
ROPE = 64
VD = 128
EPS = 1e-06
YX = ("y", "x")
NZ = 4
BF = jnp.bfloat16
F32 = jnp.float32


def zsend(values, shift):
    return lax.ppermute(values, "z", [(i, (i + shift) % NZ) for i in range(NZ)])


def swap_core(values):
    return lax.ppermute(values, "c", [(0, 1), (1, 0)])


def zgather(values):
    return [values] + [zsend(values, NZ - k) for k in (1, 2, 3)]


def zscatter(blocks, z):
    take = lambda q: lax.dynamic_index_in_dim(blocks, q, 0, keepdims=False)
    got = [zsend(take(lax.rem(z + k, NZ)), k) for k in (1, 2, 3)]
    total = take(z).astype(F32)
    for piece in got:
        total = total + piece.astype(F32)
    return total


def plane_scatter(rows_own, rows_other, weight):
    dot = lambda a: jnp.dot(a, weight, preferred_element_type=F32)
    arrived = swap_core(dot(rows_other).astype(BF))
    mine = (dot(rows_own) + arrived.astype(F32)).astype(BF)
    parts = lax.all_to_all(mine.reshape(16, 16, -1), YX, 0, 0, tiled=True)
    return jnp.sum(parts.astype(F32), axis=0)


def attend(queries, kv_cache, new_latent, lengths, latent_dim):
    score_scale = (VD + ROPE) ** (-0.5)
    slot_count = kv_cache.shape[1]
    scores = jnp.einsum("rhc,rjc->rhj", queries, kv_cache, preferred_element_type=F32) * score_scale
    self_score = jnp.einsum("rhc,rc->rh", queries, new_latent, preferred_element_type=F32) * score_scale
    live_mask = lax.broadcasted_iota(jnp.int32, (1, slot_count), 1) < lengths[:, None]
    scores = jnp.where(live_mask[:, None, :], scores, -jnp.inf)
    top_score = jnp.maximum(jnp.max(scores, axis=-1), self_score)
    expo = jnp.exp(scores - top_score[..., None])
    self_expo = jnp.exp(self_score - top_score)
    total = jnp.sum(expo, axis=-1) + self_expo
    weights = (expo / total[..., None]).astype(BF)
    self_weight = (self_expo / total).astype(BF)
    latent = jnp.einsum("rhj,rjc->rhc", weights, kv_cache[:, :, :latent_dim], preferred_element_type=F32)
    latent = latent + self_weight.astype(F32)[..., None] * new_latent[:, None, :latent_dim].astype(F32)
    return latent.astype(BF)


def sum_columns(total):
    hi = lax.reduce_precision(total, 8, 7)
    lane = lax.broadcasted_iota(jnp.int32, (1, 128), 1)
    return jnp.where(lane == 0, hi[:, None], jnp.where(lane == 1, (total - hi)[:, None], 0.0))


def shards(
    queries, kv_cache, new_latent, lengths, residual, gain_first, gain_second, value_proj, out_proj,
    dense_gate, dense_up, dense_down, route_ids, route_gates, expert_gate, expert_up, expert_down,
):
    z = lax.axis_index("z")
    c = lax.axis_index("c")
    latent_dim = value_proj.shape[1]
    quarter = residual.shape[1]

    pick = lambda w, k, axis: lax.dynamic_slice_in_dim(w, lax.rem(z + k, NZ) * quarter, quarter, axis)
    gate_parts = [pick(expert_gate[0], 0, 0)] + [zsend(pick(expert_gate[0], NZ - k, 0), NZ - k) for k in (1, 2, 3)]
    up_parts = [pick(expert_up[0], 0, 0)] + [zsend(pick(expert_up[0], NZ - k, 0), NZ - k) for k in (1, 2, 3)]
    down_parts = [pick(expert_down[0], 0, 1)] + [zsend(pick(expert_down[0], NZ - k, 1), NZ - k) for k in (1, 2, 3)]

    latent = attend(queries, kv_cache, new_latent, lengths, latent_dim)
    latent = latent.reshape(4, 16, 2, 4, latent_dim)
    mine = lax.dynamic_index_in_dim(latent, c, 2, keepdims=False)
    theirs = lax.dynamic_index_in_dim(latent, 1 - c, 2, keepdims=False)
    theirs = swap_core(theirs)
    both = jnp.stack([mine, theirs], axis=0)
    both = both.transpose(2, 3, 0, 1, 4).reshape(16, 32, latent_dim)
    moved = lax.all_to_all(both, YX, 0, 0, tiled=True).reshape(16, 4, 8, latent_dim)
    head_vals = jnp.einsum("nhpc,hcv->nphv", moved, value_proj, preferred_element_type=F32).astype(BF)
    head_vals = head_vals.reshape(128, -1)
    rows = jnp.stack(zgather(head_vals), axis=0).reshape(NZ, 16, 2, 4, -1)
    rows = rows.transpose(2, 1, 0, 3, 4).reshape(2, 256, -1)
    attn_out = plane_scatter(rows[0], rows[1], out_proj)
    attn_out = jnp.roll(attn_out, z * 4, axis=0)
    first = residual.astype(F32) + attn_out

    def spread(values):
        wide = jnp.broadcast_to(values[None], (16,) + values.shape)
        own = lax.all_to_all(wide, YX, 0, 0, tiled=True).reshape(256, -1)
        return own, swap_core(own)

    own, other = spread(first.astype(BF))
    gain_a = gain_first.astype(F32)

    def gate_up(piece):
        value = piece.astype(F32)
        normed = (value * gain_a).astype(BF)
        return jnp.concatenate(
            [
                jnp.dot(normed, dense_gate, preferred_element_type=F32),
                jnp.dot(normed, dense_up, preferred_element_type=F32),
                sum_columns(jnp.sum(value * value, axis=1)),
            ],
            axis=1,
        ).astype(BF)

    width = dense_gate.shape[1]
    partial = jnp.stack([gate_up(own).reshape(NZ, 64, -1), gate_up(other).reshape(NZ, 64, -1)], axis=1)
    summed = zscatter(partial.reshape(NZ, 128, -1), z)
    scale = lax.rsqrt((summed[:, 2 * width] + summed[:, 2 * width + 1]) / D + EPS)[:, None]
    gate_act = summed[:, :width] * scale
    hidden = (jax.nn.silu(gate_act) * (summed[:, width : 2 * width] * scale)).astype(BF)
    hidden = jnp.stack(zgather(hidden), axis=0)
    hidden = jnp.roll(hidden, z, axis=0).reshape(NZ, 2, 64, -1)
    second = first + plane_scatter(hidden[:, 0].reshape(256, -1), hidden[:, 1].reshape(256, -1), dense_down)

    tok_group, top_count = route_ids.shape
    group_count, slots, cap = 32, 8, 6
    flat_ids = route_ids.reshape(-1)
    onehot = (flat_ids[:, None] == lax.broadcasted_iota(jnp.int32, (1, group_count), 1)).astype(jnp.int32)
    before = jnp.cumsum(onehot, axis=0) - onehot
    slot = jnp.sum(before * onehot, axis=1)
    position = (flat_ids * slots + slot).reshape(tok_group, top_count)
    columns = lax.broadcasted_iota(jnp.int32, (1, 1, group_count * slots), 2)
    matches = position[:, :, None] == columns
    pick_matrix = jnp.sum(matches.astype(jnp.int32), axis=1).astype(BF)
    combine_matrix = jnp.sum(jnp.where(matches, route_gates[:, :, None], 0.0), axis=1)
    sendbuf = jnp.einsum("tp,td->pd", pick_matrix, second.astype(BF), preferred_element_type=F32).astype(BF)
    arrived = lax.all_to_all(sendbuf.reshape(group_count, slots, -1), ("y", "x", "c"), 0, 0, tiled=True)
    arrived = arrived[:, :cap].reshape(group_count * cap, -1)
    value = arrived.astype(F32)
    normed = (value * gain_second.astype(F32)).astype(BF)
    he = expert_gate.shape[2]

    def unroll(parts):
        return jnp.roll(jnp.stack(parts, axis=0), z, axis=0).transpose(1, 0, 2).reshape(parts[0].shape[0], -1)

    gate_partial = unroll([jnp.dot(normed, w, preferred_element_type=F32).astype(BF) for w in gate_parts])
    up_partial = unroll([jnp.dot(normed, w, preferred_element_type=F32).astype(BF) for w in up_parts])
    partial = jnp.concatenate([gate_partial, up_partial, sum_columns(jnp.sum(value * value, axis=1)).astype(BF)], axis=1)
    summed = zscatter(partial.reshape(NZ, group_count * cap // NZ, -1), z)
    hw = he * NZ
    scale = lax.rsqrt((summed[:, 2 * hw] + summed[:, 2 * hw + 1]) / D + EPS)[:, None]
    expert_hidden = (jax.nn.silu(summed[:, :hw] * scale) * (summed[:, hw : 2 * hw] * scale)).astype(BF)
    expert_hidden = jnp.roll(jnp.stack(zgather(expert_hidden), axis=0), z, axis=0).reshape(group_count * cap, NZ, he)
    expert_hidden = jnp.roll(expert_hidden, -z, axis=1)
    result = sum(jnp.dot(expert_hidden[:, k], down_parts[k], preferred_element_type=F32) for k in range(NZ))
    result = jnp.pad(result.astype(BF).reshape(group_count, cap, -1), ((0, 0), (0, slots - cap), (0, 0)))
    returned = lax.all_to_all(result, ("y", "x", "c"), 0, 0, tiled=True).reshape(group_count * slots, -1)
    moe_out = jnp.dot(combine_matrix, returned.astype(F32), precision=lax.Precision.HIGHEST)
    return (second + moe_out).astype(BF)


def solution(mesh):
    grid = Mesh(mesh.devices.reshape(4, 4, 2, 4), ("y", "x", "c", "z"))
    ep = ("y", "x", "c")
    both = ("y", "x", "c", "z")
    return jax.shard_map(
        shards,
        mesh=grid,
        in_specs=(
            P(both, None, None),
            P(both, None, None),
            P(both, None),
            P(both),
            P(ep, "z"),
            P("z"),
            P("z"),
            P(ep, None, None),
            P(ep, "z"),
            P("z", ep),
            P("z", ep),
            P(ep, "z"),
            P(ep, None),
            P(ep, None),
            P(ep, None, "z"),
            P(ep, None, "z"),
            P(ep, "z", None),
        ),
        out_specs=P(ep, "z"),
        check_vma=False,
    )
```

time: 481 us -> 342 us (0.71)
  blocking collectives: 117 us -> 17.4 us
  waiting for transfers between devices: 288 us -> 198 us
  starting transfers between devices: 7.63 us -> 59.4 us
  between operations: 13.5 us -> 1.03 us
  matrix products: 31.4 us -> 37.5 us
    reduce_scatter x3 -> x0, waiting for transfers between devices: 186 us -> none  [the longest x1 78.4 us: shards(): lax.psum_scatter(jnp.dot(rows, dense_down, preferred_element_type=jnp.flo...]
    ppermute x0 -> x28, waiting for transfers between devices: none -> 135 us  [the longest x24 130 us: zsend(): return lax.ppermute(values, 'z', [(i, (i + shift) % NZ) for i in range(NZ)])]
    all_to_all x2 -> x1, blocking collectives: 76.9 us -> 17.4 us  [shards(): lax.all_to_all(both, YX, 0, 0, tiled=True).reshape(16, 4, 8, latent_dim)]
    all_to_all x1 -> x5, waiting for transfers between devices: 15 us -> 63.5 us  [the longest x2 28.8 us: plane_scatter(): parts = lax.all_to_all(mine.reshape(16, 16, -1), YX, 0, 0, tiled=True)]
    all_gather x1 -> x0, waiting for transfers between devices: 44.6 us -> none  [shards(): piece = lax.all_gather(normed, 'ep', axis=0, tiled=True)]
    psum x1 -> x0, waiting for transfers between devices: 42 us -> none  [shards(): lax.psum(partial_sums.astype(jnp.bfloat16), 'tp').astype(jnp.float32)]
    ppermute x0 -> x28, starting transfers between devices: none -> 33.8 us  [the longest x24 25.7 us: zsend(): return lax.ppermute(values, 'z', [(i, (i + shift) % NZ) for i in range(NZ)])]
    all_gather x2 -> x0, blocking collectives: 22.5 us -> none  [the longest x1 12.6 us: shards(): all_vals = lax.all_gather(head_vals, 'tp', axis=1, tiled=True)]
  transfers between devices with their start and end apart: 6 -> 33, of which waited for: 6 -> 27; matrix products, arithmetic and copies ran while one was open for 0% -> 10% of each run, Pallas kernels for 0% -> 0%
where the time goes in v1:
time: 342 us; the launch traced here: 341 us
  waiting for transfers between devices  198 us (58%)
  starting transfers between devices  59.4 us (17%)
  matrix products  37.5 us (11%)
  blocking collectives  17.4 us (5%)
  local copies, waits for them, and re-layouts  17.3 us (5%)
  other arithmetic  10.2 us (3%)
    ppermute x24, waiting for transfers between devices, zsend(): return lax.ppermute(values, 'z', [(i, (i + shift) % NZ) for i in range(NZ)])  130 us
    all_to_all x2, waiting for transfers between devices, plane_scatter(): parts = lax.all_to_all(mine.reshape(16, 16, -1), YX, 0, 0, tiled=True)  28.8 us
    ppermute x24, starting transfers between devices, zsend(): return lax.ppermute(values, 'z', [(i, (i + shift) % NZ) for i in range(NZ)])  25.7 us
    all_to_all x1, blocking collectives, shards(): lax.all_to_all(both, YX, 0, 0, tiled=True).reshape(16, 4, 8, latent_dim)  17.4 us
    all_to_all x1, waiting for transfers between devices, shards(): lax.all_to_all(result, ('y', 'x', 'c'), 0, 0, tiled=True)  15.5 us
    all_to_all x1, waiting for transfers between devices, spread(): own = lax.all_to_all(wide, YX, 0, 0, tiled=True).reshape(256, -1)  14 us
    dot_general x8, matrix products, shards(): jnp.dot(normed, w, preferred_element_type=F32).astype(BF)  12.9 us
    all_to_all x1, starting transfers between devices, shards(): lax.all_to_all(result, ('y', 'x', 'c'), 0, 0, tiled=True)  9.08 us
  transfers between devices with their start and end apart: 33, of which 27 were waited for; matrix products, arithmetic and copies ran while one was open for 10% of the time, Pallas kernels for 0%

profile of v1, /device:TPU:1, one launch (start us, length us, event | category | flops | bytes accessed | tf_op | source)
XLA Modules:
  0.0 341.0 jit_solution(15623035556942150059)
XLA Ops:
  10.2 17.4 %all_to_all.30 = bf16[16,32,512]{2,1,0:T(8,128)(2,1)S(1)} all-to-all(bf16[16,32,512]{2,1,0:T(8,128)(2,1)S(1)} %copy.76), channel_id=1, replica_groups=mesh['y'=4,'x'=4,'c'=2,'z'=4] {'y','x'}, dimensions={0} | all-to-all | bytes 1048576 | tf_op jit(solution)/shard_map/all_to_all | solution.py:90
  27.9 3.8 %collective-permute-start.1 = (bf16[128,512]{1,0:T(8,128)(2,1)S(1)}, bf16[128,512]{1,0:T(8,128)(2,1)S(1)}, u32[]{:S(2)}, u32[]{:S(2)}) collective-permute-start(bf16[128,512]{1,0:T(8,128)(2,1)S(1)} %bitcast.219), channel_id=1, source_target_pairs={{0,3},{1,0},{2,1},{3,2},{4,7},{5,4},{6,5},{7,6},{8,11},{9,8},{10,9... | collective-permute-start | bytes 393224 | tf_op jit(solution)/shard_map/ppermute | solution.py:17
  47.8 3.8 %all-to-all-start.1 = ((bf16[16,16,1792]{2,1,0:T(8,128)(2,1)}), bf16[16,16,1792]{2,1,0:T(8,128)(2,1)S(1)}, u32[]{:S(2)}, u32[]{:S(2)}) async-start(bf16[16,16,1792]{2,1,0:T(8,128)(2,1)} %bitcast.14), calls=%async_computation.1 | async-start | bytes 1835008 | tf_op jit(solution)/shard_map/all_to_all | solution.py:41
  51.6 15.0 %all-to-all-done.1 = bf16[16,16,1792]{2,1,0:T(8,128)(2,1)S(1)} async-done(((bf16[16,16,1792]{2,1,0:T(8,128)(2,1)}), bf16[16,16,1792]{2,1,0:T(8,128)(2,1)S(1)}, u32[]{:S(2)}, u32[]{:S(2)}) %all-to-all-start.1) | async-done | bytes 917536 | tf_op jit(solution)/shard_map/all_to_all | solution.py:41
  67.8 3.9 %all-to-all-start.2 = ((bf16[16,16,1792]{2,1,0:T(8,128)(2,1)}), bf16[16,16,1792]{2,1,0:T(8,128)(2,1)S(1)}, u32[]{:S(2)}, u32[]{:S(2)}) async-start(bf16[16,16,1792]{2,1,0:T(8,128)(2,1)} %broadcast_in_dim.143), calls=%async_computation.2 | async-start | bytes 1835008 | tf_op jit(solution)/shard_map/all_to_all | solution.py:101
  71.8 14.0 %all-to-all-done.2 = bf16[16,16,1792]{2,1,0:T(8,128)(2,1)S(1)} async-done(((bf16[16,16,1792]{2,1,0:T(8,128)(2,1)}), bf16[16,16,1792]{2,1,0:T(8,128)(2,1)S(1)}, u32[]{:S(2)}, u32[]{:S(2)}) %all-to-all-start.2) | async-done | bytes 917536 | tf_op jit(solution)/shard_map/all_to_all | solution.py:101
  100.0 10.7 %collective-permute-done.6 = bf16[128,896]{1,0:T(8,128)(2,1)S(1)} collective-permute-done((bf16[128,896]{1,0:T(8,128)(2,1)S(1)}, bf16[128,896]{1,0:T(8,128)(2,1)S(1)}, u32[]{:S(2)}, u32[]{:S(2)}) %collective-permute-start.6) | collective-permute-done | bytes 229408 | tf_op jit(solution)/shard_map/ppermute | solution.py:17
  127.1 3.6 %all-to-all-start.3 = ((bf16[16,16,1792]{2,1,0:T(8,128)(2,1)}), bf16[16,16,1792]{2,1,0:T(8,128)(2,1)S(1)}, u32[]{:S(2)}, u32[]{:S(2)}) async-start(bf16[16,16,1792]{2,1,0:T(8,128)(2,1)} %bitcast.37), calls=%async_computation.3 | async-start | bytes 1835008 | tf_op jit(solution)/shard_map/all_to_all | solution.py:41
  132.1 13.9 %all-to-all-done.3 = bf16[16,16,1792]{2,1,0:T(8,128)(2,1)S(1)} async-done(((bf16[16,16,1792]{2,1,0:T(8,128)(2,1)}), bf16[16,16,1792]{2,1,0:T(8,128)(2,1)S(1)}, u32[]{:S(2)}, u32[]{:S(2)}) %all-to-all-start.3) | async-done | bytes 917536 | tf_op jit(solution)/shard_map/all_to_all | solution.py:41
  147.5 5.3 %all-to-all-start.4 = ((bf16[32,8,1792]{2,1,0:T(8,128)(2,1)}), bf16[32,8,1792]{2,1,0:T(8,128)(2,1)S(1)}, u32[]{:S(2)}, u32[]{:S(2)}) async-start(bf16[32,8,1792]{2,1,0:T(8,128)(2,1)} %fusion.2), calls=%async_computation.4 | async-start | bytes 1835008 | tf_op jit(solution)/shard_map/all_to_all | solution.py:141
  152.8 3.5 %dynamic-slice_bitcast_fusion.6 = (bf16[1792,256]{1,0:T(8,128)(2,1)}, bf16[1792,256]{1,0:T(8,128)(2,1)}, bf16[1792,256]{1,0:T(8,128)(2,1)}) fusion(bf16[1,7168,256]{2,1,0:T(8,128)(2,1)} %param.33, s32[]{:T(128)S(6)} %select_n.166, s32[]{:T(128)S(6)} %select_n.164, s32[]{:T(128)S(6)} %select_n.165), kind=kLoop, calls=%fused_computation.76 | loop fusion | bytes 5505036 | tf_op jit(solution)/shard_map/dynamic_slice | solution.py:78
  163.5 5.1 %all-to-all-done.4 = bf16[32,8,1792]{2,1,0:T(8,128)(2,1)S(1)} async-done(((bf16[32,8,1792]{2,1,0:T(8,128)(2,1)}), bf16[32,8,1792]{2,1,0:T(8,128)(2,1)S(1)}, u32[]{:S(2)}, u32[]{:S(2)}) %all-to-all-start.4) | async-done | bytes 917536 | tf_op jit(solution)/shard_map/all_to_all | solution.py:141
  172.6 5.6 %collective-permute-done.13 = bf16[1792,256]{1,0:T(8,128)(2,1)} collective-permute-done((bf16[1792,256]{1,0:T(8,128)(2,1)}, bf16[1792,256]{1,0:T(8,128)(2,1)}, u32[]{:S(2)}, u32[]{:S(2)}) %collective-permute-start.13) | collective-permute-done | bytes 917536 | tf_op jit(solution)/shard_map/ppermute | solution.py:17
  184.0 17.6 %collective-permute-done.15 = bf16[1792,256]{1,0:T(8,128)(2,1)} collective-permute-done((bf16[1792,256]{1,0:T(8,128)(2,1)}, bf16[1792,256]{1,0:T(8,128)(2,1)}, u32[]{:S(2)}, u32[]{:S(2)}) %collective-permute-start.15) | collective-permute-done | bytes 917536 | tf_op jit(solution)/shard_map/ppermute | solution.py:17
  205.8 11.8 %collective-permute-done.16 = bf16[1792,256]{1,0:T(8,128)(2,1)} collective-permute-done((bf16[1792,256]{1,0:T(8,128)(2,1)}, bf16[1792,256]{1,0:T(8,128)(2,1)}, u32[]{:S(2)}, u32[]{:S(2)}) %collective-permute-start.16) | collective-permute-done | bytes 917536 | tf_op jit(solution)/shard_map/ppermute | solution.py:17
  221.0 18.9 %collective-permute-done.18 = bf16[1792,256]{1,0:T(8,128)(2,1)} collective-permute-done((bf16[1792,256]{1,0:T(8,128)(2,1)S(1)}, bf16[1792,256]{1,0:T(8,128)(2,1)}, u32[]{:S(2)}, u32[]{:S(2)}) %collective-permute-start.18) | collective-permute-done | bytes 917536 | tf_op jit(solution)/shard_map/ppermute | solution.py:17
  245.6 5.4 %collective-permute-done.19 = bf16[48,2176]{1,0:T(8,128)(2,1)S(1)} collective-permute-done((bf16[48,2176]{1,0:T(8,128)(2,1)S(1)}, bf16[48,2176]{1,0:T(8,128)(2,1)S(1)}, u32[]{:S(2)}, u32[]{:S(2)}) %collective-permute-start.19) | collective-permute-done | bytes 208928 | tf_op jit(solution)/shard_map/ppermute | solution.py:17
  251.0 2.9 collective-permute-done.20
  255.5 3.0 collective-permute-start.22
  261.2 2.9 collective-permute-start.23
  264.1 38.5 %collective-permute-done.23 = bf16[48,1024]{1,0:T(8,128)(2,1)S(1)} collective-permute-done((bf16[48,1024]{1,0:T(8,128)(2,1)S(1)}, bf16[48,1024]{1,0:T(8,128)(2,1)S(1)}, u32[]{:S(2)}, u32[]{:S(2)}) %collective-permute-start.23) | collective-permute-done | bytes 98336 | tf_op jit(solution)/shard_map/ppermute | solution.py:17
  302.6 3.2 collective-permute-done.24
  315.1 9.1 %all-to-all-start.5 = ((bf16[32,8,1792]{2,1,0:T(8,128)(2,1)}), bf16[32,8,1792]{2,1,0:T(8,128)(2,1)S(1)}, u32[]{:S(2)}, u32[]{:S(2)}) async-start(bf16[32,8,1792]{2,1,0:T(8,128)(2,1)} %pad.4), calls=%async_computation.5 | async-start | bytes 1835008 | tf_op jit(solution)/shard_map/all_to_all | solution.py:161
  324.4 15.5 %all-to-all-done.5 = bf16[32,8,1792]{2,1,0:T(8,128)(2,1)S(1)} async-done(((bf16[32,8,1792]{2,1,0:T(8,128)(2,1)}), bf16[32,8,1792]{2,1,0:T(8,128)(2,1)S(1)}, u32[]{:S(2)}, u32[]{:S(2)}) %all-to-all-start.5) | async-done | bytes 917536 | tf_op jit(solution)/shard_map/all_to_all | solution.py:161
  (219 shorter events, 105.7 us)
Async XLA Ops:
  47.8 18.8 %all-to-all-start.1 = ((bf16[16,16,1792]{2,1,0:T(8,128)(2,1)}), bf16[16,16,1792]{2,1,0:T(8,128)(2,1)S(1)}, u32[]{:S(2)}, u32[]{:S(2)}) async-start(bf16[16,16,1792]{2,1,0:T(8,128)(2,1)} %bitcast.14), calls=%async_computation.1 | async-start | bytes 1835008 | tf_op jit(solution)/shard_map/all_to_all | solution.py:41
  67.8 18.0 %all-to-all-start.2 = ((bf16[16,16,1792]{2,1,0:T(8,128)(2,1)}), bf16[16,16,1792]{2,1,0:T(8,128)(2,1)S(1)}, u32[]{:S(2)}, u32[]{:S(2)}) async-start(bf16[16,16,1792]{2,1,0:T(8,128)(2,1)} %broadcast_in_dim.143), calls=%async_computation.2 | async-start | bytes 1835008 | tf_op jit(solution)/shard_map/all_to_all | solution.py:101
  97.3 13.4 %collective-permute-start.6 = (bf16[128,896]{1,0:T(8,128)(2,1)S(1)}, bf16[128,896]{1,0:T(8,128)(2,1)S(1)}, u32[]{:S(2)}, u32[]{:S(2)}) collective-permute-start(bf16[128,896]{1,0:T(8,128)(2,1)S(1)} %get-tuple-element.21), channel_id=1, source_target_pairs={{0,1},{1,2},{2,3},{3,0},{4,5},{5,6},{6,7},{7,4},{8,9},{9,10},{10,1... | collective-permute-start | bytes 688136 | tf_op jit(solution)/shard_map/ppermute | solution.py:17
  97.3 13.3 %collective-permute-start.7 = (bf16[128,896]{1,0:T(8,128)(2,1)S(1)}, bf16[128,896]{1,0:T(8,128)(2,1)S(1)}, u32[]{:S(2)}, u32[]{:S(2)}) collective-permute-start(bf16[128,896]{1,0:T(8,128)(2,1)S(1)} %get-tuple-element.23), channel_id=1, source_target_pairs={{0,2},{1,3},{2,0},{3,1},{4,6},{5,7},{6,4},{7,5},{8,10},{9,11},{10,... | collective-permute-start | bytes 688136 | tf_op jit(solution)/shard_map/ppermute | solution.py:17
  99.2 11.8 %collective-permute-start.8 = (bf16[128,896]{1,0:T(8,128)(2,1)S(1)}, bf16[128,896]{1,0:T(8,128)(2,1)S(1)}, u32[]{:S(2)}, u32[]{:S(2)}) collective-permute-start(bf16[128,896]{1,0:T(8,128)(2,1)S(1)} %get-tuple-element.22), channel_id=1, source_target_pairs={{0,3},{1,0},{2,1},{3,2},{4,7},{5,4},{6,5},{7,6},{8,11},{9,8},{10,9... | collective-permute-start | bytes 688136 | tf_op jit(solution)/shard_map/ppermute | solution.py:17
  113.9 7.6 %collective-permute-start.11 = (bf16[128,384]{1,0:T(8,128)(2,1)S(1)}, bf16[128,384]{1,0:T(8,128)(2,1)S(1)}, u32[]{:S(2)}, u32[]{:S(2)}) collective-permute-start(bf16[128,384]{1,0:T(8,128)(2,1)S(1)} %get-tuple-element.9), channel_id=1, source_target_pairs={{0,1},{1,2},{2,3},{3,0},{4,5},{5,6},{6,7},{7,4},{8,9},{9,10},{10,1... | collective-permute-start | bytes 294920 | tf_op jit(solution)/shard_map/ppermute | solution.py:17
  127.1 18.8 %all-to-all-start.3 = ((bf16[16,16,1792]{2,1,0:T(8,128)(2,1)}), bf16[16,16,1792]{2,1,0:T(8,128)(2,1)S(1)}, u32[]{:S(2)}, u32[]{:S(2)}) async-start(bf16[16,16,1792]{2,1,0:T(8,128)(2,1)} %bitcast.37), calls=%async_computation.3 | async-start | bytes 1835008 | tf_op jit(solution)/shard_map/all_to_all | solution.py:41
  147.5 21.1 %all-to-all-start.4 = ((bf16[32,8,1792]{2,1,0:T(8,128)(2,1)}), bf16[32,8,1792]{2,1,0:T(8,128)(2,1)S(1)}, u32[]{:S(2)}, u32[]{:S(2)}) async-start(bf16[32,8,1792]{2,1,0:T(8,128)(2,1)} %fusion.2), calls=%async_computation.4 | async-start | bytes 1835008 | tf_op jit(solution)/shard_map/all_to_all | solution.py:141
  156.3 21.9 %collective-permute-start.13 = (bf16[1792,256]{1,0:T(8,128)(2,1)}, bf16[1792,256]{1,0:T(8,128)(2,1)}, u32[]{:S(2)}, u32[]{:S(2)}) collective-permute-start(bf16[1792,256]{1,0:T(8,128)(2,1)} %get-tuple-element.14), channel_id=1, source_target_pairs={{0,3},{1,0},{2,1},{3,2},{4,7},{5,4},{6,5},{7,6},{8,11},{9,8},{10,9... | collective-permute-start | bytes 2752520 | tf_op jit(solution)/shard_map/ppermute | solution.py:17
  156.9 23.1 %collective-permute-start.14 = (bf16[1792,256]{1,0:T(8,128)(2,1)}, bf16[1792,256]{1,0:T(8,128)(2,1)}, u32[]{:S(2)}, u32[]{:S(2)}) collective-permute-start(bf16[1792,256]{1,0:T(8,128)(2,1)} %get-tuple-element.15), channel_id=1, source_target_pairs={{0,2},{1,3},{2,0},{3,1},{4,6},{5,7},{6,4},{7,5},{8,10},{9,11},{10,... | collective-permute-start | bytes 2752520 | tf_op jit(solution)/shard_map/ppermute | solution.py:17
  156.9 44.7 %collective-permute-start.15 = (bf16[1792,256]{1,0:T(8,128)(2,1)}, bf16[1792,256]{1,0:T(8,128)(2,1)}, u32[]{:S(2)}, u32[]{:S(2)}) collective-permute-start(bf16[1792,256]{1,0:T(8,128)(2,1)} %get-tuple-element.13), channel_id=1, source_target_pairs={{0,1},{1,2},{2,3},{3,0},{4,5},{5,6},{6,7},{7,4},{8,9},{9,10},{10,1... | collective-permute-start | bytes 2752520 | tf_op jit(solution)/shard_map/ppermute | solution.py:17
  159.3 58.2 %collective-permute-start.16 = (bf16[1792,256]{1,0:T(8,128)(2,1)}, bf16[1792,256]{1,0:T(8,128)(2,1)}, u32[]{:S(2)}, u32[]{:S(2)}) collective-permute-start(bf16[1792,256]{1,0:T(8,128)(2,1)} %get-tuple-element.17), channel_id=1, source_target_pairs={{0,3},{1,0},{2,1},{3,2},{4,7},{5,4},{6,5},{7,6},{8,11},{9,8},{10,9... | collective-permute-start | bytes 2752520 | tf_op jit(solution)/shard_map/ppermute | solution.py:17
  161.7 57.7 %collective-permute-start.17 = (bf16[1792,256]{1,0:T(8,128)(2,1)}, bf16[1792,256]{1,0:T(8,128)(2,1)}, u32[]{:S(2)}, u32[]{:S(2)}) collective-permute-start(bf16[1792,256]{1,0:T(8,128)(2,1)} %get-tuple-element.18), channel_id=1, source_target_pairs={{0,2},{1,3},{2,0},{3,1},{4,6},{5,7},{6,4},{7,5},{8,10},{9,11},{10,... | collective-permute-start | bytes 2752520 | tf_op jit(solution)/shard_map/ppermute | solution.py:17
  178.2 61.7 %collective-permute-start.18 = (bf16[1792,256]{1,0:T(8,128)(2,1)S(1)}, bf16[1792,256]{1,0:T(8,128)(2,1)}, u32[]{:S(2)}, u32[]{:S(2)}) collective-permute-start(bf16[1792,256]{1,0:T(8,128)(2,1)S(1)} %copy-done.6), channel_id=1, source_target_pairs={{0,1},{1,2},{2,3},{3,0},{4,5},{5,6},{6,7},{7,4},{8,9},{9,10},{10,1... | collective-permute-start | bytes 2752520 | tf_op jit(solution)/shard_map/ppermute | solution.py:17
  242.9 8.2 %collective-permute-start.19 = (bf16[48,2176]{1,0:T(8,128)(2,1)S(1)}, bf16[48,2176]{1,0:T(8,128)(2,1)S(1)}, u32[]{:S(2)}, u32[]{:S(2)}) collective-permute-start(bf16[48,2176]{1,0:T(8,128)(2,1)S(1)} %get-tuple-element.24), channel_id=1, source_target_pairs={{0,1},{1,2},{2,3},{3,0},{4,5},{5,6},{6,7},{7,4},{8,9},{9,10},{10,1... | collective-permute-start | bytes 626696 | tf_op jit(solution)/shard_map/ppermute | solution.py:17
  242.9 11.0 %collective-permute-start.20 = (bf16[48,2176]{1,0:T(8,128)(2,1)S(1)}, bf16[48,2176]{1,0:T(8,128)(2,1)S(1)}, u32[]{:S(2)}, u32[]{:S(2)}) collective-permute-start(bf16[48,2176]{1,0:T(8,128)(2,1)S(1)} %get-tuple-element.26), channel_id=1, source_target_pairs={{0,2},{1,3},{2,0},{3,1},{4,6},{5,7},{6,4},{7,5},{8,10},{9,11},{10,... | collective-permute-start | bytes 626696 | tf_op jit(solution)/shard_map/ppermute | solution.py:17
  245.4 9.6 %collective-permute-start.21 = (bf16[48,2176]{1,0:T(8,128)(2,1)S(1)}, bf16[48,2176]{1,0:T(8,128)(2,1)S(1)}, u32[]{:S(2)}, u32[]{:S(2)}) collective-permute-start(bf16[48,2176]{1,0:T(8,128)(2,1)S(1)} %get-tuple-element.25), channel_id=1, source_target_pairs={{0,3},{1,0},{2,1},{3,2},{4,7},{5,4},{6,5},{7,6},{8,11},{9,8},{10,9... | collective-permute-start | bytes 626696 | tf_op jit(solution)/shard_map/ppermute | solution.py:17
  255.5 8.6 %collective-permute-start.22 = (bf16[48,1024]{1,0:T(8,128)(2,1)S(1)}, bf16[48,1024]{1,0:T(8,128)(2,1)S(1)}, u32[]{:S(2)}, u32[]{:S(2)}) collective-permute-start(bf16[48,1024]{1,0:T(8,128)(2,1)S(1)} %get-tuple-element.7), channel_id=1, source_target_pairs={{0,3},{1,0},{2,1},{3,2},{4,7},{5,4},{6,5},{7,6},{8,11},{9,8},{10,9... | collective-permute-start | bytes 294920 | tf_op jit(solution)/shard_map/ppermute | solution.py:17
  259.7 50.9 %collective-permute-start.25 = (bf16[256,1792]{1,0:T(8,128)(2,1)S(1)}, bf16[256,1792]{1,0:T(8,128)(2,1)}, u32[]{:S(2)}, u32[]{:S(2)}) collective-permute-start(bf16[256,1792]{1,0:T(8,128)(2,1)S(1)} %get-tuple-element.11), channel_id=1, source_target_pairs={{0,3},{1,0},{2,1},{3,2},{4,7},{5,4},{6,5},{7,6},{8,11},{9,8},{10,9... | collective-permute-start | bytes 2752520 | tf_op jit(solution)/shard_map/ppermute | solution.py:17
  259.7 49.4 %collective-permute-start.27 = (bf16[256,1792]{1,0:T(8,128)(2,1)}, bf16[256,1792]{1,0:T(8,128)(2,1)}, u32[]{:S(2)}, u32[]{:S(2)}) collective-permute-start(bf16[256,1792]{1,0:T(8,128)(2,1)} %get-tuple-element.12), channel_id=1, source_target_pairs={{0,1},{1,2},{2,3},{3,0},{4,5},{5,6},{6,7},{7,4},{8,9},{9,10},{10,1... | collective-permute-start | bytes 2752520 | tf_op jit(solution)/shard_map/ppermute | solution.py:17
  261.1 51.0 %collective-permute-start.26 = (bf16[256,1792]{1,0:T(8,128)(2,1)S(1)}, bf16[256,1792]{1,0:T(8,128)(2,1)}, u32[]{:S(2)}, u32[]{:S(2)}) collective-permute-start(bf16[256,1792]{1,0:T(8,128)(2,1)S(1)} %get-tuple-element.10), channel_id=1, source_target_pairs={{0,2},{1,3},{2,0},{3,1},{4,6},{5,7},{6,4},{7,5},{8,10},{9,11},{10,... | collective-permute-start | bytes 2752520 | tf_op jit(solution)/shard_map/ppermute | solution.py:17
  261.2 41.5 %collective-permute-start.23 = (bf16[48,1024]{1,0:T(8,128)(2,1)S(1)}, bf16[48,1024]{1,0:T(8,128)(2,1)S(1)}, u32[]{:S(2)}, u32[]{:S(2)}) collective-permute-start(bf16[48,1024]{1,0:T(8,128)(2,1)S(1)} %get-tuple-element.7), channel_id=1, source_target_pairs={{0,2},{1,3},{2,0},{3,1},{4,6},{5,7},{6,4},{7,5},{8,10},{9,11},{10,... | collective-permute-start | bytes 294920 | tf_op jit(solution)/shard_map/ppermute | solution.py:17
  264.1 41.7 %collective-permute-start.24 = (bf16[48,1024]{1,0:T(8,128)(2,1)S(1)}, bf16[48,1024]{1,0:T(8,128)(2,1)S(1)}, u32[]{:S(2)}, u32[]{:S(2)}) collective-permute-start(bf16[48,1024]{1,0:T(8,128)(2,1)S(1)} %get-tuple-element.7), channel_id=1, source_target_pairs={{0,1},{1,2},{2,3},{3,0},{4,5},{5,6},{6,7},{7,4},{8,9},{9,10},{10,1... | collective-permute-start | bytes 294920 | tf_op jit(solution)/shard_map/ppermute | solution.py:17
  315.1 24.8 %all-to-all-start.5 = ((bf16[32,8,1792]{2,1,0:T(8,128)(2,1)}), bf16[32,8,1792]{2,1,0:T(8,128)(2,1)S(1)}, u32[]{:S(2)}, u32[]{:S(2)}) async-start(bf16[32,8,1792]{2,1,0:T(8,128)(2,1)} %pad.4), calls=%async_computation.5 | async-start | bytes 1835008 | tf_op jit(solution)/shard_map/all_to_all | solution.py:161
  (33 other events, 377.9 us)

commit v2 on v1

v2 whole, which is shorter than its diff:
```python
import jax
import jax.numpy as jnp
from jax import lax
from jax.experimental import pallas as pl
from jax.experimental.pallas import tpu as pltpu
from jax.sharding import Mesh, PartitionSpec as P

D = 7168
ROPE = 64
VD = 128
EPS = 1e-06
YX = ("y", "x")
NZ = 4
BF = jnp.bfloat16
F32 = jnp.float32


def zsend(values, shift):
    return lax.ppermute(values, "z", [(i, (i + shift) % NZ) for i in range(NZ)])


def swap_core(values):
    return lax.ppermute(values, "c", [(0, 1), (1, 0)])


def zgather(values):
    return [values] + [zsend(values, NZ - k) for k in (1, 2, 3)]


def zscatter(blocks):
    got = [zsend(blocks[k], k) for k in (1, 2, 3)]
    total = blocks[0].astype(F32)
    for piece in got:
        total = total + piece.astype(F32)
    return total


def plane_scatter(kernel, z, blocks, weight):
    arrived = swap_core(plane_dot(kernel, z, blocks, weight, 1, BF))
    mine = (plane_dot(kernel, z, blocks, weight, 0, F32) + arrived.astype(F32)).astype(BF)
    parts = lax.all_to_all(mine.reshape(16, 16, -1), YX, 0, 0, tiled=True)
    return jnp.sum(parts.astype(F32), axis=0)


def attend(queries, kv_cache, new_latent, lengths, latent_dim):
    score_scale = (VD + ROPE) ** (-0.5)
    slot_count = kv_cache.shape[1]
    scores = jnp.einsum("rhc,rjc->rhj", queries, kv_cache, preferred_element_type=F32) * score_scale
    self_score = jnp.einsum("rhc,rc->rh", queries, new_latent, preferred_element_type=F32) * score_scale
    live_mask = lax.broadcasted_iota(jnp.int32, (1, slot_count), 1) < lengths[:, None]
    scores = jnp.where(live_mask[:, None, :], scores, -jnp.inf)
    top_score = jnp.maximum(jnp.max(scores, axis=-1), self_score)
    expo = jnp.exp(scores - top_score[..., None])
    self_expo = jnp.exp(self_score - top_score)
    total = jnp.sum(expo, axis=-1) + self_expo
    weights = (expo / total[..., None]).astype(BF)
    self_weight = (self_expo / total).astype(BF)
    latent = jnp.einsum("rhj,rjc->rhc", weights, kv_cache[:, :, :latent_dim], preferred_element_type=F32)
    latent = latent + self_weight.astype(F32)[..., None] * new_latent[:, None, :latent_dim].astype(F32)
    return latent.astype(BF)


def params():
    return pltpu.CompilerParams(dimension_semantics=("arbitrary",), vmem_limit_bytes=40 * 1024 * 1024)


def tail_of(squares):
    total = jnp.sum(squares, axis=1, keepdims=True)
    hi = total.astype(BF).astype(F32)
    lane = lax.broadcasted_iota(jnp.int32, (total.shape[0], 128), 1)
    return jnp.where(lane == 0, hi, jnp.where(lane == 1, total - hi, 0.0)).astype(BF)


def dense_in_kernel(z_ref, own, other, gain, gate, up, o0, o1, o2, o3, acc, squares, tail):
    step = pl.program_id(0)
    width = gate.shape[1]

    @pl.when(step == 0)
    def _():
        acc[...] = jnp.zeros_like(acc)
        squares[...] = jnp.zeros_like(squares)

    scale = gain[...].astype(F32)
    for rel, ref in enumerate((own, other)):
        value = ref[...].astype(F32)
        normed = (value * scale).astype(BF)
        acc[rel, :, :width] += jnp.dot(normed, gate[...], preferred_element_type=F32)
        acc[rel, :, width:] += jnp.dot(normed, up[...], preferred_element_type=F32)
        square = value * value
        squares[rel] += square[:, :128] + square[:, 128:]

    @pl.when(step == pl.num_programs(0) - 1)
    def _():
        z = z_ref[0]
        for rel in range(2):
            tail[rel] = tail_of(squares[rel])
        for k, out in enumerate((o0, o1, o2, o3)):
            at = pl.multiple_of(lax.rem(z + k, NZ) * 64, 64)
            for rel in range(2):
                rows = pl.ds(rel * 64, 64)
                out[rows, : 2 * width] = acc[rel, pl.ds(at, 64), :].astype(BF)
                out[rows, 2 * width :] = tail[rel, pl.ds(at, 64), :]


def dense_in(z, own, other, gain, gate, up):
    depth, width = gate.shape
    step = 256
    rows = own.shape[0]
    lhs = pl.BlockSpec((rows, step), lambda i, z: (0, i))
    weight = pl.BlockSpec((step, width), lambda i, z: (i, 0))
    lanes = 2 * width + 128
    return pl.pallas_call(
        dense_in_kernel,
        grid_spec=pltpu.PrefetchScalarGridSpec(
            num_scalar_prefetch=1,
            grid=(depth // step,),
            in_specs=[lhs, lhs, pl.BlockSpec((1, step), lambda i, z: (0, i)), weight, weight],
            out_specs=[pl.BlockSpec((rows // 2, lanes), lambda i, z: (0, 0))] * NZ,
            scratch_shapes=[
                pltpu.VMEM((2, rows, 2 * width), F32),
                pltpu.VMEM((2, rows, 128), F32),
                pltpu.VMEM((2, rows, 128), BF),
            ],
        ),
        out_shape=[jax.ShapeDtypeStruct((rows // 2, lanes), BF)] * NZ,
        compiler_params=params(),
        cost_estimate=pl.CostEstimate(flops=8 * rows * depth * width, bytes_accessed=4 * depth * (rows + width), transcendentals=0),
        name="dense_in",
    )(z, own, other, gain.reshape(1, -1), gate, up)


def silu(value):
    return value / (1.0 + jnp.exp(-value))


def expert_in_kernel(z_ref, x0, x1, x2, *refs):
    gates, ups, out, (gate_acc, up_acc) = refs[:4], refs[4:8], refs[8], refs[9:]
    step = pl.program_id(0)

    @pl.when(step == 0)
    def _():
        gate_acc[...] = jnp.zeros_like(gate_acc)
        up_acc[...] = jnp.zeros_like(up_acc)

    rows, wide = out.shape[0], x0.shape[0]
    row = lax.broadcasted_iota(jnp.int32, (rows, wide), 0)
    col = lax.broadcasted_iota(jnp.int32, (rows, wide), 1)
    block, place = (col >> 3) * 6, col & 7
    onehot = lambda hit: jnp.where(hit, 1.0, 0.0).astype(BF)
    keep = onehot((place < 6) & (row == block + place))
    rest = None
    quarters = []
    for m, ref in enumerate((x0, x1, x2)):
        x = ref[...]
        quarters.append(jnp.dot(keep, x, preferred_element_type=F32).astype(BF))
        pick = onehot((place >= 6) & (row == block + 3 * (place - 6) + m))
        term = jnp.dot(pick, x, preferred_element_type=F32)
        rest = term if rest is None else rest + term
    quarters.append(rest.astype(BF))
    for m in range(NZ):
        gate_acc[...] += jnp.dot(quarters[m], gates[m][...], preferred_element_type=F32)
        up_acc[...] += jnp.dot(quarters[m], ups[m][...], preferred_element_type=F32)

    @pl.when(step == pl.num_programs(0) - 1)
    def _():
        out[...] = (silu(gate_acc[...]) * up_acc[...]).astype(BF)


def expert_in(z, x, gate, up, rows):
    depth, width = gate.shape
    step = 256
    steps = depth // NZ // step
    xs = [pl.BlockSpec((x.shape[0], step), lambda i, z, m=m: (0, m * steps + i)) for m in range(3)]
    ws = [pl.BlockSpec((step, width), lambda i, z, m=m: (lax.rem(z[0] + m, NZ) * steps + i, 0)) for m in range(NZ)]
    return pl.pallas_call(
        expert_in_kernel,
        grid_spec=pltpu.PrefetchScalarGridSpec(
            num_scalar_prefetch=1,
            grid=(steps,),
            in_specs=xs + ws + ws,
            out_specs=pl.BlockSpec((rows, width), lambda i, z: (0, 0)),
            scratch_shapes=[pltpu.VMEM((rows, width), F32)] * 2,
        ),
        out_shape=jax.ShapeDtypeStruct((rows, width), BF),
        compiler_params=params(),
        cost_estimate=pl.CostEstimate(flops=4 * rows * depth * width, bytes_accessed=4 * depth * width, transcendentals=0),
        name="expert_in",
    )(z, x, x, x, *[gate] * 4, *[up] * 4)


def expert_out_kernel(z_ref, *refs):
    hidden, weights, out, wide = refs[:4], refs[4:8], refs[8], refs[9]

    @pl.when(pl.program_id(0) == 0)
    def _():
        shape = (wide.shape[1], hidden[0].shape[0])
        row = lax.broadcasted_iota(jnp.int32, shape, 0)
        col = lax.broadcasted_iota(jnp.int32, shape, 1)
        keep = ((row & 7) < 6) & (col == (row >> 3) * 6 + (row & 7))
        keep = jnp.where(keep, 1.0, 0.0).astype(BF)
        for k in range(NZ):
            wide[k] = jnp.dot(keep, hidden[k][...], preferred_element_type=F32).astype(BF)

    total = None
    for k in range(NZ):
        term = jnp.dot(wide[k], weights[k][...], preferred_element_type=F32)
        total = term if total is None else total + term
    out[...] = total.astype(BF)


def expert_out(z, hidden, down, got, wide):
    rows, width = hidden[0].shape
    columns = got[0].shape[1]
    step = 256
    steps = columns // step
    return pl.pallas_call(
        expert_out_kernel,
        grid_spec=pltpu.PrefetchScalarGridSpec(
            num_scalar_prefetch=1,
            grid=(steps,),
            in_specs=[pl.BlockSpec((rows, width), lambda i, z: (0, 0))] * NZ
            + [pl.BlockSpec((width, step), lambda i, z: (0, z[0] * steps + i))]
            + [pl.BlockSpec((width, step), lambda i, z: (0, i))] * 3,
            out_specs=pl.BlockSpec((wide, step), lambda i, z: (0, i)),
            scratch_shapes=[pltpu.VMEM((NZ, wide, width), BF)],
        ),
        out_shape=jax.ShapeDtypeStruct((wide, columns), BF),
        compiler_params=params(),
        cost_estimate=pl.CostEstimate(flops=8 * wide * width * columns, bytes_accessed=8 * width * columns, transcendentals=0),
        name="expert_out",
    )(z, *hidden, down, *got)


def dense_out_kernel(z_ref, h0, h1, h2, h3, weight, out, held, *, rel):
    @pl.when(pl.program_id(0) == 0)
    def _():
        z = z_ref[0]
        for k, ref in enumerate((h0, h1, h2, h3)):
            at = pl.multiple_of(lax.rem(z + k, NZ) * 64, 64)
            held[pl.ds(at, 64), :] = ref[...]

    out[...] = jnp.dot(held[...], weight[...], preferred_element_type=F32).astype(out.dtype)


def out_proj_kernel(z_ref, h0, h1, h2, h3, weight, out, held, *, rel):
    @pl.when(pl.program_id(0) == 0)
    def _():
        z = z_ref[0]
        rows, cols = held.shape[0], h0.shape[0]
        row = lax.broadcasted_iota(jnp.int32, (rows, cols), 0)
        col = lax.broadcasted_iota(jnp.int32, (rows, cols), 1)
        match = col == (row >> 4) * 8 + rel * 4 + (row & 3)
        total = None
        for k, ref in enumerate((h0, h1, h2, h3)):
            hit = match & (((row >> 2) & 3) == lax.rem(z + k, NZ))
            term = jnp.dot(jnp.where(hit, 1.0, 0.0).astype(BF), ref[...], preferred_element_type=F32)
            total = term if total is None else total + term
        held[...] = total.astype(BF)

    out[...] = jnp.dot(held[...], weight[...], preferred_element_type=F32).astype(out.dtype)


def plane_dot(kernel, z, blocks, weight, rel, dtype):
    depth, columns = weight.shape
    step = 256
    block_rows, at = (64, rel) if kernel is dense_out_kernel else (128, 0)
    return pl.pallas_call(
        lambda *refs: kernel(*refs, rel=rel),
        grid_spec=pltpu.PrefetchScalarGridSpec(
            num_scalar_prefetch=1,
            grid=(columns // step,),
            in_specs=[pl.BlockSpec((block_rows, depth), lambda i, z: (at, 0))] * NZ
            + [pl.BlockSpec((depth, step), lambda i, z: (0, i))],
            out_specs=pl.BlockSpec((256, step), lambda i, z: (0, i)),
            scratch_shapes=[pltpu.VMEM((256, depth), BF)],
        ),
        out_shape=jax.ShapeDtypeStruct((256, columns), dtype),
        compiler_params=params(),
        cost_estimate=pl.CostEstimate(flops=512 * depth * columns, bytes_accessed=2 * depth * columns, transcendentals=0),
        name=("dense_out" if kernel is dense_out_kernel else "out_proj") + ("_other" if rel else "_own"),
    )(z, *blocks, weight)


def shards(
    queries, kv_cache, new_latent, lengths, residual, gain_first, gain_second, value_proj, out_proj,
    dense_gate, dense_up, dense_down, route_ids, route_gates, expert_gate, expert_up, expert_down,
):
    z = lax.axis_index("z")
    c = lax.axis_index("c")
    latent_dim = value_proj.shape[1]
    quarter = residual.shape[1]

    zs = z.astype(jnp.int32).reshape(1)

    def pick(w, k, axis):
        return lax.dynamic_slice_in_dim(w, lax.rem(z + k, NZ) * quarter, quarter, axis)

    def cut(w, axis, which):
        return {k: pick(w, NZ - k, axis) for k in which}

    def tied(value, *groups):
        flat = [group[k] for group in groups for k in group]
        value, *flat = lax.optimization_barrier((value, *flat))
        at = iter(flat)
        return (value, *[{k: next(at) for k in group} for group in groups])

    def fetch(group):
        return {k: zsend(group[k], NZ - k) for k in group}

    down_a = fetch(cut(expert_down[0], 1, (1, 3)))
    down_cut = cut(expert_down[0], 1, (2,))
    gains = zgather(gain_second.reshape(1, -1))

    latent = attend(queries, kv_cache, new_latent, lengths, latent_dim)
    latent = latent.reshape(4, 16, 2, 4, latent_dim)
    mine = lax.dynamic_index_in_dim(latent, c, 2, keepdims=False)
    theirs = lax.dynamic_index_in_dim(latent, 1 - c, 2, keepdims=False)
    theirs = swap_core(theirs)
    both = jnp.stack([mine, theirs], axis=0)
    both = both.transpose(2, 3, 0, 1, 4).reshape(16, 32, latent_dim)
    moved = lax.all_to_all(both, YX, 0, 0, tiled=True).reshape(16, 4, 8, latent_dim)
    moved, down_a, down_cut = tied(moved, down_a, down_cut)
    head_vals = jnp.einsum("nhpc,hcv->nphv", moved, value_proj, preferred_element_type=F32).astype(BF)
    head_vals = head_vals.reshape(128, -1)
    rows = zgather(head_vals)
    rows, down_cut = tied(rows, down_cut)
    down_b = fetch(down_cut)
    attn_out = plane_scatter(out_proj_kernel, zs, rows, out_proj)
    attn_out, down_b = tied(attn_out, down_b)
    first = residual.astype(F32) + attn_out

    def spread(values):
        wide = jnp.broadcast_to(values[None], (16,) + values.shape)
        own = lax.all_to_all(wide, YX, 0, 0, tiled=True).reshape(256, -1)
        return own, swap_core(own)

    own, other = spread(first.astype(BF))
    width = dense_gate.shape[1]
    own, other = lax.optimization_barrier((own, other))
    blocks = dense_in(zs, own, other, gain_first, dense_gate, dense_up)
    summed = zscatter(blocks)
    scale = lax.rsqrt((summed[:, 2 * width] + summed[:, 2 * width + 1]) / D + EPS)[:, None]
    gate_act = summed[:, :width] * scale
    hidden = (jax.nn.silu(gate_act) * (summed[:, width : 2 * width] * scale)).astype(BF)
    second = first + plane_scatter(dense_out_kernel, zs, zgather(hidden), dense_down)

    tok_group, top_count = route_ids.shape
    group_count, slots, cap = 32, 8, 6
    flat_ids = route_ids.reshape(-1)
    onehot = (flat_ids[:, None] == lax.broadcasted_iota(jnp.int32, (1, group_count), 1)).astype(jnp.int32)
    before = jnp.cumsum(onehot, axis=0) - onehot
    slot = jnp.sum(before * onehot, axis=1)
    position = (flat_ids * slots + slot).reshape(tok_group, top_count)
    columns = lax.broadcasted_iota(jnp.int32, (1, 1, group_count * slots), 2)
    matches = position[:, :, None] == columns
    combine_matrix = jnp.sum(jnp.where(matches, route_gates[:, :, None], 0.0), axis=1)
    wide = zgather(second.astype(BF))
    total = sum(jnp.sum(jnp.square(q.astype(F32)), axis=1, keepdims=True) for q in wide)
    scale = lax.rsqrt(total / D + EPS)
    normed = [(q.astype(F32) * scale * g.astype(F32)).astype(BF) for q, g in zip(wide, gains)]
    column = lax.broadcasted_iota(jnp.int32, (group_count * slots, 1, 1), 0)
    block, place = column >> 3, column & 7
    ids = flat_ids.reshape(1, tok_group, top_count)
    at = slot.reshape(1, tok_group, top_count)
    hot = lambda want: jnp.sum(((ids == block) & (at == want)).astype(jnp.int32), axis=2).astype(BF)
    head = hot(jnp.where(place < cap, place, -1))
    sendbuf = []
    for m in range(3):
        tail = hot(jnp.where(place >= cap, 3 * (place - cap) + m, -1))
        both = jnp.concatenate([normed[m], normed[3]], axis=0)
        sendbuf.append(jnp.dot(jnp.concatenate([head, tail], axis=1), both, preferred_element_type=F32).astype(BF))
    sendbuf = jnp.concatenate(sendbuf, axis=1).reshape(group_count, slots, -1)
    arrived = lax.all_to_all(sendbuf, ("y", "x", "c"), 0, 0, tiled=True).reshape(group_count * slots, -1)
    expert_hidden = expert_in(zs, arrived, expert_gate[0], expert_up[0], group_count * cap)
    result = expert_out(zs, zgather(expert_hidden), expert_down[0], [down_a[1], down_b[2], down_a[3]], group_count * slots)
    result = result.reshape(group_count, slots, -1)
    returned = lax.all_to_all(result, ("y", "x", "c"), 0, 0, tiled=True).reshape(group_count * slots, -1)
    moe_out = jnp.dot(combine_matrix, returned.astype(F32), precision=lax.Precision.HIGHEST)
    return (second + moe_out).astype(BF)


def solution(mesh):
    grid = Mesh(mesh.devices.reshape(4, 4, 2, 4), ("y", "x", "c", "z"))
    ep = ("y", "x", "c")
    both = ("y", "x", "c", "z")
    return jax.shard_map(
        shards,
        mesh=grid,
        in_specs=(
            P(both, None, None),
            P(both, None, None),
            P(both, None),
            P(both),
            P(ep, "z"),
            P("z"),
            P("z"),
            P(ep, None, None),
            P(ep, "z"),
            P("z", ep),
            P("z", ep),
            P(ep, "z"),
            P(ep, None),
            P(ep, None),
            P(ep, None, "z"),
            P(ep, None, "z"),
            P(ep, "z", None),
        ),
        out_specs=P(ep, "z"),
        check_vma=False,
    )
```

time: 342 us -> 249 us (0.73)
  waiting for transfers between devices: 198 us -> 79 us
  blocking collectives: 17.4 us -> 80.1 us
  matrix products: 37.5 us -> 6.26 us
  Pallas kernels: 0 us -> 21.8 us
  local copies, waits for them, and re-layouts: 17.3 us -> 4.62 us
  starting transfers between devices: 59.4 us -> 48.8 us
    ppermute x24 -> x21, waiting for transfers between devices: 130 us -> 31.6 us  [zsend(): return lax.ppermute(values, 'z', [(i, (i + shift) % NZ) for i in range(NZ)])]
    all_to_all x0 -> x2, blocking collectives: none -> 62.8 us  [the longest x1 42.5 us: shards(): lax.all_to_all(sendbuf, ('y', 'x', 'c'), 0, 0, tiled=True)]
    dot_general x21 -> x3, matrix products: 31.2 us -> 1.26 us  [shards(): jnp.dot(jnp.concatenate([head, tail], axis=1), both, preferred_element_ty...]
    pallas_call x0 -> x7, Pallas kernels: none -> 21.8 us  [the longest x4 8.36 us: plane_dot(): pl.pallas_call(lambda *refs: kernel(*refs, rel=rel), grid_spec=pltpu.Pref...]
    all_to_all x2 -> x0, waiting for transfers between devices: 19.2 us -> none  [the longest x1 14 us: spread(): own = lax.all_to_all(wide, YX, 0, 0, tiled=True).reshape(256, -1)]
    all_to_all x2 -> x0, starting transfers between devices: 9.12 us -> none  [the longest x1 5.25 us: shards(): lax.all_to_all(sendbuf.reshape(group_count, slots, -1), ('y', 'x', 'c'),...]
    all_to_all x1, starting transfers between devices: 9.08 us -> 5.39 us  [shards(): lax.all_to_all(result, ('y', 'x', 'c'), 0, 0, tiled=True)]
    ppermute x24 -> x21, starting transfers between devices: 25.7 us -> 27.6 us  [zsend(): return lax.ppermute(values, 'z', [(i, (i + shift) % NZ) for i in range(NZ)])]
  transfers between devices with their start and end apart: 33 -> 28, of which waited for: 27 -> 20; matrix products, arithmetic and copies ran while one was open for 10% -> 4% of each run, Pallas kernels for 0% -> 2%
where the time goes in v2:
time: 249 us
  blocking collectives  80.1 us (32%)
  waiting for transfers between devices  79 us (32%)
  starting transfers between devices  48.8 us (20%)
  Pallas kernels  21.8 us (9%)
  other arithmetic  7.63 us (3%)
  matrix products  6.26 us (3%)
  local copies, waits for them, and re-layouts  4.62 us (2%)
    all_to_all x1, blocking collectives, shards(): lax.all_to_all(sendbuf, ('y', 'x', 'c'), 0, 0, tiled=True)  42.5 us
    ppermute x21, waiting for transfers between devices, zsend(): return lax.ppermute(values, 'z', [(i, (i + shift) % NZ) for i in range(NZ)])  31.6 us
    all_to_all x2, waiting for transfers between devices, plane_scatter(): parts = lax.all_to_all(mine.reshape(16, 16, -1), YX, 0, 0, tiled=True)  28.6 us
    ppermute x21, starting transfers between devices, zsend(): return lax.ppermute(values, 'z', [(i, (i + shift) % NZ) for i in range(NZ)])  27.6 us
    all_to_all x1, blocking collectives, spread(): own = lax.all_to_all(wide, YX, 0, 0, tiled=True).reshape(256, -1)  20.3 us
    all_to_all x1, blocking collectives, shards(): lax.all_to_all(both, YX, 0, 0, tiled=True).reshape(16, 4, 8, latent_dim)  17.3 us
    all_to_all x1, waiting for transfers between devices, shards(): lax.all_to_all(result, ('y', 'x', 'c'), 0, 0, tiled=True)  15.6 us
    pallas_call x4, Pallas kernels, plane_dot(): pl.pallas_call(lambda *refs: kernel(*refs, rel=rel), grid_spec=pltpu.Pref...  8.36 us
  transfers between devices with their start and end apart: 28, of which 20 were waited for; matrix products, arithmetic and copies ran while one was open for 4% of the time, Pallas kernels for 2%

profile of v2, /device:TPU:1, one launch (start us, length us, event | category | flops | bytes accessed | tf_op | source)
XLA Modules:
  0.0 248.7 jit_solution(3024137074723265710)
XLA Ops:
  0.0 3.4 %dynamic-slice_bitcast_fusion = (bf16[256,1792]{1,0:T(8,128)(2,1)}, bf16[256,1792]{1,0:T(8,128)(2,1)}, bf16[256,1792]{1,0:T(8,128)(2,1)}) fusion(bf16[1,256,7168]{2,1,0:T(8,128)(2,1)} %param.33, s32[]{:T(128)S(6)} %select_n.62, s32[]{:T(128)S(6)} %select_n.61, s32[]{:T(128)S(6)} %select_n.60), kind=kLoop, calls=%fused_computation.22 | loop fusion | bytes 5505036 | tf_op jit(solution)/shard_map/dynamic_slice | solution.py:296
  3.4 2.5 collective-permute-start.2
  8.3 2.5 %fusion.55 = (f32[4,128]{1,0:T(4,128)S(1)}, f32[4,128,512]{2,1,0:T(8,128)S(1)}) fusion(bf16[4,128,576]{1,2,0:T(8,128)(2,1)S(1)} %copy-done, bf16[4,512,576]{1,2,0:T(8,128)(2,1)} %param.18, pred[4,512]{1,0:T(4,128)(4,1)S(1)} %iota_compare_fusion.2), kind=kOutput, calls=%fused_computation.119 | convolution fusion | flops 302775808 | bytes 4001792 | tf_op jit(solution)/shard_map/rhc,rjc->rhj/dot_general | solution.py:48
  15.0 17.3 %all_to_all.30 = bf16[16,32,512]{2,1,0:T(8,128)(2,1)S(1)} all-to-all(bf16[16,32,512]{2,1,0:T(8,128)(2,1)S(1)} %copy.47), channel_id=1, replica_groups=mesh['y'=4,'x'=4,'c'=2,'z'=4] {'y','x'}, dimensions={0} | all-to-all | bytes 1048576 | tf_op jit(solution)/shard_map/all_to_all | solution.py:321
  32.7 2.9 %collective-permute-start.4 = (bf16[128,512]{1,0:T(8,128)(2,1)S(1)}, bf16[128,512]{1,0:T(8,128)(2,1)S(1)}, u32[]{:S(2)}, u32[]{:S(2)}) collective-permute-start(bf16[128,512]{1,0:T(8,128)(2,1)S(1)} %bitcast.61), channel_id=1, source_target_pairs={{0,2},{1,3},{2,0},{3,1},{4,6},{5,7},{6,4},{7,5},{8,10},{9,11},{10,... | collective-permute-start | bytes 393224 | tf_op jit(solution)/shard_map/ppermute | solution.py:19
  42.6 3.1 %collective-permute-start.6 = (bf16[256,1792]{1,0:T(8,128)(2,1)S(1)}, bf16[256,1792]{1,0:T(8,128)(2,1)S(1)}, u32[]{:S(2)}, u32[]{:S(2)}) collective-permute-start(bf16[256,1792]{1,0:T(8,128)(2,1)S(1)} %out_proj_other.1), channel_id=1, source_target_pairs={{0,4},{4,0},{1,5},{5,1},{2,6},{6,2},{3,7},{7,3},{8,12},{12,8},{9,1... | collective-permute-start | bytes 2752520 | tf_op jit(solution)/shard_map/ppermute | solution.py:23
  49.1 4.3 %all-to-all-start.1 = ((bf16[16,16,1792]{2,1,0:T(8,128)(2,1)}), bf16[16,16,1792]{2,1,0:T(8,128)(2,1)}, u32[]{:S(2)}, u32[]{:S(2)}) async-start(bf16[16,16,1792]{2,1,0:T(8,128)(2,1)} %bitcast.17), calls=%async_computation.1 | async-start | bytes 1835008 | tf_op jit(solution)/shard_map/all_to_all | solution.py:41
  55.1 14.6 %all-to-all-done.1 = bf16[16,16,1792]{2,1,0:T(8,128)(2,1)} async-done(((bf16[16,16,1792]{2,1,0:T(8,128)(2,1)}), bf16[16,16,1792]{2,1,0:T(8,128)(2,1)}, u32[]{:S(2)}, u32[]{:S(2)}) %all-to-all-start.1) | async-done | bytes 917536 | tf_op jit(solution)/shard_map/all_to_all | solution.py:41
  71.1 5.9 %collective-permute-done.7.refs_6_ = bf16[256,1792]{1,0:T(8,128)(2,1)S(1)} collective-permute-done((bf16[256,1792]{1,0:T(8,128)(2,1)}, bf16[256,1792]{1,0:T(8,128)(2,1)S(1)}, u32[]{:S(2)}, u32[]{:S(2)}) %collective-permute-start.7) | collective-permute-done | bytes 917536 | tf_op jit(solution)/shard_map/ppermute | solution.py:19
  77.1 20.3 %all_to_all.31 = bf16[16,16,1792]{2,1,0:T(8,128)(2,1)S(1)} all-to-all(bf16[16,16,1792]{2,1,0:T(8,128)(2,1)S(1)} %broadcast_in_dim.51), channel_id=1, replica_groups=mesh['y'=4,'x'=4,'c'=2,'z'=4] {'y','x'}, dimensions={0} | all-to-all | bytes 1835008 | tf_op jit(solution)/shard_map/all_to_all | solution.py:334
  102.0 3.6 %dense_in.1 = (bf16[128,896]{1,0:T(8,128)(2,1)S(1)}, bf16[128,896]{1,0:T(8,128)(2,1)S(1)}, bf16[128,896]{1,0:T(8,128)(2,1)S(1)}, bf16[128,896]{1,0:T(8,128)(2,1)S(1)}) custom-call(s32[1]{0:T(128)} %bitcast.refs_0_.z_ref, bf16[256,1792]{1,0:T(8,128)(2,1)S(1)} %bitcast.66, bf16[256,1792]{1,0:T(8,128)(2,1)S(1)} %collective-permute-done.8.other, ...), custom_call_target="tpu_custom_call" | custom-call | flops 1409286144 | bytes 4587520 | tf_op jit(solution)/shard_map/dense_in/pallas_call | solution.py:112
  106.6 2.6 %collective-permute-start.10 = (bf16[128,896]{1,0:T(8,128)(2,1)S(1)}, bf16[128,896]{1,0:T(8,128)(2,1)S(1)}, u32[]{:S(2)}, u32[]{:S(2)}) collective-permute-start(bf16[128,896]{1,0:T(8,128)(2,1)S(1)} %get-tuple-element.34), channel_id=1, source_target_pairs={{0,2},{1,3},{2,0},{3,1},{4,6},{5,7},{6,4},{7,5},{8,10},{9,11},{10,... | collective-permute-start | bytes 688136 | tf_op jit(solution)/shard_map/ppermute | solution.py:19
  109.3 4.4 %collective-permute-done.9 = bf16[128,896]{1,0:T(8,128)(2,1)S(1)} collective-permute-done((bf16[128,896]{1,0:T(8,128)(2,1)S(1)}, bf16[128,896]{1,0:T(8,128)(2,1)S(1)}, u32[]{:S(2)}, u32[]{:S(2)}) %collective-permute-start.9) | collective-permute-done | bytes 229408 | tf_op jit(solution)/shard_map/ppermute | solution.py:19
  113.7 5.8 %collective-permute-done.10 = bf16[128,896]{1,0:T(8,128)(2,1)S(1)} collective-permute-done((bf16[128,896]{1,0:T(8,128)(2,1)S(1)}, bf16[128,896]{1,0:T(8,128)(2,1)S(1)}, u32[]{:S(2)}, u32[]{:S(2)}) %collective-permute-start.10) | collective-permute-done | bytes 229408 | tf_op jit(solution)/shard_map/ppermute | solution.py:19
  121.4 2.6 %collective-permute-start.13 = (bf16[128,384]{1,0:T(8,128)(2,1)S(1)}, bf16[128,384]{1,0:T(8,128)(2,1)S(1)}, u32[]{:S(2)}, u32[]{:S(2)}) collective-permute-start(bf16[128,384]{1,0:T(8,128)(2,1)S(1)} %fusion.18.refs_1_), channel_id=1, source_target_pairs={{0,2},{1,3},{2,0},{3,1},{4,6},{5,7},{6,4},{7,5},{8,10},{9,11},{10,... | collective-permute-start | bytes 294920 | tf_op jit(solution)/shard_map/ppermute | solution.py:19
  124.8 3.7 %collective-permute-done.13.refs_3_ = bf16[128,384]{1,0:T(8,128)(2,1)S(1)} collective-permute-done((bf16[128,384]{1,0:T(8,128)(2,1)S(1)}, bf16[128,384]{1,0:T(8,128)(2,1)S(1)}, u32[]{:S(2)}, u32[]{:S(2)}) %collective-permute-start.13) | collective-permute-done | bytes 98336 | tf_op jit(solution)/shard_map/ppermute | solution.py:19
  139.1 3.6 %all-to-all-start.3 = ((bf16[16,16,1792]{2,1,0:T(8,128)(2,1)}), bf16[16,16,1792]{2,1,0:T(8,128)(2,1)S(1)}, u32[]{:S(2)}, u32[]{:S(2)}) async-start(bf16[16,16,1792]{2,1,0:T(8,128)(2,1)} %bitcast.19), calls=%async_computation.3 | async-start | bytes 1835008 | tf_op jit(solution)/shard_map/all_to_all | solution.py:41
  143.7 14.0 %all-to-all-done.3 = bf16[16,16,1792]{2,1,0:T(8,128)(2,1)S(1)} async-done(((bf16[16,16,1792]{2,1,0:T(8,128)(2,1)}), bf16[16,16,1792]{2,1,0:T(8,128)(2,1)S(1)}, u32[]{:S(2)}, u32[]{:S(2)}) %all-to-all-start.3) | async-done | bytes 917536 | tf_op jit(solution)/shard_map/all_to_all | solution.py:41
  158.8 2.9 %collective-permute-start.17 = (bf16[16,1792]{1,0:T(8,128)(2,1)S(1)}, bf16[16,1792]{1,0:T(8,128)(2,1)S(1)}, u32[]{:S(2)}, u32[]{:S(2)}) collective-permute-start(bf16[16,1792]{1,0:T(8,128)(2,1)S(1)} %get-tuple-element.44), channel_id=1, source_target_pairs={{0,2},{1,3},{2,0},{3,1},{4,6},{5,7},{6,4},{7,5},{8,10},{9,11},{10,... | collective-permute-start | bytes 172040 | tf_op jit(solution)/shard_map/ppermute | solution.py:19
  166.6 42.5 %all_to_all.32 = bf16[32,8,5376]{2,1,0:T(8,128)(2,1)S(1)} all-to-all(bf16[32,8,5376]{2,1,0:T(8,128)(2,1)S(1)} %maximum_bitcast_fusion), channel_id=1, replica_groups=mesh['y'=4,'x'=4,'c'=2,'z'=4] {'y','x','c'}, dimensions={0} | all-to-all | bytes 5505024 | tf_op jit(solution)/shard_map/all_to_all | solution.py:373
  209.1 5.4 %expert_in.1.refs_0_ = bf16[192,256]{1,0:T(8,128)(2,1)S(1)} custom-call(s32[1]{0:T(128)} %bitcast.refs_0_.z_ref, bf16[256,5376]{1,0:T(8,128)(2,1)S(1)} %bitcast.56, bf16[256,5376]{1,0:T(8,128)(2,1)S(1)} %bitcast.57, bf16[256,5376]{1,0:T(8,128)(2,1)S(1)} %bitcast.58, bf16[7168,256]{1,0:T(8,128)(2,1)S(1)} %bitcast.48, bf16[7168,256]{1,0:T(8,128)(2,1)S(1)} %bitcast.49, ...), custom_call_target="tpu_custom_call" | custom-call | flops 1409286144 | bytes 7340032 | tf_op jit(solution)/shard_map/expert_in/pallas_call | solution.py:175
  222.0 4.4 %expert_out.1 = bf16[256,1792]{1,0:T(8,128)(2,1)} custom-call(s32[1]{0:T(128)} %bitcast.refs_0_.z_ref, bf16[192,256]{1,0:T(8,128)(2,1)S(1)} %expert_in.1.refs_0_, bf16[192,256]{1,0:T(8,128)(2,1)S(1)} %collective-permute-done.22.refs_1_, bf16[192,256]{1,0:T(8,128)(2,1)S(1)} %collective-permute-done.23.refs_2_, ...), custom_call_target="tpu_custom_call" | custom-call | flops 939524096 | bytes 3670016 | tf_op jit(solution)/shard_map/expert_out/pallas_call | solution.py:216
  226.4 5.4 %all-to-all-start.5 = ((bf16[32,8,1792]{2,1,0:T(8,128)(2,1)}), bf16[32,8,1792]{2,1,0:T(8,128)(2,1)S(1)}, u32[]{:S(2)}, u32[]{:S(2)}) async-start(bf16[32,8,1792]{2,1,0:T(8,128)(2,1)} %bitcast.25), calls=%async_computation.5 | async-start | bytes 1835008 | tf_op jit(solution)/shard_map/all_to_all | solution.py:377
  232.0 15.6 %all-to-all-done.5 = bf16[32,8,1792]{2,1,0:T(8,128)(2,1)S(1)} async-done(((bf16[32,8,1792]{2,1,0:T(8,128)(2,1)}), bf16[32,8,1792]{2,1,0:T(8,128)(2,1)S(1)}, u32[]{:S(2)}, u32[]{:S(2)}) %all-to-all-start.5) | async-done | bytes 917536 | tf_op jit(solution)/shard_map/all_to_all | solution.py:377
  (148 shorter events, 54.8 us)
Async XLA Ops:
  3.4 28.9 %collective-permute-start.2 = (bf16[256,1792]{1,0:T(8,128)(2,1)}, bf16[256,1792]{1,0:T(8,128)(2,1)S(1)}, u32[]{:S(2)}, u32[]{:S(2)}) collective-permute-start(bf16[256,1792]{1,0:T(8,128)(2,1)} %get-tuple-element.46), channel_id=1, source_target_pairs={{0,1},{1,2},{2,3},{3,0},{4,5},{5,6},{6,7},{7,4},{8,9},{9,10},{10,1... | collective-permute-start | bytes 2752520 | tf_op jit(solution)/shard_map/ppermute | solution.py:19
  5.9 26.4 %collective-permute-start.1 = (bf16[256,1792]{1,0:T(8,128)(2,1)}, bf16[256,1792]{1,0:T(8,128)(2,1)S(1)}, u32[]{:S(2)}, u32[]{:S(2)}) collective-permute-start(bf16[256,1792]{1,0:T(8,128)(2,1)} %get-tuple-element.47), channel_id=1, source_target_pairs={{0,3},{1,0},{2,1},{3,2},{4,7},{5,4},{6,5},{7,6},{8,11},{9,8},{10,9... | collective-permute-start | bytes 2752520 | tf_op jit(solution)/shard_map/ppermute | solution.py:19
  32.7 5.1 %collective-permute-start.5 = (bf16[128,512]{1,0:T(8,128)(2,1)S(1)}, bf16[128,512]{1,0:T(8,128)(2,1)S(1)}, u32[]{:S(2)}, u32[]{:S(2)}) collective-permute-start(bf16[128,512]{1,0:T(8,128)(2,1)S(1)} %bitcast.60), channel_id=1, source_target_pairs={{0,1},{1,2},{2,3},{3,0},{4,5},{5,6},{6,7},{7,4},{8,9},{9,10},{10,1... | collective-permute-start | bytes 393224 | tf_op jit(solution)/shard_map/ppermute | solution.py:19
  32.7 7.2 %collective-permute-start.4 = (bf16[128,512]{1,0:T(8,128)(2,1)S(1)}, bf16[128,512]{1,0:T(8,128)(2,1)S(1)}, u32[]{:S(2)}, u32[]{:S(2)}) collective-permute-start(bf16[128,512]{1,0:T(8,128)(2,1)S(1)} %bitcast.61), channel_id=1, source_target_pairs={{0,2},{1,3},{2,0},{3,1},{4,6},{5,7},{6,4},{7,5},{8,10},{9,11},{10,... | collective-permute-start | bytes 393224 | tf_op jit(solution)/shard_map/ppermute | solution.py:19
  35.7 4.6 %collective-permute-start.3 = (bf16[128,512]{1,0:T(8,128)(2,1)S(1)}, bf16[128,512]{1,0:T(8,128)(2,1)S(1)}, u32[]{:S(2)}, u32[]{:S(2)}) collective-permute-start(bf16[128,512]{1,0:T(8,128)(2,1)S(1)} %bitcast.62), channel_id=1, source_target_pairs={{0,3},{1,0},{2,1},{3,2},{4,7},{5,4},{6,5},{7,6},{8,11},{9,8},{10,9... | collective-permute-start | bytes 393224 | tf_op jit(solution)/shard_map/ppermute | solution.py:19
  42.6 5.4 %collective-permute-start.6 = (bf16[256,1792]{1,0:T(8,128)(2,1)S(1)}, bf16[256,1792]{1,0:T(8,128)(2,1)S(1)}, u32[]{:S(2)}, u32[]{:S(2)}) collective-permute-start(bf16[256,1792]{1,0:T(8,128)(2,1)S(1)} %out_proj_other.1), channel_id=1, source_target_pairs={{0,4},{4,0},{1,5},{5,1},{2,6},{6,2},{3,7},{7,3},{8,12},{12,8},{9,1... | collective-permute-start | bytes 2752520 | tf_op jit(solution)/shard_map/ppermute | solution.py:23
  49.1 20.6 %all-to-all-start.1 = ((bf16[16,16,1792]{2,1,0:T(8,128)(2,1)}), bf16[16,16,1792]{2,1,0:T(8,128)(2,1)}, u32[]{:S(2)}, u32[]{:S(2)}) async-start(bf16[16,16,1792]{2,1,0:T(8,128)(2,1)} %bitcast.17), calls=%async_computation.1 | async-start | bytes 1835008 | tf_op jit(solution)/shard_map/all_to_all | solution.py:41
  53.5 23.6 %collective-permute-start.7 = (bf16[256,1792]{1,0:T(8,128)(2,1)}, bf16[256,1792]{1,0:T(8,128)(2,1)S(1)}, u32[]{:S(2)}, u32[]{:S(2)}) collective-permute-start(bf16[256,1792]{1,0:T(8,128)(2,1)} %get-tuple-element.28), channel_id=1, source_target_pairs={{0,2},{1,3},{2,0},{3,1},{4,6},{5,7},{6,4},{7,5},{8,10},{9,11},{10,... | collective-permute-start | bytes 2752520 | tf_op jit(solution)/shard_map/ppermute | solution.py:19
  105.6 8.1 %collective-permute-start.9 = (bf16[128,896]{1,0:T(8,128)(2,1)S(1)}, bf16[128,896]{1,0:T(8,128)(2,1)S(1)}, u32[]{:S(2)}, u32[]{:S(2)}) collective-permute-start(bf16[128,896]{1,0:T(8,128)(2,1)S(1)} %get-tuple-element.33), channel_id=1, source_target_pairs={{0,1},{1,2},{2,3},{3,0},{4,5},{5,6},{6,7},{7,4},{8,9},{9,10},{10,1... | collective-permute-start | bytes 688136 | tf_op jit(solution)/shard_map/ppermute | solution.py:19
  106.6 12.9 %collective-permute-start.10 = (bf16[128,896]{1,0:T(8,128)(2,1)S(1)}, bf16[128,896]{1,0:T(8,128)(2,1)S(1)}, u32[]{:S(2)}, u32[]{:S(2)}) collective-permute-start(bf16[128,896]{1,0:T(8,128)(2,1)S(1)} %get-tuple-element.34), channel_id=1, source_target_pairs={{0,2},{1,3},{2,0},{3,1},{4,6},{5,7},{6,4},{7,5},{8,10},{9,11},{10,... | collective-permute-start | bytes 688136 | tf_op jit(solution)/shard_map/ppermute | solution.py:19
  109.2 10.3 %collective-permute-start.11 = (bf16[128,896]{1,0:T(8,128)(2,1)S(1)}, bf16[128,896]{1,0:T(8,128)(2,1)S(1)}, u32[]{:S(2)}, u32[]{:S(2)}) collective-permute-start(bf16[128,896]{1,0:T(8,128)(2,1)S(1)} %get-tuple-element.35), channel_id=1, source_target_pairs={{0,3},{1,0},{2,1},{3,2},{4,7},{5,4},{6,5},{7,6},{8,11},{9,8},{10,9... | collective-permute-start | bytes 688136 | tf_op jit(solution)/shard_map/ppermute | solution.py:19
  120.0 4.9 %collective-permute-start.14 = (bf16[128,384]{1,0:T(8,128)(2,1)S(1)}, bf16[128,384]{1,0:T(8,128)(2,1)S(1)}, u32[]{:S(2)}, u32[]{:S(2)}) collective-permute-start(bf16[128,384]{1,0:T(8,128)(2,1)S(1)} %fusion.18.refs_1_), channel_id=1, source_target_pairs={{0,1},{1,2},{2,3},{3,0},{4,5},{5,6},{6,7},{7,4},{8,9},{9,10},{10,1... | collective-permute-start | bytes 294920 | tf_op jit(solution)/shard_map/ppermute | solution.py:19
  121.4 7.1 %collective-permute-start.13 = (bf16[128,384]{1,0:T(8,128)(2,1)S(1)}, bf16[128,384]{1,0:T(8,128)(2,1)S(1)}, u32[]{:S(2)}, u32[]{:S(2)}) collective-permute-start(bf16[128,384]{1,0:T(8,128)(2,1)S(1)} %fusion.18.refs_1_), channel_id=1, source_target_pairs={{0,2},{1,3},{2,0},{3,1},{4,6},{5,7},{6,4},{7,5},{8,10},{9,11},{10,... | collective-permute-start | bytes 294920 | tf_op jit(solution)/shard_map/ppermute | solution.py:19
  124.0 4.8 %collective-permute-start.12 = (bf16[128,384]{1,0:T(8,128)(2,1)S(1)}, bf16[128,384]{1,0:T(8,128)(2,1)S(1)}, u32[]{:S(2)}, u32[]{:S(2)}) collective-permute-start(bf16[128,384]{1,0:T(8,128)(2,1)S(1)} %fusion.18.refs_1_), channel_id=1, source_target_pairs={{0,3},{1,0},{2,1},{3,2},{4,7},{5,4},{6,5},{7,6},{8,11},{9,8},{10,9... | collective-permute-start | bytes 294920 | tf_op jit(solution)/shard_map/ppermute | solution.py:19
  130.7 6.1 %collective-permute-start.15 = (bf16[256,1792]{1,0:T(8,128)(2,1)S(1)}, bf16[256,1792]{1,0:T(8,128)(2,1)}, u32[]{:S(2)}, u32[]{:S(2)}) collective-permute-start(bf16[256,1792]{1,0:T(8,128)(2,1)S(1)} %dense_out_other.1), channel_id=1, source_target_pairs={{0,4},{4,0},{1,5},{5,1},{2,6},{6,2},{3,7},{7,3},{8,12},{12,8},{9,1... | collective-permute-start | bytes 2752520 | tf_op jit(solution)/shard_map/ppermute | solution.py:23
  132.0 11.6 %collective-permute-start.21 = (bf16[1,1792]{1,0:T(2,128)(2,1)S(1)}, bf16[1,1792]{1,0:T(2,128)(2,1)S(1)}, u32[]{:S(2)}, u32[]{:S(2)}) collective-permute-start(bf16[1,1792]{1,0:T(2,128)(2,1)S(1)} %reshape.145), channel_id=1, source_target_pairs={{0,2},{1,3},{2,0},{3,1},{4,6},{5,7},{6,4},{7,5},{8,10},{9,11},{10,... | collective-permute-start | bytes 10760 | tf_op jit(solution)/shard_map/ppermute | solution.py:19
  133.0 10.7 %collective-permute-start.20 = (bf16[1,1792]{1,0:T(2,128)(2,1)S(1)}, bf16[1,1792]{1,0:T(2,128)(2,1)S(1)}, u32[]{:S(2)}, u32[]{:S(2)}) collective-permute-start(bf16[1,1792]{1,0:T(2,128)(2,1)S(1)} %reshape.145), channel_id=1, source_target_pairs={{0,3},{1,0},{2,1},{3,2},{4,7},{5,4},{6,5},{7,6},{8,11},{9,8},{10,9... | collective-permute-start | bytes 10760 | tf_op jit(solution)/shard_map/ppermute | solution.py:19
  134.8 24.0 %collective-permute-start.19 = (bf16[1,1792]{1,0:T(2,128)(2,1)S(1)}, bf16[1,1792]{1,0:T(2,128)(2,1)S(1)}, u32[]{:S(2)}, u32[]{:S(2)}) collective-permute-start(bf16[1,1792]{1,0:T(2,128)(2,1)S(1)} %reshape.145), channel_id=1, source_target_pairs={{0,1},{1,2},{2,3},{3,0},{4,5},{5,6},{6,7},{7,4},{8,9},{9,10},{10,1... | collective-permute-start | bytes 10760 | tf_op jit(solution)/shard_map/ppermute | solution.py:19
  139.1 18.6 %all-to-all-start.3 = ((bf16[16,16,1792]{2,1,0:T(8,128)(2,1)}), bf16[16,16,1792]{2,1,0:T(8,128)(2,1)S(1)}, u32[]{:S(2)}, u32[]{:S(2)}) async-start(bf16[16,16,1792]{2,1,0:T(8,128)(2,1)} %bitcast.19), calls=%async_computation.3 | async-start | bytes 1835008 | tf_op jit(solution)/shard_map/all_to_all | solution.py:41
  158.8 4.9 %collective-permute-start.17 = (bf16[16,1792]{1,0:T(8,128)(2,1)S(1)}, bf16[16,1792]{1,0:T(8,128)(2,1)S(1)}, u32[]{:S(2)}, u32[]{:S(2)}) collective-permute-start(bf16[16,1792]{1,0:T(8,128)(2,1)S(1)} %get-tuple-element.44), channel_id=1, source_target_pairs={{0,2},{1,3},{2,0},{3,1},{4,6},{5,7},{6,4},{7,5},{8,10},{9,11},{10,... | collective-permute-start | bytes 172040 | tf_op jit(solution)/shard_map/ppermute | solution.py:19
  214.5 5.7 %collective-permute-start.24 = (bf16[192,256]{1,0:T(8,128)(2,1)S(1)}, bf16[192,256]{1,0:T(8,128)(2,1)S(1)}, u32[]{:S(2)}, u32[]{:S(2)}) collective-permute-start(bf16[192,256]{1,0:T(8,128)(2,1)S(1)} %expert_in.1.refs_0_), channel_id=1, source_target_pairs={{0,1},{1,2},{2,3},{3,0},{4,5},{5,6},{6,7},{7,4},{8,9},{9,10},{10,1... | collective-permute-start | bytes 294920 | tf_op jit(solution)/shard_map/ppermute | solution.py:19
  214.6 6.7 %collective-permute-start.23 = (bf16[192,256]{1,0:T(8,128)(2,1)S(1)}, bf16[192,256]{1,0:T(8,128)(2,1)S(1)}, u32[]{:S(2)}, u32[]{:S(2)}) collective-permute-start(bf16[192,256]{1,0:T(8,128)(2,1)S(1)} %expert_in.1.refs_0_), channel_id=1, source_target_pairs={{0,2},{1,3},{2,0},{3,1},{4,6},{5,7},{6,4},{7,5},{8,10},{9,11},{10,... | collective-permute-start | bytes 294920 | tf_op jit(solution)/shard_map/ppermute | solution.py:19
  216.9 5.0 %collective-permute-start.22 = (bf16[192,256]{1,0:T(8,128)(2,1)S(1)}, bf16[192,256]{1,0:T(8,128)(2,1)S(1)}, u32[]{:S(2)}, u32[]{:S(2)}) collective-permute-start(bf16[192,256]{1,0:T(8,128)(2,1)S(1)} %expert_in.1.refs_0_), channel_id=1, source_target_pairs={{0,3},{1,0},{2,1},{3,2},{4,7},{5,4},{6,5},{7,6},{8,11},{9,8},{10,9... | collective-permute-start | bytes 294920 | tf_op jit(solution)/shard_map/ppermute | solution.py:19
  226.4 21.2 %all-to-all-start.5 = ((bf16[32,8,1792]{2,1,0:T(8,128)(2,1)}), bf16[32,8,1792]{2,1,0:T(8,128)(2,1)S(1)}, u32[]{:S(2)}, u32[]{:S(2)}) async-start(bf16[32,8,1792]{2,1,0:T(8,128)(2,1)} %bitcast.25), calls=%async_computation.5 | async-start | bytes 1835008 | tf_op jit(solution)/shard_map/all_to_all | solution.py:377
  (27 other events, 518.7 us)

commit v3 on v2

v3 whole, which is shorter than its diff:
```python
import jax
import jax.numpy as jnp
from jax import lax
from jax.experimental import pallas as pl
from jax.experimental.pallas import tpu as pltpu
from jax.sharding import Mesh, PartitionSpec as P

D = 7168
ROPE = 64
VD = 128
EPS = 1e-06
YX = ("y", "x")
NZ = 4
BF = jnp.bfloat16
F32 = jnp.float32


def zsend(values, shift):
    return lax.ppermute(values, "z", [(i, (i + shift) % NZ) for i in range(NZ)])


def swap_core(values):
    return lax.ppermute(values, "c", [(0, 1), (1, 0)])


def zgather(values):
    return [values] + [zsend(values, NZ - k) for k in (1, 2, 3)]


def zscatter(blocks):
    got = [zsend(blocks[k], k) for k in (1, 2, 3)]
    total = blocks[0].astype(F32)
    for piece in got:
        total = total + piece.astype(F32)
    return total


def plane_scatter(kernel, z, blocks, weight):
    arrived = swap_core(plane_dot(kernel, z, blocks, weight, 1))
    mine = plane_dot(kernel, z, blocks, weight, 0, arrived)
    return lax.all_to_all(mine.reshape(16, 16, -1), YX, 0, 0, tiled=True)


def onehot(hit):
    return jnp.where(hit, 1.0, 0.0).astype(BF)


def grid_of(shape):
    return lax.broadcasted_iota(jnp.int32, shape, 0), lax.broadcasted_iota(jnp.int32, shape, 1)


def exact(a, b):
    return jnp.dot(a, b, preferred_element_type=F32).astype(BF)


def attend_kernel(len_ref, c_ref, q_ref, kv_ref, new_ref, keep, send, latents):
    step = pl.program_id(0)
    heads = q_ref.shape[2]
    half = heads // 2
    lat = latents.shape[3]
    row, col = grid_of((heads, heads))
    core = jnp.where(row < half, c_ref[0], 1 - c_ref[0])
    order = onehot(col == ((row >> 2) & 15) * 8 + core * 4 + (row & 3))
    new = new_ref[...].astype(F32)
    score_scale = (VD + ROPE) ** (-0.5)
    for i in range(q_ref.shape[0]):
        r = step * q_ref.shape[0] + i
        q = lax.dot_general(order, q_ref[i], (((1,), (1,)), ((), ())), preferred_element_type=F32)
        fresh = jnp.sum(jnp.where(lax.broadcasted_iota(jnp.int32, new.shape, 0) == r, new, 0.0), axis=0, keepdims=True)
        scores = jnp.dot(q.astype(BF), kv_ref[i], preferred_element_type=F32) * score_scale
        self_score = jnp.sum(q * fresh, axis=1, keepdims=True) * score_scale
        live = lax.broadcasted_iota(jnp.int32, (1, scores.shape[1]), 1) < len_ref[r]
        scores = jnp.where(live, scores, -jnp.inf)
        top = jnp.maximum(jnp.max(scores, axis=1, keepdims=True), self_score)
        expo = jnp.exp(scores - top)
        self_expo = jnp.exp(self_score - top)
        total = jnp.sum(expo, axis=1, keepdims=True) + self_expo
        weights = (expo / total).astype(BF)
        self_weight = (self_expo / total).astype(BF).astype(F32)
        latent = lax.dot_general(weights, kv_ref[i, :lat, :], (((1,), (1,)), ((), ())), preferred_element_type=F32)
        latent = (latent + self_weight * fresh[:, :lat]).astype(BF)
        latents[0, r] = latent[:half]
        latents[1, r] = latent[half:]

    @pl.when(step == pl.num_programs(0) - 1)
    def _():
        rows = keep.shape[0]
        row, col = grid_of((rows, rows))
        order = onehot(col == ((row >> 2) & 3) * half + (row >> 4) * 4 + (row & 3))
        keep[...] = exact(order, latents[0].reshape(rows, lat))
        send[...] = exact(order, latents[1].reshape(rows, lat))


def attend(lengths, c, queries, kv_cache, new_latent, lat):
    reqs, heads, width = queries.shape
    slots = kv_cache.shape[1]
    rows = reqs * heads // 2
    out = pl.BlockSpec((rows, lat), lambda r, n, c: (0, 0))
    return pl.pallas_call(
        attend_kernel,
        grid_spec=pltpu.PrefetchScalarGridSpec(
            num_scalar_prefetch=2,
            grid=(reqs // 2,),
            in_specs=[
                pl.BlockSpec((2, width, heads), lambda r, n, c: (r, 0, 0)),
                pl.BlockSpec((2, width, slots), lambda r, n, c: (r, 0, 0)),
                pl.BlockSpec((reqs, width), lambda r, n, c: (0, 0)),
            ],
            out_specs=[out, out],
            scratch_shapes=[pltpu.VMEM((2, reqs, heads // 2, lat), BF)],
        ),
        out_shape=[jax.ShapeDtypeStruct((rows, lat), BF)] * 2,
        compiler_params=params(60),
        cost_estimate=pl.CostEstimate(flops=4 * reqs * heads * slots * width, bytes_accessed=2 * reqs * slots * width, transcendentals=reqs * heads * slots),
        name="attend",
    )(lengths, c, queries.transpose(0, 2, 1), kv_cache.transpose(0, 2, 1), new_latent)


def heads_kernel(x, values, out):
    rows, wide = out.shape[0], x.shape[0]
    row, col = grid_of((rows, wide))
    width = values.shape[2]
    for hh in range(values.shape[0]):
        latent = exact(onehot(col == row * 4 + hh), x[...])
        out[:, hh * width : (hh + 1) * width] = jnp.dot(latent, values[hh], preferred_element_type=F32).astype(BF)


def head_values(x, values):
    count, lat, width = values.shape
    rows = x.shape[0] // count
    return pl.pallas_call(
        heads_kernel,
        out_shape=jax.ShapeDtypeStruct((rows, count * width), BF),
        compiler_params=pltpu.CompilerParams(vmem_limit_bytes=16 * 1024 * 1024),
        cost_estimate=pl.CostEstimate(flops=2 * rows * count * lat * (width + x.shape[0]), bytes_accessed=2 * count * lat * width, transcendentals=0),
        name="head_values",
    )(x, values)


def first_kernel(parts, residual, first, wide):
    total = residual[...].astype(F32)
    for i in range(parts.shape[0]):
        total = total + parts[i].astype(F32)
    first[...] = total
    for i in range(parts.shape[0]):
        wide[i] = total.astype(BF)


def first_sum(parts, residual):
    return pl.pallas_call(
        first_kernel,
        out_shape=[jax.ShapeDtypeStruct(residual.shape, F32), jax.ShapeDtypeStruct(parts.shape, BF)],
        compiler_params=pltpu.CompilerParams(vmem_limit_bytes=16 * 1024 * 1024),
        cost_estimate=pl.CostEstimate(flops=parts.size, bytes_accessed=4 * parts.size, transcendentals=0),
        name="first_sum",
    )(parts, residual)


def second_kernel(parts, first, gain, second, scaled):
    total = first[...]
    for i in range(parts.shape[0]):
        total = total + parts[i].astype(F32)
    second[...] = total
    width = total.shape[1]
    scaled[:, :width] = (total * gain[...].astype(F32)).astype(BF)
    square = total * total
    lanes = square[:, :128]
    for j in range(1, width // 128):
        lanes = lanes + square[:, j * 128 : (j + 1) * 128]
    scaled[:, width:] = tail_of(lanes)


def second_sum(parts, first, gain):
    rows, width = first.shape
    return pl.pallas_call(
        second_kernel,
        out_shape=[jax.ShapeDtypeStruct(first.shape, F32), jax.ShapeDtypeStruct((rows, width + 128), BF)],
        compiler_params=pltpu.CompilerParams(vmem_limit_bytes=16 * 1024 * 1024),
        cost_estimate=pl.CostEstimate(flops=parts.size, bytes_accessed=2 * parts.size, transcendentals=0),
        name="second_sum",
    )(parts, first, gain.reshape(1, -1))


def route_kernel(picks, hots, combs, *, top):
    count = picks.shape[0]
    experts = 32
    ids, gates = picks[:, :top], picks[:, top : 2 * top]
    core = picks[:1, 2 * top : 2 * top + 1]
    expert = lax.broadcasted_iota(jnp.int32, (count, experts), 1).astype(F32)
    named = jnp.zeros((count, experts), F32)
    gate = jnp.zeros((count, experts), F32)
    for k in range(top):
        hit = ids[:, k : k + 1] == expert
        named = named + jnp.where(hit, 1.0, 0.0)
        gate = gate + jnp.where(hit, gates[:, k : k + 1], 0.0)
    row, col = grid_of((count, count))
    earlier = onehot((col < row) & ((col >> 4) == (row >> 4)))
    place = jnp.dot(earlier, named.astype(BF), preferred_element_type=F32)
    token = lax.broadcasted_iota(jnp.int32, (count, experts), 0)
    place = place + jnp.where(token >= 16, 6.0, 0.0)
    place = jnp.where(named > 0.5, place, 100.0)
    across = lambda rows, chip_of, values: lax.dot_general(
        onehot(grid_of((rows, experts))[1].astype(F32) == chip_of(grid_of((rows, experts))[0]).astype(F32) * 2.0 + core),
        values.astype(BF),
        (((1,), (1,)), ((), ())),
        preferred_element_type=F32,
    )
    rows = hots.shape[1]
    at = across(rows, lambda r: r >> 4, place)
    p = lax.broadcasted_iota(jnp.int32, (rows, 1), 0) & 15
    head = onehot(at == jnp.where(p < 12, p, -1).astype(F32))
    for m in range(3):
        tail = onehot(at == jnp.where(p >= 12, 3 * (p - 12) + m, -1).astype(F32))
        hots[m] = jnp.concatenate([head, tail], axis=1)
    rows = combs.shape[2]
    at = across(rows, lambda r: r >> 3, place)
    p = lax.broadcasted_iota(jnp.int32, (rows, 1), 0) & 7
    high = gate.astype(BF)
    for j, part in enumerate((high, gate - high.astype(F32))):
        value = across(rows, lambda r: r >> 3, part)
        for m in range(3):
            want = p if m == 0 else jnp.where((p & 1) == m - 1, 8 + (p >> 1), -1)
            combs[j, m] = jnp.where(at == want.astype(F32), value, 0.0).astype(BF)


def route(picks, top):
    count = picks.shape[0]
    return pl.pallas_call(
        lambda *refs: route_kernel(*refs, top=top),
        out_shape=[jax.ShapeDtypeStruct((3, 256, 2 * count), BF), jax.ShapeDtypeStruct((2, 3, 128, count), BF)],
        compiler_params=pltpu.CompilerParams(vmem_limit_bytes=16 * 1024 * 1024),
        cost_estimate=pl.CostEstimate(flops=1 << 22, bytes_accessed=1 << 18, transcendentals=0),
        name="route",
    )(picks)


def combine_kernel(returned, combs, second, own, other):
    width = own.shape[1]
    half = width // 2
    sums = []
    for m in range(3):
        x = returned[:, :width] if m == 0 else returned[:, width:]
        sums.append(
            sum(lax.dot_general(combs[j, m], x, (((0,), (0,)), ((), ())), preferred_element_type=F32) for j in range(2))
        )
    rows = own.shape[0]
    for m in range(2):
        lanes = slice(m * half, (m + 1) * half)
        total = sums[0][:, lanes] + sums[1 + m]
        own[:, lanes] = second[:, lanes] + total[:rows]
        other[:, lanes] = total[rows:]


def combine(returned, combs, second):
    return pl.pallas_call(
        combine_kernel,
        out_shape=[jax.ShapeDtypeStruct(second.shape, F32)] * 2,
        compiler_params=pltpu.CompilerParams(vmem_limit_bytes=16 * 1024 * 1024),
        cost_estimate=pl.CostEstimate(flops=12 * 32 * 128 * 1792, bytes_accessed=1 << 20, transcendentals=0),
        name="combine",
    )(returned, combs, second)


def pack_kernel(w0, w1, w2, w3, hot, out, *, width):
    total = None
    refs = (w0, w1, w2, w3)
    for ref in refs:
        part = jnp.sum(ref[:, width:].astype(F32), axis=1, keepdims=True)
        total = part if total is None else total + part
    scale = lax.rsqrt(total / D + EPS)
    normed = lambda ref: (ref[:, :width].astype(F32) * scale).astype(BF)
    step = pl.program_id(0)
    for m in range(3):

        @pl.when(step == m)
        def _():
            both = jnp.concatenate([normed(refs[m]), normed(w3)], axis=0)
            out[...] = exact(hot[0], both)


def pack(wide, hot, width):
    rows, depth = hot.shape[1:]
    whole = lambda ref: pl.BlockSpec(ref.shape, lambda i: (0, 0))
    return pl.pallas_call(
        lambda *refs: pack_kernel(*refs, width=width),
        grid=(3,),
        in_specs=[whole(w) for w in wide] + [pl.BlockSpec((1, rows, depth), lambda i: (i, 0, 0))],
        out_specs=pl.BlockSpec((rows, width), lambda i: (0, i)),
        out_shape=jax.ShapeDtypeStruct((rows, 3 * width), BF),
        compiler_params=params(),
        cost_estimate=pl.CostEstimate(flops=6 * rows * width * depth, bytes_accessed=6 * rows * width, transcendentals=0),
        name="pack",
    )(*wide, hot)


def params(mib=16):
    return pltpu.CompilerParams(dimension_semantics=("arbitrary",), vmem_limit_bytes=mib * 1024 * 1024)


def tail_of(squares):
    total = jnp.sum(squares, axis=1, keepdims=True)
    hi = total.astype(BF).astype(F32)
    lane = lax.broadcasted_iota(jnp.int32, (total.shape[0], 128), 1)
    return jnp.where(lane == 0, hi, jnp.where(lane == 1, total - hi, 0.0)).astype(BF)


def dense_in_kernel(z_ref, own, other, gain, gate, up, o0, o1, o2, o3, acc, squares, tail):
    step = pl.program_id(0)
    width = gate.shape[1]

    @pl.when(step == 0)
    def _():
        acc[...] = jnp.zeros_like(acc)
        squares[...] = jnp.zeros_like(squares)

    scale = gain[...].astype(F32)
    for rel, ref in enumerate((own, other)):
        value = ref[...].astype(F32)
        normed = (value * scale).astype(BF)
        acc[rel, :, :width] += jnp.dot(normed, gate[...], preferred_element_type=F32)
        acc[rel, :, width:] += jnp.dot(normed, up[...], preferred_element_type=F32)
        square = value * value
        for j in range(square.shape[1] // 128):
            squares[rel] += square[:, j * 128 : (j + 1) * 128]

    @pl.when(step == pl.num_programs(0) - 1)
    def _():
        z = z_ref[0]
        for rel in range(2):
            tail[rel] = tail_of(squares[rel])
        for k, out in enumerate((o0, o1, o2, o3)):
            at = pl.multiple_of(lax.rem(z + k, NZ) * 64, 64)
            for rel in range(2):
                rows = pl.ds(rel * 64, 64)
                out[rows, : 2 * width] = acc[rel, pl.ds(at, 64), :].astype(BF)
                out[rows, 2 * width :] = tail[rel, pl.ds(at, 64), :]


def dense_in(z, own, other, gain, gate, up):
    depth, width = gate.shape
    step = depth // 2
    rows = own.shape[0]
    lhs = pl.BlockSpec((rows, step), lambda i, z: (0, i))
    weight = pl.BlockSpec((step, width), lambda i, z: (i, 0))
    lanes = 2 * width + 128
    return pl.pallas_call(
        dense_in_kernel,
        grid_spec=pltpu.PrefetchScalarGridSpec(
            num_scalar_prefetch=1,
            grid=(depth // step,),
            in_specs=[lhs, lhs, pl.BlockSpec((1, step), lambda i, z: (0, i)), weight, weight],
            out_specs=[pl.BlockSpec((rows // 2, lanes), lambda i, z: (0, 0))] * NZ,
            scratch_shapes=[
                pltpu.VMEM((2, rows, 2 * width), F32),
                pltpu.VMEM((2, rows, 128), F32),
                pltpu.VMEM((2, rows, 128), BF),
            ],
        ),
        out_shape=[jax.ShapeDtypeStruct((rows // 2, lanes), BF)] * NZ,
        compiler_params=params(),
        cost_estimate=pl.CostEstimate(flops=8 * rows * depth * width, bytes_accessed=4 * depth * (rows + width), transcendentals=0),
        name="dense_in",
    )(z, own, other, gain.reshape(1, -1), gate, up)


def silu(value):
    return value / (1.0 + jnp.exp(-value))


def expert_in_kernel(z_ref, x0, x1, x2, *refs):
    gates, ups, out, (gate_acc, up_acc) = refs[:4], refs[4:8], refs[8], refs[9:]
    step = pl.program_id(0)

    @pl.when(step == 0)
    def _():
        gate_acc[...] = jnp.zeros_like(gate_acc)
        up_acc[...] = jnp.zeros_like(up_acc)

    rows, wide = out.shape[0], x0.shape[0]
    row, col = grid_of((wide, wide))
    place = row & 15
    third = sum(jnp.where(place >= n, 1, 0) for n in (3, 6, 9))
    source = jnp.where(place < 12, (row & ~15) + 12 + third, -1)
    rest = None
    quarters = []
    for m, ref in enumerate((x0, x1, x2)):
        quarters.append(ref[...])
        pick = onehot((col == source) & (place - 3 * third == m))
        term = jnp.dot(pick, ref[...], preferred_element_type=F32)
        rest = term if rest is None else rest + term
    quarters.append(rest.astype(BF))
    for m in range(NZ):
        gate_acc[...] += jnp.dot(quarters[m], gates[m][...], preferred_element_type=F32)
        up_acc[...] += jnp.dot(quarters[m], ups[m][...], preferred_element_type=F32)

    @pl.when(step == pl.num_programs(0) - 1)
    def _():
        hidden = (silu(gate_acc[...]) * up_acc[...]).astype(BF)
        row, col = grid_of((rows, wide))
        keep = ((col & 15) < 12) & (row == (col >> 4) * 12 + (col & 15))
        out[...] = exact(onehot(keep), hidden)


def expert_in(z, x, gate, up, rows):
    depth, width = gate.shape
    steps = 2
    step = depth // NZ // steps
    xs = [pl.BlockSpec((x.shape[0], step), lambda i, z, m=m: (0, m * steps + i)) for m in range(3)]
    ws = [pl.BlockSpec((step, width), lambda i, z, m=m: (lax.rem(z[0] + m, NZ) * steps + i, 0)) for m in range(NZ)]
    return pl.pallas_call(
        expert_in_kernel,
        grid_spec=pltpu.PrefetchScalarGridSpec(
            num_scalar_prefetch=1,
            grid=(steps,),
            in_specs=xs + ws + ws,
            out_specs=pl.BlockSpec((rows, width), lambda i, z: (0, 0)),
            scratch_shapes=[pltpu.VMEM((x.shape[0], width), F32)] * 2,
        ),
        out_shape=jax.ShapeDtypeStruct((rows, width), BF),
        compiler_params=params(),
        cost_estimate=pl.CostEstimate(flops=4 * rows * depth * width, bytes_accessed=4 * depth * width, transcendentals=0),
        name="expert_in",
    )(z, x, x, x, *[gate] * 4, *[up] * 4)


def expert_out_kernel(z_ref, *refs):
    hidden, weights, out, wide = refs[:4], refs[4:8], refs[8], refs[9]
    step = pl.program_id(0)
    rows = out.shape[0]

    @pl.when(step == 0)
    def _():
        row, col = grid_of((2 * rows, hidden[0].shape[0]))
        at = row & (rows - 1)
        slot = jnp.where(row < rows, at & 7, 8 + ((at & 7) >> 1))
        order = onehot(col == (at >> 3) * 12 + slot)
        for k in range(NZ):
            wide[k] = exact(order, hidden[k][...])

    half = weights[0].shape[1]
    mine = (lax.broadcasted_iota(jnp.int32, (rows, 128), 0) & 1) == step
    for n in range(0, half, 128):
        total = None
        for k in range(NZ):
            term = jnp.dot(wide[k], weights[k][:, n : n + 128], preferred_element_type=F32)
            total = term if total is None else total + term
        total = total.astype(BF)
        out[:, pl.ds(pl.multiple_of(step * half + n, 128), 128)] = total[:rows]
        lanes = slice(2 * half + n, 2 * half + n + 128)
        out[:, lanes] = jnp.where(mine, total[rows:], out[:, lanes])


def expert_out(z, hidden, down, got):
    rows, width = hidden[0].shape
    columns = got[0].shape[1]
    steps = 2
    step = columns // steps
    whole = (rows // 12 * 8, columns + step)
    return pl.pallas_call(
        expert_out_kernel,
        grid_spec=pltpu.PrefetchScalarGridSpec(
            num_scalar_prefetch=1,
            grid=(steps,),
            in_specs=[pl.BlockSpec((rows, width), lambda i, z: (0, 0))] * NZ
            + [pl.BlockSpec((width, step), lambda i, z: (0, z[0] * steps + i))]
            + [pl.BlockSpec((width, step), lambda i, z: (0, i))] * 3,
            out_specs=pl.BlockSpec(whole, lambda i, z: (0, 0)),
            scratch_shapes=[pltpu.VMEM((NZ, 2 * whole[0], width), BF)],
        ),
        out_shape=jax.ShapeDtypeStruct(whole, BF),
        compiler_params=params(),
        cost_estimate=pl.CostEstimate(flops=16 * whole[0] * width * columns, bytes_accessed=8 * width * columns, transcendentals=0),
        name="expert_out",
    )(z, *hidden, down, *got)


def dense_out_kernel(z_ref, h0, h1, h2, h3, weight, *refs, rel):
    *arrived, out, held = refs

    @pl.when(pl.program_id(0) == 0)
    def _():
        z = z_ref[0]
        for k, ref in enumerate((h0, h1, h2, h3)):
            at = pl.multiple_of(lax.rem(z + k, NZ) * 64, 64)
            held[pl.ds(at, 64), :] = ref[...]

    total = jnp.dot(held[...], weight[...], preferred_element_type=F32)
    for ref in arrived:
        total = total + ref[...].astype(F32)
    out[...] = total.astype(BF)


def out_proj_kernel(z_ref, h0, h1, h2, h3, weight, *refs, rel):
    *arrived, out, held = refs

    @pl.when(pl.program_id(0) == 0)
    def _():
        z = z_ref[0]
        rows, cols = held.shape[0], h0.shape[0]
        row = lax.broadcasted_iota(jnp.int32, (rows, cols), 0)
        col = lax.broadcasted_iota(jnp.int32, (rows, cols), 1)
        match = col == (row >> 4) * 8 + rel * 4 + (row & 3)
        total = None
        for k, ref in enumerate((h0, h1, h2, h3)):
            hit = match & (((row >> 2) & 3) == lax.rem(z + k, NZ))
            term = jnp.dot(jnp.where(hit, 1.0, 0.0).astype(BF), ref[...], preferred_element_type=F32)
            total = term if total is None else total + term
        held[...] = total.astype(BF)

    total = jnp.dot(held[...], weight[...], preferred_element_type=F32)
    for ref in arrived:
        total = total + ref[...].astype(F32)
    out[...] = total.astype(BF)


def plane_dot(kernel, z, blocks, weight, rel, *arrived):
    depth, columns = weight.shape
    step = columns // 2
    block_rows, at = (64, rel) if kernel is dense_out_kernel else (128, 0)
    return pl.pallas_call(
        lambda *refs: kernel(*refs, rel=rel),
        grid_spec=pltpu.PrefetchScalarGridSpec(
            num_scalar_prefetch=1,
            grid=(columns // step,),
            in_specs=[pl.BlockSpec((block_rows, depth), lambda i, z: (at, 0))] * NZ
            + [pl.BlockSpec((depth, step), lambda i, z: (0, i))]
            + [pl.BlockSpec((256, step), lambda i, z: (0, i))] * len(arrived),
            out_specs=pl.BlockSpec((256, step), lambda i, z: (0, i)),
            scratch_shapes=[pltpu.VMEM((256, depth), BF)],
        ),
        out_shape=jax.ShapeDtypeStruct((256, columns), BF),
        compiler_params=params(),
        cost_estimate=pl.CostEstimate(flops=512 * depth * columns, bytes_accessed=2 * depth * columns, transcendentals=0),
        name=("dense_out" if kernel is dense_out_kernel else "out_proj") + ("_other" if rel else "_own"),
    )(z, *blocks, weight, *arrived)


def shards(
    queries, kv_cache, new_latent, lengths, residual, gain_first, gain_second, value_proj, out_proj,
    dense_gate, dense_up, dense_down, route_ids, route_gates, expert_gate, expert_up, expert_down,
):
    z = lax.axis_index("z")
    c = lax.axis_index("c")
    latent_dim = value_proj.shape[1]
    quarter = residual.shape[1]

    zs = z.astype(jnp.int32).reshape(1)

    def pick(w, k, axis):
        return lax.dynamic_slice_in_dim(w, lax.rem(z + k, NZ) * quarter, quarter, axis)

    def cut(w, axis, which):
        return {k: pick(w, NZ - k, axis) for k in which}

    def tied(value, *groups):
        flat = [group[k] for group in groups for k in group]
        value, *flat = lax.optimization_barrier((value, *flat))
        at = iter(flat)
        return (value, *[{k: next(at) for k in group} for group in groups])

    def fetch(group):
        return {k: zsend(group[k], NZ - k) for k in group}

    only = lambda group, *which: {k: group[k] for k in which}
    picks = jnp.concatenate([route_ids.astype(F32), route_gates], axis=1)
    picks = jnp.concatenate([picks, swap_core(picks)], axis=0)
    picks = jnp.concatenate([picks, jnp.broadcast_to(c.astype(F32), (picks.shape[0], 1))], axis=1)
    hots, combs = route(picks, route_ids.shape[1])

    keep, send = attend(lengths, c.astype(jnp.int32).reshape(1), queries, kv_cache, new_latent, latent_dim)
    both = jnp.stack([keep.reshape(16, 16, -1), swap_core(send).reshape(16, 16, -1)], axis=1)
    moved = lax.all_to_all(both.reshape(16, 32, -1), YX, 0, 0, tiled=True)
    rows = zgather(head_values(moved.reshape(512, -1), value_proj))
    rows, down_cut = tied(rows, cut(expert_down[0], 1, (1, 2, 3)))
    down_a = fetch(only(down_cut, 1, 3))
    parts = plane_scatter(out_proj_kernel, zs, rows, out_proj)
    parts, down_a, down_cut = tied(parts, down_a, only(down_cut, 2))
    first, spread = first_sum(parts, residual)
    own = lax.all_to_all(spread, YX, 0, 0, tiled=True).reshape(256, -1)
    other = swap_core(own)
    width = dense_gate.shape[1]
    blocks = dense_in(zs, own, other, gain_first, dense_gate, dense_up)
    summed = zscatter(blocks)
    scale = lax.rsqrt((summed[:, 2 * width] + summed[:, 2 * width + 1]) / D + EPS)[:, None]
    gate_act = summed[:, :width] * scale
    hidden = (jax.nn.silu(gate_act) * (summed[:, width : 2 * width] * scale)).astype(BF)
    hidden = zgather(hidden)
    hidden, down_cut = tied(hidden, down_cut)
    down_b = fetch(down_cut)
    parts = plane_scatter(dense_out_kernel, zs, hidden, dense_down)
    parts, down_b = tied(parts, down_b)
    second, scaled = second_sum(parts, first, gain_second)

    scaled = jnp.concatenate([scaled, swap_core(scaled)], axis=0)
    wide = zgather(scaled)
    sendbuf = pack(wide, hots, quarter).reshape(16, 16, -1)
    arrived = lax.all_to_all(sendbuf, YX, 0, 0, tiled=True).reshape(256, -1)
    expert_hidden = expert_in(zs, arrived, expert_gate[0], expert_up[0], 192)
    result = expert_out(zs, zgather(expert_hidden), expert_down[0], [down_a[1], down_b[2], down_a[3]])
    returned = lax.all_to_all(result.reshape(16, 8, -1), YX, 0, 0, tiled=True).reshape(128, -1)
    total, theirs = combine(returned, combs, second)
    return (total + swap_core(theirs)).astype(BF)


def solution(mesh):
    grid = Mesh(mesh.devices.reshape(4, 4, 2, 4), ("y", "x", "c", "z"))
    ep = ("y", "x", "c")
    both = ("y", "x", "c", "z")
    return jax.shard_map(
        shards,
        mesh=grid,
        in_specs=(
            P(both, None, None),
            P(both, None, None),
            P(both, None),
            P(both),
            P(ep, "z"),
            P("z"),
            P("z"),
            P(ep, None, None),
            P(ep, "z"),
            P("z", ep),
            P("z", ep),
            P(ep, "z"),
            P(ep, None),
            P(ep, None),
            P(ep, None, "z"),
            P(ep, None, "z"),
            P(ep, "z", None),
        ),
        out_specs=P(ep, "z"),
        check_vma=False,
    )
```

time: 249 us -> 230 us (0.924)
  blocking collectives: 80.1 us -> 69 us
  matrix products: 6.26 us -> 0 us
  Pallas kernels: 21.8 us -> 27.7 us
  other arithmetic: 7.63 us -> 2.22 us
  waiting for transfers between devices: 79 us -> 73.6 us
  starting transfers between devices: 48.8 us -> 52.1 us
    all_to_all x3, waiting for transfers between devices: 44.2 us -> 10.7 us  [the longest x1 10.7 us: shards(): moved = lax.all_to_all(both.reshape(16, 32, -1), YX, 0, 0, tiled=True)]
    ppermute x21 -> x18, waiting for transfers between devices: 31.6 us -> 55.7 us  [zsend(): return lax.ppermute(values, 'z', [(i, (i + shift) % NZ) for i in range(NZ)])]
    all_to_all x3, blocking collectives: 80.1 us -> 69 us  [the longest x1 36.8 us: shards(): arrived = lax.all_to_all(sendbuf, YX, 0, 0, tiled=True).reshape(256, -1)]
    pallas_call x0 -> x7, Pallas kernels: none -> 10.3 us  [the longest x1 6.26 us: attend(): pl.pallas_call(attend_kernel, grid_spec=pltpu.PrefetchScalarGridSpec(num_...]
    dot_general x8 -> x0, matrix products: 6.26 us -> none  [the longest x1 2.55 us: attend(): jnp.einsum('rhc,rjc->rhj', queries, kv_cache, preferred_element_type=F32)]
    ppermute x4 -> x7, starting transfers between devices: 7.82 us -> 13.3 us  [swap_core(): return lax.ppermute(values, 'c', [(0, 1), (1, 0)])]
    ppermute x4 -> x7, waiting for transfers between devices: 3.18 us -> 7.22 us  [swap_core(): return lax.ppermute(values, 'c', [(0, 1), (1, 0)])]
    ppermute x21 -> x18, starting transfers between devices: 27.6 us -> 24.5 us  [zsend(): return lax.ppermute(values, 'z', [(i, (i + shift) % NZ) for i in range(NZ)])]
  transfers between devices with their start and end apart: 28 -> 28, of which waited for: 20 -> 22; matrix products, arithmetic and copies ran while one was open for 4% -> 2% of each run, Pallas kernels for 2% -> 2%
where the time goes in v3:
time: 230 us; the launch traced here: 229 us
  waiting for transfers between devices  73.6 us (32%)
  blocking collectives  69 us (30%)
  starting transfers between devices  52.1 us (23%)
  Pallas kernels  27.7 us (12%)
  local copies, waits for them, and re-layouts  4.39 us (2%)
    ppermute x18, waiting for transfers between devices, zsend(): return lax.ppermute(values, 'z', [(i, (i + shift) % NZ) for i in range(NZ)])  55.7 us
    all_to_all x1, blocking collectives, shards(): arrived = lax.all_to_all(sendbuf, YX, 0, 0, tiled=True).reshape(256, -1)  36.8 us
    ppermute x18, starting transfers between devices, zsend(): return lax.ppermute(values, 'z', [(i, (i + shift) % NZ) for i in range(NZ)])  24.5 us
    all_to_all x1, blocking collectives, shards(): own = lax.all_to_all(spread, YX, 0, 0, tiled=True).reshape(256, -1)  17.4 us
    all_to_all x1, blocking collectives, shards(): lax.all_to_all(result.reshape(16, 8, -1), YX, 0, 0, tiled=True)  14.7 us
    ppermute x7, starting transfers between devices, swap_core(): return lax.ppermute(values, 'c', [(0, 1), (1, 0)])  13.3 us
    all_to_all x1, waiting for transfers between devices, shards(): moved = lax.all_to_all(both.reshape(16, 32, -1), YX, 0, 0, tiled=True)  10.7 us
    all_to_all x2, starting transfers between devices, plane_scatter(): return lax.all_to_all(mine.reshape(16, 16, -1), YX, 0, 0, tiled=True)  7.4 us
  transfers between devices with their start and end apart: 28, of which 22 were waited for; matrix products, arithmetic and copies ran while one was open for 2% of the time, Pallas kernels for 2%

profile of v3, /device:TPU:1, one launch (start us, length us, event | category | flops | bytes accessed | tf_op | source)
XLA Modules:
  0.0 229.2 jit_solution(18412337743409522857)
XLA Ops:
  0.0 6.3 %attend.1 = (bf16[256,512]{1,0:T(8,128)(2,1)}, bf16[256,512]{1,0:T(8,128)(2,1)}) custom-call(s32[4]{0:T(128)} %len_ref.1, s32[1]{0:T(128)} %bitcast.1.c_ref, bf16[4,576,128]{2,1,0:T(8,128)(2,1)} %bitcast.43, bf16[4,576,512]{2,1,0:T(8,128)(2,1)} %bitcast.42, bf16[4,576]{1,0:T(4,128)(2,1)} %new_ref.1), custom_call_target="tpu_custom_call" | custom-call | flops 603979776 | bytes 2359296 | tf_op jit(solution)/shard_map/attend/pallas_call | solution.py:99
  10.9 6.8 %all-to-all-start = ((bf16[16,32,512]{2,1,0:T(8,128)(2,1)}), bf16[16,32,512]{2,1,0:T(8,128)(2,1)S(1)}, u32[]{:S(2)}, u32[]{:S(2)}) async-start(bf16[16,32,512]{2,1,0:T(8,128)(2,1)} %bitcast.6), calls=%async_computation | async-start | bytes 1048576 | tf_op jit(solution)/shard_map/all_to_all | solution.py:572
  17.8 10.7 %all-to-all-done = bf16[16,32,512]{2,1,0:T(8,128)(2,1)S(1)} async-done(((bf16[16,32,512]{2,1,0:T(8,128)(2,1)}), bf16[16,32,512]{2,1,0:T(8,128)(2,1)S(1)}, u32[]{:S(2)}, u32[]{:S(2)}) %all-to-all-start) | async-done | bytes 524320 | tf_op jit(solution)/shard_map/all_to_all | solution.py:572
  31.2 3.3 %collective-permute-start.2 = (bf16[128,512]{1,0:T(8,128)(2,1)S(1)}, bf16[128,512]{1,0:T(8,128)(2,1)S(1)}, u32[]{:S(2)}, u32[]{:S(2)}) collective-permute-start(bf16[128,512]{1,0:T(8,128)(2,1)S(1)} %head_values.1.refs_1_), channel_id=1, source_target_pairs={{0,2},{1,3},{2,0},{3,1},{4,6},{5,7},{6,4},{7,5},{8,10},{9,11},{10,... | collective-permute-start | bytes 393224 | tf_op jit(solution)/shard_map/ppermute | solution.py:19
  35.2 3.3 %dynamic-slice_bitcast_fusion = (bf16[256,1792]{1,0:T(8,128)(2,1)}, bf16[256,1792]{1,0:T(8,128)(2,1)}, bf16[256,1792]{1,0:T(8,128)(2,1)}) fusion(bf16[1,256,7168]{2,1,0:T(8,128)(2,1)} %param.33, s32[]{:T(128)S(6)} %select_n.11, s32[]{:T(128)S(6)} %select_n.10, s32[]{:T(128)S(6)} %select_n.9), kind=kLoop, calls=%fused_computation | loop fusion | bytes 5505036 | tf_op jit(solution)/shard_map/dynamic_slice | solution.py:550
  48.2 3.8 %all-to-all-start.1 = ((bf16[16,16,1792]{2,1,0:T(8,128)(2,1)}), bf16[16,16,1792]{2,1,0:T(8,128)(2,1)S(1)}, u32[]{:S(2)}, u32[]{:S(2)}) async-start(bf16[16,16,1792]{2,1,0:T(8,128)(2,1)} %bitcast.11), calls=%async_computation.1 | async-start | bytes 1835008 | tf_op jit(solution)/shard_map/all_to_all | solution.py:41
  51.9 13.8 %collective-permute-done.5.refs_5_ = bf16[256,1792]{1,0:T(8,128)(2,1)S(1)} collective-permute-done((bf16[256,1792]{1,0:T(8,128)(2,1)}, bf16[256,1792]{1,0:T(8,128)(2,1)S(1)}, u32[]{:S(2)}, u32[]{:S(2)}) %collective-permute-start.5) | collective-permute-done | bytes 917536 | tf_op jit(solution)/shard_map/ppermute | solution.py:19
  65.8 3.0 %collective-permute-done.6.refs_7_ = bf16[256,1792]{1,0:T(8,128)(2,1)S(1)} collective-permute-done((bf16[256,1792]{1,0:T(8,128)(2,1)}, bf16[256,1792]{1,0:T(8,128)(2,1)S(1)}, u32[]{:S(2)}, u32[]{:S(2)}) %collective-permute-start.6) | collective-permute-done | bytes 917536 | tf_op jit(solution)/shard_map/ppermute | solution.py:19
  68.9 17.4 %all_to_all.30 = bf16[16,16,1792]{2,1,0:T(8,128)(2,1)S(1)} all-to-all(bf16[16,16,1792]{2,1,0:T(8,128)(2,1)S(1)} %get-tuple-element.47), channel_id=1, replica_groups=mesh['y'=4,'x'=4,'c'=2,'z'=4] {'y','x'}, dimensions={0} | all-to-all | bytes 1835008 | tf_op jit(solution)/shard_map/all_to_all | solution.py:579
  90.8 2.9 %dense_in.1 = (bf16[128,896]{1,0:T(8,128)(2,1)S(1)}, bf16[128,896]{1,0:T(8,128)(2,1)S(1)}, bf16[128,896]{1,0:T(8,128)(2,1)S(1)}, bf16[128,896]{1,0:T(8,128)(2,1)S(1)}) custom-call(s32[1]{0:T(128)} %bitcast.refs_0_.z_ref, bf16[256,1792]{1,0:T(8,128)(2,1)S(1)} %bitcast.40, bf16[256,1792]{1,0:T(8,128)(2,1)S(1)} %collective-permute-done.7.other, ...), custom_call_target="tpu_custom_call" | custom-call | flops 1409286144 | bytes 4587520 | tf_op jit(solution)/shard_map/dense_in/pallas_call | solution.py:346
  96.7 5.2 %collective-permute-done.8 = bf16[128,896]{1,0:T(8,128)(2,1)S(1)} collective-permute-done((bf16[128,896]{1,0:T(8,128)(2,1)S(1)}, bf16[128,896]{1,0:T(8,128)(2,1)S(1)}, u32[]{:S(2)}, u32[]{:S(2)}) %collective-permute-start.8) | collective-permute-done | bytes 229408 | tf_op jit(solution)/shard_map/ppermute | solution.py:19
  101.9 4.9 %collective-permute-done.9 = bf16[128,896]{1,0:T(8,128)(2,1)S(1)} collective-permute-done((bf16[128,896]{1,0:T(8,128)(2,1)S(1)}, bf16[128,896]{1,0:T(8,128)(2,1)S(1)}, u32[]{:S(2)}, u32[]{:S(2)}) %collective-permute-start.9) | collective-permute-done | bytes 229408 | tf_op jit(solution)/shard_map/ppermute | solution.py:19
  108.8 3.2 %collective-permute-start.12 = (bf16[128,384]{1,0:T(8,128)(2,1)S(1)}, bf16[128,384]{1,0:T(8,128)(2,1)S(1)}, u32[]{:S(2)}, u32[]{:S(2)}) collective-permute-start(bf16[128,384]{1,0:T(8,128)(2,1)S(1)} %fusion.1.refs_1_), channel_id=1, source_target_pairs={{0,2},{1,3},{2,0},{3,1},{4,6},{5,7},{6,4},{7,5},{8,10},{9,11},{10,... | collective-permute-start | bytes 294920 | tf_op jit(solution)/shard_map/ppermute | solution.py:19
  112.7 3.2 %collective-permute-done.12.refs_3_ = bf16[128,384]{1,0:T(8,128)(2,1)S(1)} collective-permute-done((bf16[128,384]{1,0:T(8,128)(2,1)S(1)}, bf16[128,384]{1,0:T(8,128)(2,1)S(1)}, u32[]{:S(2)}, u32[]{:S(2)}) %collective-permute-start.12) | collective-permute-done | bytes 98336 | tf_op jit(solution)/shard_map/ppermute | solution.py:19
  123.1 3.6 %all-to-all-start.3 = ((bf16[16,16,1792]{2,1,0:T(8,128)(2,1)}), bf16[16,16,1792]{2,1,0:T(8,128)(2,1)S(1)}, u32[]{:S(2)}, u32[]{:S(2)}) async-start(bf16[16,16,1792]{2,1,0:T(8,128)(2,1)} %bitcast.13), calls=%async_computation.3 | async-start | bytes 1835008 | tf_op jit(solution)/shard_map/all_to_all | solution.py:41
  127.0 15.7 %collective-permute-done.15.refs_6_ = bf16[256,1792]{1,0:T(8,128)(2,1)} collective-permute-done((bf16[256,1792]{1,0:T(8,128)(2,1)}, bf16[256,1792]{1,0:T(8,128)(2,1)}, u32[]{:S(2)}, u32[]{:S(2)}) %collective-permute-start.15) | collective-permute-done | bytes 917536 | tf_op jit(solution)/shard_map/ppermute | solution.py:19
  144.9 2.9 %collective-permute-start.18 = (bf16[32,1920]{1,0:T(8,128)(2,1)S(1)}, bf16[32,1920]{1,0:T(8,128)(2,1)S(1)}, u32[]{:S(2)}, u32[]{:S(2)}) collective-permute-start(bf16[32,1920]{1,0:T(8,128)(2,1)S(1)} %constant_dynamic-update-slice_fusion.refs_0_), channel_id=1, source_target_pairs={{0,2},{1,3},{2,0},{3,1},{4,6},{5,7},{6,4},{7,5},{8,10},{9,11},{10,... | collective-permute-start | bytes 368648 | tf_op jit(solution)/shard_map/ppermute | solution.py:19
  150.7 2.8 %collective-permute-done.18.refs_2_ = bf16[32,1920]{1,0:T(8,128)(2,1)S(1)} collective-permute-done((bf16[32,1920]{1,0:T(8,128)(2,1)S(1)}, bf16[32,1920]{1,0:T(8,128)(2,1)S(1)}, u32[]{:S(2)}, u32[]{:S(2)}) %collective-permute-start.18) | collective-permute-done | bytes 122912 | tf_op jit(solution)/shard_map/ppermute | solution.py:19
  155.2 36.8 %all_to_all.31 = bf16[16,16,5376]{2,1,0:T(8,128)(2,1)S(1)} all-to-all(bf16[16,16,5376]{2,1,0:T(8,128)(2,1)S(1)} %bitcast.36), channel_id=1, replica_groups=mesh['y'=4,'x'=4,'c'=2,'z'=4] {'y','x'}, dimensions={0} | all-to-all | bytes 5505024 | tf_op jit(solution)/shard_map/all_to_all | solution.py:597
  192.0 4.0 %expert_in.1.refs_0_ = bf16[192,256]{1,0:T(8,128)(2,1)S(1)} custom-call(s32[1]{0:T(128)} %bitcast.refs_0_.z_ref, bf16[256,5376]{1,0:T(8,128)(2,1)S(1)} %bitcast.32, bf16[256,5376]{1,0:T(8,128)(2,1)S(1)} %bitcast.33, bf16[256,5376]{1,0:T(8,128)(2,1)S(1)} %bitcast.34, bf16[7168,256]{1,0:T(8,128)(2,1)S(1)} %bitcast.24, bf16[7168,256]{1,0:T(8,128)(2,1)S(1)} %bitcast.25, ...), custom_call_target="tpu_custom_call" | custom-call | flops 1409286144 | bytes 7340032 | tf_op jit(solution)/shard_map/expert_in/pallas_call | solution.py:410
  197.2 4.0 %collective-permute-start.22 = (bf16[192,256]{1,0:T(8,128)(2,1)S(1)}, bf16[192,256]{1,0:T(8,128)(2,1)S(1)}, u32[]{:S(2)}, u32[]{:S(2)}) collective-permute-start(bf16[192,256]{1,0:T(8,128)(2,1)S(1)} %expert_in.1.refs_0_), channel_id=1, source_target_pairs={{0,2},{1,3},{2,0},{3,1},{4,6},{5,7},{6,4},{7,5},{8,10},{9,11},{10,... | collective-permute-start | bytes 294920 | tf_op jit(solution)/shard_map/ppermute | solution.py:19
  205.5 3.7 %expert_out.1 = bf16[128,2688]{1,0:T(8,128)(2,1)S(1)} custom-call(s32[1]{0:T(128)} %bitcast.refs_0_.z_ref, bf16[192,256]{1,0:T(8,128)(2,1)S(1)} %expert_in.1.refs_0_, bf16[192,256]{1,0:T(8,128)(2,1)S(1)} %collective-permute-done.21.refs_1_, bf16[192,256]{1,0:T(8,128)(2,1)S(1)} %collective-permute-done.22.refs_2_, ...), custom_call_target="tpu_custom_call" | custom-call | flops 939524096 | bytes 3670016 | tf_op jit(solution)/shard_map/expert_out/pallas_call | solution.py:459
  209.1 14.7 %all_to_all.32 = bf16[16,8,2688]{2,1,0:T(8,128)(2,1)S(1)} all-to-all(bf16[16,8,2688]{2,1,0:T(8,128)(2,1)S(1)} %bitcast.38), channel_id=1, replica_groups=mesh['y'=4,'x'=4,'c'=2,'z'=4] {'y','x'}, dimensions={0} | all-to-all | bytes 1376256 | tf_op jit(solution)/shard_map/all_to_all | solution.py:600
  224.3 3.4 %collective-permute-start.24 = (f32[16,1792]{1,0:T(8,128)S(1)}, f32[16,1792]{1,0:T(8,128)S(1)}, u32[]{:S(2)}, u32[]{:S(2)}) collective-permute-start(f32[16,1792]{1,0:T(8,128)S(1)} %get-tuple-element.68), channel_id=1, source_target_pairs={{0,4},{4,0},{1,5},{5,1},{2,6},{6,2},{3,7},{7,3},{8,12},{12,8},{9,1... | collective-permute-start | bytes 344072 | tf_op jit(solution)/shard_map/ppermute | solution.py:23
  (91 shorter events, 49.6 us)
Async XLA Ops:
  10.9 17.6 %all-to-all-start = ((bf16[16,32,512]{2,1,0:T(8,128)(2,1)}), bf16[16,32,512]{2,1,0:T(8,128)(2,1)S(1)}, u32[]{:S(2)}, u32[]{:S(2)}) async-start(bf16[16,32,512]{2,1,0:T(8,128)(2,1)} %bitcast.6), calls=%async_computation | async-start | bytes 1048576 | tf_op jit(solution)/shard_map/all_to_all | solution.py:572
  29.5 9.0 %collective-permute-start.3 = (bf16[128,512]{1,0:T(8,128)(2,1)S(1)}, bf16[128,512]{1,0:T(8,128)(2,1)S(1)}, u32[]{:S(2)}, u32[]{:S(2)}) collective-permute-start(bf16[128,512]{1,0:T(8,128)(2,1)S(1)} %head_values.1.refs_1_), channel_id=1, source_target_pairs={{0,1},{1,2},{2,3},{3,0},{4,5},{5,6},{6,7},{7,4},{8,9},{9,10},{10,1... | collective-permute-start | bytes 393224 | tf_op jit(solution)/shard_map/ppermute | solution.py:19
  31.2 7.6 %collective-permute-start.2 = (bf16[128,512]{1,0:T(8,128)(2,1)S(1)}, bf16[128,512]{1,0:T(8,128)(2,1)S(1)}, u32[]{:S(2)}, u32[]{:S(2)}) collective-permute-start(bf16[128,512]{1,0:T(8,128)(2,1)S(1)} %head_values.1.refs_1_), channel_id=1, source_target_pairs={{0,2},{1,3},{2,0},{3,1},{4,6},{5,7},{6,4},{7,5},{8,10},{9,11},{10,... | collective-permute-start | bytes 393224 | tf_op jit(solution)/shard_map/ppermute | solution.py:19
  34.5 5.0 %collective-permute-start.1 = (bf16[128,512]{1,0:T(8,128)(2,1)S(1)}, bf16[128,512]{1,0:T(8,128)(2,1)S(1)}, u32[]{:S(2)}, u32[]{:S(2)}) collective-permute-start(bf16[128,512]{1,0:T(8,128)(2,1)S(1)} %head_values.1.refs_1_), channel_id=1, source_target_pairs={{0,3},{1,0},{2,1},{3,2},{4,7},{5,4},{6,5},{7,6},{8,11},{9,8},{10,9... | collective-permute-start | bytes 393224 | tf_op jit(solution)/shard_map/ppermute | solution.py:19
  41.0 4.7 %collective-permute-start.4 = (bf16[256,1792]{1,0:T(8,128)(2,1)S(1)}, bf16[256,1792]{1,0:T(8,128)(2,1)S(1)}, u32[]{:S(2)}, u32[]{:S(2)}) collective-permute-start(bf16[256,1792]{1,0:T(8,128)(2,1)S(1)} %out_proj_other.1), channel_id=1, source_target_pairs={{0,4},{4,0},{1,5},{5,1},{2,6},{6,2},{3,7},{7,3},{8,12},{12,8},{9,1... | collective-permute-start | bytes 2752520 | tf_op jit(solution)/shard_map/ppermute | solution.py:23
  43.5 22.3 %collective-permute-start.5 = (bf16[256,1792]{1,0:T(8,128)(2,1)}, bf16[256,1792]{1,0:T(8,128)(2,1)S(1)}, u32[]{:S(2)}, u32[]{:S(2)}) collective-permute-start(bf16[256,1792]{1,0:T(8,128)(2,1)} %get-tuple-element.43), channel_id=1, source_target_pairs={{0,3},{1,0},{2,1},{3,2},{4,7},{5,4},{6,5},{7,6},{8,11},{9,8},{10,9... | collective-permute-start | bytes 2752520 | tf_op jit(solution)/shard_map/ppermute | solution.py:19
  45.8 23.0 %collective-permute-start.6 = (bf16[256,1792]{1,0:T(8,128)(2,1)}, bf16[256,1792]{1,0:T(8,128)(2,1)S(1)}, u32[]{:S(2)}, u32[]{:S(2)}) collective-permute-start(bf16[256,1792]{1,0:T(8,128)(2,1)} %get-tuple-element.44), channel_id=1, source_target_pairs={{0,1},{1,2},{2,3},{3,0},{4,5},{5,6},{6,7},{7,4},{8,9},{9,10},{10,1... | collective-permute-start | bytes 2752520 | tf_op jit(solution)/shard_map/ppermute | solution.py:19
  48.2 20.6 %all-to-all-start.1 = ((bf16[16,16,1792]{2,1,0:T(8,128)(2,1)}), bf16[16,16,1792]{2,1,0:T(8,128)(2,1)S(1)}, u32[]{:S(2)}, u32[]{:S(2)}) async-start(bf16[16,16,1792]{2,1,0:T(8,128)(2,1)} %bitcast.11), calls=%async_computation.1 | async-start | bytes 1835008 | tf_op jit(solution)/shard_map/all_to_all | solution.py:41
  86.4 4.5 %collective-permute-start.7 = (bf16[256,1792]{1,0:T(8,128)(2,1)S(1)}, bf16[256,1792]{1,0:T(8,128)(2,1)S(1)}, u32[]{:S(2)}, u32[]{:S(2)}) collective-permute-start(bf16[256,1792]{1,0:T(8,128)(2,1)S(1)} %bitcast.39), channel_id=1, source_target_pairs={{0,4},{4,0},{1,5},{5,1},{2,6},{6,2},{3,7},{7,3},{8,12},{12,8},{9,1... | collective-permute-start | bytes 2752520 | tf_op jit(solution)/shard_map/ppermute | solution.py:23
  93.8 8.1 %collective-permute-start.8 = (bf16[128,896]{1,0:T(8,128)(2,1)S(1)}, bf16[128,896]{1,0:T(8,128)(2,1)S(1)}, u32[]{:S(2)}, u32[]{:S(2)}) collective-permute-start(bf16[128,896]{1,0:T(8,128)(2,1)S(1)} %get-tuple-element.49), channel_id=1, source_target_pairs={{0,1},{1,2},{2,3},{3,0},{4,5},{5,6},{6,7},{7,4},{8,9},{9,10},{10,1... | collective-permute-start | bytes 688136 | tf_op jit(solution)/shard_map/ppermute | solution.py:19
  93.9 12.9 %collective-permute-start.9 = (bf16[128,896]{1,0:T(8,128)(2,1)S(1)}, bf16[128,896]{1,0:T(8,128)(2,1)S(1)}, u32[]{:S(2)}, u32[]{:S(2)}) collective-permute-start(bf16[128,896]{1,0:T(8,128)(2,1)S(1)} %get-tuple-element.50), channel_id=1, source_target_pairs={{0,2},{1,3},{2,0},{3,1},{4,6},{5,7},{6,4},{7,5},{8,10},{9,11},{10,... | collective-permute-start | bytes 688136 | tf_op jit(solution)/shard_map/ppermute | solution.py:19
  96.5 10.6 %collective-permute-start.10 = (bf16[128,896]{1,0:T(8,128)(2,1)S(1)}, bf16[128,896]{1,0:T(8,128)(2,1)S(1)}, u32[]{:S(2)}, u32[]{:S(2)}) collective-permute-start(bf16[128,896]{1,0:T(8,128)(2,1)S(1)} %get-tuple-element.51), channel_id=1, source_target_pairs={{0,3},{1,0},{2,1},{3,2},{4,7},{5,4},{6,5},{7,6},{8,11},{9,8},{10,9... | collective-permute-start | bytes 688136 | tf_op jit(solution)/shard_map/ppermute | solution.py:19
  107.6 5.1 %collective-permute-start.13 = (bf16[128,384]{1,0:T(8,128)(2,1)S(1)}, bf16[128,384]{1,0:T(8,128)(2,1)S(1)}, u32[]{:S(2)}, u32[]{:S(2)}) collective-permute-start(bf16[128,384]{1,0:T(8,128)(2,1)S(1)} %fusion.1.refs_1_), channel_id=1, source_target_pairs={{0,1},{1,2},{2,3},{3,0},{4,5},{5,6},{6,7},{7,4},{8,9},{9,10},{10,1... | collective-permute-start | bytes 294920 | tf_op jit(solution)/shard_map/ppermute | solution.py:19
  108.8 7.2 %collective-permute-start.12 = (bf16[128,384]{1,0:T(8,128)(2,1)S(1)}, bf16[128,384]{1,0:T(8,128)(2,1)S(1)}, u32[]{:S(2)}, u32[]{:S(2)}) collective-permute-start(bf16[128,384]{1,0:T(8,128)(2,1)S(1)} %fusion.1.refs_1_), channel_id=1, source_target_pairs={{0,2},{1,3},{2,0},{3,1},{4,6},{5,7},{6,4},{7,5},{8,10},{9,11},{10,... | collective-permute-start | bytes 294920 | tf_op jit(solution)/shard_map/ppermute | solution.py:19
  111.9 4.7 %collective-permute-start.11 = (bf16[128,384]{1,0:T(8,128)(2,1)S(1)}, bf16[128,384]{1,0:T(8,128)(2,1)S(1)}, u32[]{:S(2)}, u32[]{:S(2)}) collective-permute-start(bf16[128,384]{1,0:T(8,128)(2,1)S(1)} %fusion.1.refs_1_), channel_id=1, source_target_pairs={{0,3},{1,0},{2,1},{3,2},{4,7},{5,4},{6,5},{7,6},{8,11},{9,8},{10,9... | collective-permute-start | bytes 294920 | tf_op jit(solution)/shard_map/ppermute | solution.py:19
  119.1 23.5 %collective-permute-start.15 = (bf16[256,1792]{1,0:T(8,128)(2,1)}, bf16[256,1792]{1,0:T(8,128)(2,1)}, u32[]{:S(2)}, u32[]{:S(2)}) collective-permute-start(bf16[256,1792]{1,0:T(8,128)(2,1)} %get-tuple-element.57), channel_id=1, source_target_pairs={{0,2},{1,3},{2,0},{3,1},{4,6},{5,7},{6,4},{7,5},{8,10},{9,11},{10,... | collective-permute-start | bytes 2752520 | tf_op jit(solution)/shard_map/ppermute | solution.py:19
  123.1 19.5 %all-to-all-start.3 = ((bf16[16,16,1792]{2,1,0:T(8,128)(2,1)}), bf16[16,16,1792]{2,1,0:T(8,128)(2,1)S(1)}, u32[]{:S(2)}, u32[]{:S(2)}) async-start(bf16[16,16,1792]{2,1,0:T(8,128)(2,1)} %bitcast.13), calls=%async_computation.3 | async-start | bytes 1835008 | tf_op jit(solution)/shard_map/all_to_all | solution.py:41
  144.9 5.8 %collective-permute-start.19 = (bf16[32,1920]{1,0:T(8,128)(2,1)S(1)}, bf16[32,1920]{1,0:T(8,128)(2,1)S(1)}, u32[]{:S(2)}, u32[]{:S(2)}) collective-permute-start(bf16[32,1920]{1,0:T(8,128)(2,1)S(1)} %constant_dynamic-update-slice_fusion.refs_0_), channel_id=1, source_target_pairs={{0,1},{1,2},{2,3},{3,0},{4,5},{5,6},{6,7},{7,4},{8,9},{9,10},{10,1... | collective-permute-start | bytes 368648 | tf_op jit(solution)/shard_map/ppermute | solution.py:19
  144.9 8.6 %collective-permute-start.18 = (bf16[32,1920]{1,0:T(8,128)(2,1)S(1)}, bf16[32,1920]{1,0:T(8,128)(2,1)S(1)}, u32[]{:S(2)}, u32[]{:S(2)}) collective-permute-start(bf16[32,1920]{1,0:T(8,128)(2,1)S(1)} %constant_dynamic-update-slice_fusion.refs_0_), channel_id=1, source_target_pairs={{0,2},{1,3},{2,0},{3,1},{4,6},{5,7},{6,4},{7,5},{8,10},{9,11},{10,... | collective-permute-start | bytes 368648 | tf_op jit(solution)/shard_map/ppermute | solution.py:19
  147.8 5.8 %collective-permute-start.17 = (bf16[32,1920]{1,0:T(8,128)(2,1)S(1)}, bf16[32,1920]{1,0:T(8,128)(2,1)S(1)}, u32[]{:S(2)}, u32[]{:S(2)}) collective-permute-start(bf16[32,1920]{1,0:T(8,128)(2,1)S(1)} %constant_dynamic-update-slice_fusion.refs_0_), channel_id=1, source_target_pairs={{0,3},{1,0},{2,1},{3,2},{4,7},{5,4},{6,5},{7,6},{8,11},{9,8},{10,9... | collective-permute-start | bytes 368648 | tf_op jit(solution)/shard_map/ppermute | solution.py:19
  196.0 6.0 %collective-permute-start.23 = (bf16[192,256]{1,0:T(8,128)(2,1)S(1)}, bf16[192,256]{1,0:T(8,128)(2,1)S(1)}, u32[]{:S(2)}, u32[]{:S(2)}) collective-permute-start(bf16[192,256]{1,0:T(8,128)(2,1)S(1)} %expert_in.1.refs_0_), channel_id=1, source_target_pairs={{0,1},{1,2},{2,3},{3,0},{4,5},{5,6},{6,7},{7,4},{8,9},{9,10},{10,1... | collective-permute-start | bytes 294920 | tf_op jit(solution)/shard_map/ppermute | solution.py:19
  197.2 7.2 %collective-permute-start.22 = (bf16[192,256]{1,0:T(8,128)(2,1)S(1)}, bf16[192,256]{1,0:T(8,128)(2,1)S(1)}, u32[]{:S(2)}, u32[]{:S(2)}) collective-permute-start(bf16[192,256]{1,0:T(8,128)(2,1)S(1)} %expert_in.1.refs_0_), channel_id=1, source_target_pairs={{0,2},{1,3},{2,0},{3,1},{4,6},{5,7},{6,4},{7,5},{8,10},{9,11},{10,... | collective-permute-start | bytes 294920 | tf_op jit(solution)/shard_map/ppermute | solution.py:19
  201.2 4.3 %collective-permute-start.21 = (bf16[192,256]{1,0:T(8,128)(2,1)S(1)}, bf16[192,256]{1,0:T(8,128)(2,1)S(1)}, u32[]{:S(2)}, u32[]{:S(2)}) collective-permute-start(bf16[192,256]{1,0:T(8,128)(2,1)S(1)} %expert_in.1.refs_0_), channel_id=1, source_target_pairs={{0,3},{1,0},{2,1},{3,2},{4,7},{5,4},{6,5},{7,6},{8,11},{9,8},{10,9... | collective-permute-start | bytes 294920 | tf_op jit(solution)/shard_map/ppermute | solution.py:19
  224.3 4.3 %collective-permute-start.24 = (f32[16,1792]{1,0:T(8,128)S(1)}, f32[16,1792]{1,0:T(8,128)S(1)}, u32[]{:S(2)}, u32[]{:S(2)}) collective-permute-start(f32[16,1792]{1,0:T(8,128)S(1)} %get-tuple-element.68), channel_id=1, source_target_pairs={{0,4},{4,0},{1,5},{5,1},{2,6},{6,2},{3,7},{7,3},{8,12},{12,8},{9,1... | collective-permute-start | bytes 344072 | tf_op jit(solution)/shard_map/ppermute | solution.py:23
  (17 other events, 305.3 us)

commit v4 on v3

v4 whole, which is shorter than its diff:
```python
import jax
import jax.numpy as jnp
from jax import lax
from jax.experimental import pallas as pl
from jax.experimental.pallas import tpu as pltpu
from jax.sharding import Mesh, PartitionSpec as P

D = 7168
ROPE = 64
VD = 128
EPS = 1e-06
YX = ("y", "x")
NZ = 4
BF = jnp.bfloat16
F32 = jnp.float32


def zsend(values, shift):
    return lax.ppermute(values, "z", [(i, (i + shift) % NZ) for i in range(NZ)])


def swap_core(values):
    return lax.ppermute(values, "c", [(0, 1), (1, 0)])


def zgather(values):
    return [values] + [zsend(values, NZ - k) for k in (1, 2, 3)]


def zscatter(blocks):
    got = [zsend(blocks[k], k) for k in (1, 2, 3)]
    total = blocks[0].astype(F32)
    for piece in got:
        total = total + piece.astype(F32)
    return total


def plane_scatter(mine, other):
    mine = (mine + swap_core(other).astype(F32)).astype(BF)
    return lax.all_to_all(mine.reshape(16, 16, -1), YX, 0, 0, tiled=True)


def onehot(hit):
    return jnp.where(hit, 1.0, 0.0).astype(BF)


def grid_of(shape):
    return lax.broadcasted_iota(jnp.int32, shape, 0), lax.broadcasted_iota(jnp.int32, shape, 1)


def exact(a, b):
    return jnp.dot(a, b, preferred_element_type=F32).astype(BF)


def attend_kernel(len_ref, c_ref, q_ref, kv_ref, new_ref, out, latents):
    step = pl.program_id(0)
    lat = latents.shape[2]
    new = new_ref[...].astype(F32)
    score_scale = (VD + ROPE) ** (-0.5)
    down = (((0,), (0,)), ((), ()))
    for i in range(q_ref.shape[0]):
        r = step * q_ref.shape[0] + i
        q = q_ref[i]
        fresh = jnp.sum(jnp.where(lax.broadcasted_iota(jnp.int32, new.shape, 0) == r, new, 0.0), axis=0, keepdims=True)
        scores = lax.dot_general(q, kv_ref[i], down, preferred_element_type=F32) * score_scale
        own = lax.dot_general(q, new_ref[...], (((0,), (1,)), ((), ())), preferred_element_type=F32)
        own = jnp.where(lax.broadcasted_iota(jnp.int32, own.shape, 1) == r, own, 0.0)
        self_score = jnp.sum(own, axis=1, keepdims=True) * score_scale
        live = lax.broadcasted_iota(jnp.int32, (1, scores.shape[1]), 1) < len_ref[r]
        scores = jnp.where(live, scores, -jnp.inf)
        top = jnp.maximum(jnp.max(scores, axis=1, keepdims=True), self_score)
        expo = jnp.exp(scores - top)
        self_expo = jnp.exp(self_score - top)
        total = 1.0 / (jnp.sum(expo, axis=1, keepdims=True) + self_expo)
        weights = (expo * total).astype(BF)
        self_weight = (self_expo * total).astype(BF).astype(F32)
        latent = lax.dot_general(weights, kv_ref[i, :lat, :], (((1,), (1,)), ((), ())), preferred_element_type=F32)
        latents[r] = (latent + self_weight * fresh[:, :lat]).astype(BF)

    @pl.when(step == pl.num_programs(0) - 1)
    def _():
        rows = out.shape[0]
        heads = rows // latents.shape[0]
        held = latents[...].reshape(rows, lat)
        part = rows // 2
        for i in range(2):
            row, col = grid_of((part, rows))
            row = row + i * part
            core = jnp.where((row & 16) == 0, c_ref[0], 1 - c_ref[0])
            order = onehot(col == ((row >> 2) & 3) * heads + (row >> 5) * 8 + core * 4 + (row & 3))
            out[i * part : (i + 1) * part, :] = exact(order, held)


def attend(lengths, c, queries, kv_cache, new_latent, lat):
    reqs, heads, width = queries.shape
    slots = kv_cache.shape[1]
    rows = reqs * heads
    return pl.pallas_call(
        attend_kernel,
        grid_spec=pltpu.PrefetchScalarGridSpec(
            num_scalar_prefetch=2,
            grid=(reqs // 2,),
            in_specs=[
                pl.BlockSpec((2, width, heads), lambda r, n, c: (r, 0, 0)),
                pl.BlockSpec((2, width, slots), lambda r, n, c: (r, 0, 0)),
                pl.BlockSpec((reqs, width), lambda r, n, c: (0, 0)),
            ],
            out_specs=pl.BlockSpec((rows, lat), lambda r, n, c: (0, 0)),
            scratch_shapes=[pltpu.VMEM((reqs, heads, lat), BF)],
        ),
        out_shape=jax.ShapeDtypeStruct((rows, lat), BF),
        compiler_params=params(60),
        cost_estimate=pl.CostEstimate(flops=4 * reqs * heads * slots * width, bytes_accessed=2 * reqs * slots * width, transcendentals=reqs * heads * slots),
        name="attend",
    )(lengths, c, queries.transpose(0, 2, 1), kv_cache.transpose(0, 2, 1), new_latent)


def heads_kernel(x, got, values, out):
    width = values.shape[2]
    for hh in range(values.shape[0]):
        row, col = grid_of((out.shape[0], x.shape[0]))
        pick = onehot(((row & 4) == 0) & (col == (row >> 3) * 32 + (row & 3) * 4 + hh))
        latent = jnp.dot(pick, x[...], preferred_element_type=F32)
        row, col = grid_of((out.shape[0], got.shape[0]))
        pick = onehot(((row & 4) != 0) & (col == (row >> 3) * 16 + (row & 3) * 4 + hh))
        latent = latent + jnp.dot(pick, got[...], preferred_element_type=F32)
        latent = jnp.dot(latent.astype(BF), values[hh], preferred_element_type=F32)
        out[:, hh * width : (hh + 1) * width] = latent.astype(BF)


def head_values(x, got, values):
    count, lat, width = values.shape
    rows = x.shape[0] // count
    return pl.pallas_call(
        heads_kernel,
        out_shape=jax.ShapeDtypeStruct((rows, count * width), BF),
        compiler_params=pltpu.CompilerParams(vmem_limit_bytes=16 * 1024 * 1024),
        cost_estimate=pl.CostEstimate(flops=2 * rows * count * lat * (width + x.shape[0]), bytes_accessed=2 * count * lat * width, transcendentals=0),
        name="head_values",
    )(x, got, values)


def first_kernel(parts, residual, first, wide):
    total = residual[...].astype(F32)
    for i in range(parts.shape[0]):
        total = total + parts[i].astype(F32)
    first[...] = total
    for i in range(parts.shape[0]):
        wide[i] = total.astype(BF)


def first_sum(parts, residual):
    return pl.pallas_call(
        first_kernel,
        out_shape=[jax.ShapeDtypeStruct(residual.shape, F32), jax.ShapeDtypeStruct(parts.shape, BF)],
        compiler_params=pltpu.CompilerParams(vmem_limit_bytes=16 * 1024 * 1024),
        cost_estimate=pl.CostEstimate(flops=parts.size, bytes_accessed=24 * parts.size, transcendentals=0),
        name="first_sum",
    )(parts, residual)


def second_kernel(parts, first, gain, second, scaled):
    total = first[...]
    for i in range(parts.shape[0]):
        total = total + parts[i].astype(F32)
    second[...] = total
    width = total.shape[1]
    scaled[:, :width] = (total * gain[...].astype(F32)).astype(BF)
    square = total * total
    lanes = square[:, :128]
    for j in range(1, width // 128):
        lanes = lanes + square[:, j * 128 : (j + 1) * 128]
    scaled[:, width:] = tail_of(lanes)


def second_sum(parts, first, gain):
    rows, width = first.shape
    return pl.pallas_call(
        second_kernel,
        out_shape=[jax.ShapeDtypeStruct(first.shape, F32), jax.ShapeDtypeStruct((rows, width + 128), BF)],
        compiler_params=pltpu.CompilerParams(vmem_limit_bytes=16 * 1024 * 1024),
        cost_estimate=pl.CostEstimate(flops=parts.size, bytes_accessed=2 * parts.size, transcendentals=0),
        name="second_sum",
    )(parts, first, gain.reshape(1, -1))


def route_kernel(picks, hots, combs, *, top):
    count = picks.shape[0]
    experts = 32
    ids, gates = picks[:, :top], picks[:, top : 2 * top]
    core = picks[:1, 2 * top : 2 * top + 1]
    expert = lax.broadcasted_iota(jnp.int32, (count, experts), 1).astype(F32)
    named = jnp.zeros((count, experts), F32)
    gate = jnp.zeros((count, experts), F32)
    for k in range(top):
        hit = ids[:, k : k + 1] == expert
        named = named + jnp.where(hit, 1.0, 0.0)
        gate = gate + jnp.where(hit, gates[:, k : k + 1], 0.0)
    row, col = grid_of((count, count))
    earlier = onehot((col < row) & ((col >> 4) == (row >> 4)))
    place = jnp.dot(earlier, named.astype(BF), preferred_element_type=F32)
    token = lax.broadcasted_iota(jnp.int32, (count, experts), 0)
    place = place + jnp.where(token >= 16, 6.0, 0.0)
    place = jnp.where(named > 0.5, place, 100.0)
    across = lambda rows, chip_of, values: lax.dot_general(
        onehot(grid_of((rows, experts))[1].astype(F32) == chip_of(grid_of((rows, experts))[0]).astype(F32) * 2.0 + core),
        values.astype(BF),
        (((1,), (1,)), ((), ())),
        preferred_element_type=F32,
    )
    rows = combs.shape[2]
    at = across(rows, lambda r: r >> 3, place)
    p = lax.broadcasted_iota(jnp.int32, (rows, 1), 0) & 7
    hots[0] = onehot(at == p.astype(F32))
    hots[1] = onehot(at == (8 + (p >> 1)).astype(F32))
    high = gate.astype(BF)
    for j, part in enumerate((high, gate - high.astype(F32))):
        value = across(rows, lambda r: r >> 3, part)
        for m in range(3):
            want = p if m == 0 else jnp.where((p & 1) == m - 1, 8 + (p >> 1), -1)
            combs[j, m] = jnp.where(at == want.astype(F32), value, 0.0).astype(BF)


def route(picks, top):
    count = picks.shape[0]
    return pl.pallas_call(
        lambda *refs: route_kernel(*refs, top=top),
        out_shape=[jax.ShapeDtypeStruct((2, 128, count), BF), jax.ShapeDtypeStruct((2, 3, 128, count), BF)],
        compiler_params=pltpu.CompilerParams(vmem_limit_bytes=16 * 1024 * 1024),
        cost_estimate=pl.CostEstimate(flops=1 << 22, bytes_accessed=1 << 18, transcendentals=0),
        name="route",
    )(picks)


def combine_kernel(returned, combs, second, own, other):
    width = own.shape[1]
    half = width // 2
    sums = []
    for m in range(3):
        x = returned[:, :width] if m == 0 else returned[:, width:]
        sums.append(
            sum(lax.dot_general(combs[j, m], x, (((0,), (0,)), ((), ())), preferred_element_type=F32) for j in range(2))
        )
    rows = own.shape[0]
    for m in range(2):
        lanes = slice(m * half, (m + 1) * half)
        total = sums[0][:, lanes] + sums[1 + m]
        own[:, lanes] = second[:, lanes] + total[:rows]
        other[:, lanes] = total[rows:]


def combine(returned, combs, second):
    return pl.pallas_call(
        combine_kernel,
        out_shape=[jax.ShapeDtypeStruct(second.shape, F32)] * 2,
        compiler_params=pltpu.CompilerParams(vmem_limit_bytes=16 * 1024 * 1024),
        cost_estimate=pl.CostEstimate(flops=12 * 32 * 128 * 1792, bytes_accessed=1 << 20, transcendentals=0),
        name="combine",
    )(returned, combs, second)


def pack_kernel(x, hots, out, *, width):
    half = width // 2
    rows = out.shape[0]
    head = exact(hots[0], x[...])
    tail = exact(hots[1], x[...])
    out[:, :width] = head[:, :width]
    even = (lax.broadcasted_iota(jnp.int32, (rows, half), 0) & 1) == 0
    out[:, width : width + half] = jnp.where(even, tail[:, :half], tail[:, half:width])
    lane = lax.broadcasted_iota(jnp.int32, (rows, 128), 1)
    out[:, width + half :] = jnp.where(lane < 2, head[:, width:], tail[:, width:])


def pack(x, hots, width):
    rows = hots.shape[1]
    return pl.pallas_call(
        lambda *refs: pack_kernel(*refs, width=width),
        out_shape=jax.ShapeDtypeStruct((rows, width * 3 // 2 + 128), BF),
        compiler_params=pltpu.CompilerParams(vmem_limit_bytes=16 * 1024 * 1024),
        cost_estimate=pl.CostEstimate(flops=4 * rows * width * 32, bytes_accessed=3 * rows * width, transcendentals=0),
        name="pack",
    )(x, hots)


def params(mib=16):
    return pltpu.CompilerParams(dimension_semantics=("arbitrary",), vmem_limit_bytes=mib * 1024 * 1024)


def tail_of(squares):
    total = jnp.sum(squares, axis=1, keepdims=True)
    hi = total.astype(BF).astype(F32)
    lane = lax.broadcasted_iota(jnp.int32, (total.shape[0], 128), 1)
    return jnp.where(lane < 4, jnp.where((lane & 1) == 0, hi, total - hi), 0.0).astype(BF)


def dense_in_kernel(z_ref, x, gain, gate, up, o0, o1, o2, o3, acc, squares, tail):
    step = pl.program_id(0)
    width = gate.shape[1]

    @pl.when(step == 0)
    def _():
        acc[...] = jnp.zeros_like(acc)
        squares[...] = jnp.zeros_like(squares)

    value = x[...].astype(F32)
    normed = (value * gain[...].astype(F32)).astype(BF)
    acc[:, :width] += jnp.dot(normed, gate[...], preferred_element_type=F32)
    acc[:, width:] += jnp.dot(normed, up[...], preferred_element_type=F32)
    square = value * value
    for j in range(square.shape[1] // 128):
        squares[...] += square[:, j * 128 : (j + 1) * 128]

    @pl.when(step == pl.num_programs(0) - 1)
    def _():
        z = z_ref[0]
        tail[...] = tail_of(squares[...])
        part = acc.shape[0] // NZ
        for k, out in enumerate((o0, o1, o2, o3)):
            at = pl.ds(pl.multiple_of(lax.rem(z + k, NZ) * part, part), part)
            out[:, : 2 * width] = acc[at, :].astype(BF)
            out[:, 2 * width :] = tail[at, :]


def dense_in(z, x, gain, gate, up, name):
    depth, width = gate.shape
    step = depth // 2
    rows = x.shape[0]
    weight = pl.BlockSpec((step, width), lambda i, z: (i, 0))
    lanes = 2 * width + 128
    return pl.pallas_call(
        dense_in_kernel,
        grid_spec=pltpu.PrefetchScalarGridSpec(
            num_scalar_prefetch=1,
            grid=(depth // step,),
            in_specs=[
                pl.BlockSpec((rows, step), lambda i, z: (0, i)),
                pl.BlockSpec((1, step), lambda i, z: (0, i)),
                weight,
                weight,
            ],
            out_specs=[pl.BlockSpec((rows // NZ, lanes), lambda i, z: (0, 0))] * NZ,
            scratch_shapes=[
                pltpu.VMEM((rows, 2 * width), F32),
                pltpu.VMEM((rows, 128), F32),
                pltpu.VMEM((rows, 128), BF),
            ],
        ),
        out_shape=[jax.ShapeDtypeStruct((rows // NZ, lanes), BF)] * NZ,
        compiler_params=params(),
        cost_estimate=pl.CostEstimate(flops=4 * rows * depth * width, bytes_accessed=4 * depth * (rows + width), transcendentals=0),
        name=name,
    )(z, x, gain.reshape(1, -1), gate, up)


def silu(value):
    return value / (1.0 + jnp.exp(-value))


def expert_in_kernel(z_ref, *refs):
    heads, tails, sums, gates, ups = (refs[4 * j : 4 * j + 4] for j in range(5))
    out, gate_acc, up_acc = refs[20:]
    step = pl.program_id(0)

    @pl.when(step == 0)
    def _():
        gate_acc[...] = jnp.zeros_like(gate_acc)
        up_acc[...] = jnp.zeros_like(up_acc)

    rows = heads[0].shape[0]
    row, col = grid_of((rows // 2, rows))
    pick = onehot(col == 2 * row + step)
    for m in range(NZ):
        x = jnp.concatenate([heads[m][...], exact(pick, tails[m][...])], axis=0)
        gate_acc[...] += jnp.dot(x, gates[m][...], preferred_element_type=F32)
        up_acc[...] += jnp.dot(x, ups[m][...], preferred_element_type=F32)

    @pl.when(step == pl.num_programs(0) - 1)
    def _():
        lane = lax.broadcasted_iota(jnp.int32, (1, 128), 1)
        total = None
        for ref in sums:
            square = jnp.concatenate(
                [
                    jnp.where(lane < 2, ref[...].astype(F32), 0.0),
                    jnp.where((lane >= 2) & (lane < 4), jnp.dot(pick, ref[...], preferred_element_type=F32), 0.0),
                ],
                axis=0,
            )
            total = square if total is None else total + square
        scale = lax.rsqrt(jnp.sum(total, axis=1, keepdims=True) / D + EPS)
        out[...] = (silu(gate_acc[...] * scale) * (up_acc[...] * scale)).astype(BF)


def expert_in(z, xs, gate, up):
    depth, width = gate.shape
    steps = 2
    step = depth // NZ // steps
    rows = xs[0].shape[0]
    heads = [pl.BlockSpec((rows, step), lambda i, z: (0, i))] * NZ
    tails = [pl.BlockSpec((rows, step), lambda i, z: (0, 2))] * NZ
    sums = [pl.BlockSpec((rows, 128), lambda i, z: (0, 3 * step // 128))] * NZ
    ws = [pl.BlockSpec((step, width), lambda i, z, m=m: (lax.rem(z[0] + m, NZ) * steps + i, 0)) for m in range(NZ)]
    total = rows * 3 // 2
    return pl.pallas_call(
        expert_in_kernel,
        grid_spec=pltpu.PrefetchScalarGridSpec(
            num_scalar_prefetch=1,
            grid=(steps,),
            in_specs=heads + tails + sums + ws + ws,
            out_specs=pl.BlockSpec((total, width), lambda i, z: (0, 0)),
            scratch_shapes=[pltpu.VMEM((total, width), F32)] * 2,
        ),
        out_shape=jax.ShapeDtypeStruct((total, width), BF),
        compiler_params=params(),
        cost_estimate=pl.CostEstimate(flops=4 * total * depth * width, bytes_accessed=4 * depth * width, transcendentals=0),
        name="expert_in",
    )(z, *xs, *xs, *xs, *[gate] * 4, *[up] * 4)


def expert_out_kernel(z_ref, *refs):
    hidden, weights, out, wide = refs[:4], refs[4:8], refs[8], refs[9]
    step = pl.program_id(0)
    rows = out.shape[0]

    @pl.when(step == 0)
    def _():
        row, col = grid_of((rows, rows // 2))
        order = onehot(col == row >> 1)
        for k in range(NZ):
            wide[k, :rows] = hidden[k][:rows]
            wide[k, rows:] = exact(order, hidden[k][rows:])

    half = weights[0].shape[1]
    for n in range(0, half, 256):
        tile = min(256, half - n)
        total = None
        for k in range(NZ):
            term = jnp.dot(wide[k], weights[k][:, n : n + tile], preferred_element_type=F32)
            total = term if total is None else total + term
        total = total.astype(BF)
        out[:, pl.ds(pl.multiple_of(step * half + n, 128), tile)] = total[:rows]
        lanes = slice(2 * half + n, 2 * half + n + tile)
        mine = (lax.broadcasted_iota(jnp.int32, (rows, tile), 0) & 1) == step
        out[:, lanes] = jnp.where(mine, total[rows:], out[:, lanes])


def expert_out(z, hidden, down, got):
    rows, width = hidden[0].shape
    columns = got[0].shape[1]
    steps = 2
    step = columns // steps
    whole = (rows // 12 * 8, columns + step)
    return pl.pallas_call(
        expert_out_kernel,
        grid_spec=pltpu.PrefetchScalarGridSpec(
            num_scalar_prefetch=1,
            grid=(steps,),
            in_specs=[pl.BlockSpec((rows, width), lambda i, z: (0, 0))] * NZ
            + [pl.BlockSpec((width, step), lambda i, z: (0, z[0] * steps + i))]
            + [pl.BlockSpec((width, step), lambda i, z: (0, i))] * 3,
            out_specs=pl.BlockSpec(whole, lambda i, z: (0, 0)),
            scratch_shapes=[pltpu.VMEM((NZ, 2 * whole[0], width), BF)],
        ),
        out_shape=jax.ShapeDtypeStruct(whole, BF),
        compiler_params=params(),
        cost_estimate=pl.CostEstimate(flops=16 * whole[0] * width * columns, bytes_accessed=8 * width * columns, transcendentals=0),
        name="expert_out",
    )(z, *hidden, down, *got)


def dense_out_kernel(z_ref, h0, h1, h2, h3, weight, *refs, rel):
    out, held = refs

    @pl.when(pl.program_id(0) == 0)
    def _():
        z = z_ref[0]
        for k, ref in enumerate((h0, h1, h2, h3)):
            at = pl.multiple_of(lax.rem(z + k, NZ) * 64, 64)
            held[pl.ds(at, 64), :] = ref[...]

    total = jnp.dot(held[...], weight[...], preferred_element_type=F32)
    out[...] = total.astype(out.dtype)


def out_proj_kernel(z_ref, h0, h1, h2, h3, weight, *refs, rel):
    out, held = refs

    @pl.when(pl.program_id(0) == 0)
    def _():
        z = z_ref[0]
        rows, cols = held.shape[0], h0.shape[0]
        row = lax.broadcasted_iota(jnp.int32, (rows, cols), 0)
        col = lax.broadcasted_iota(jnp.int32, (rows, cols), 1)
        match = col == (row >> 4) * 8 + rel * 4 + (row & 3)
        total = None
        for k, ref in enumerate((h0, h1, h2, h3)):
            hit = match & (((row >> 2) & 3) == lax.rem(z + k, NZ))
            term = jnp.dot(jnp.where(hit, 1.0, 0.0).astype(BF), ref[...], preferred_element_type=F32)
            total = term if total is None else total + term
        held[...] = total.astype(BF)

    total = jnp.dot(held[...], weight[...], preferred_element_type=F32)
    out[...] = total.astype(out.dtype)


def plane_dot(kernel, z, blocks, weight, rel):
    depth, columns = weight.shape
    step = columns
    block_rows = blocks[0].shape[0]
    return pl.pallas_call(
        lambda *refs: kernel(*refs, rel=rel),
        grid_spec=pltpu.PrefetchScalarGridSpec(
            num_scalar_prefetch=1,
            grid=(columns // step,),
            in_specs=[pl.BlockSpec((block_rows, depth), lambda i, z: (0, 0))] * NZ
            + [pl.BlockSpec((depth, step), lambda i, z: (0, i))],
            out_specs=pl.BlockSpec((256, step), lambda i, z: (0, i)),
            scratch_shapes=[pltpu.VMEM((256, depth), BF)],
        ),
        out_shape=jax.ShapeDtypeStruct((256, columns), BF if rel else F32),
        compiler_params=params(),
        cost_estimate=pl.CostEstimate(flops=512 * depth * columns, bytes_accessed=2 * depth * columns, transcendentals=0),
        name=("dense_out" if kernel is dense_out_kernel else "out_proj") + ("_other" if rel else "_own"),
    )(z, *blocks, weight)


def shards(
    queries, kv_cache, new_latent, lengths, residual, gain_first, gain_second, value_proj, out_proj,
    dense_gate, dense_up, dense_down, route_ids, route_gates, expert_gate, expert_up, expert_down,
):
    z = lax.axis_index("z")
    c = lax.axis_index("c")
    latent_dim = value_proj.shape[1]
    quarter = residual.shape[1]

    zs = z.astype(jnp.int32).reshape(1)

    def pick(w, k, axis):
        return lax.dynamic_slice_in_dim(w, lax.rem(z + k, NZ) * quarter, quarter, axis)

    def cut(w, axis, which):
        return {k: pick(w, NZ - k, axis) for k in which}

    def tied(value, *groups):
        flat = [group[k] for group in groups for k in group]
        value, *flat = lax.optimization_barrier((value, *flat))
        at = iter(flat)
        return (value, *[{k: next(at) for k in group} for group in groups])

    def fetch(group):
        return {k: zsend(group[k], NZ - k) for k in group}

    only = lambda group, *which: {k: group[k] for k in which}
    picks = jnp.concatenate([route_ids.astype(F32), route_gates], axis=1)
    picks = jnp.concatenate([picks, swap_core(picks)], axis=0)
    picks = jnp.concatenate([picks, jnp.broadcast_to(c.astype(F32), (picks.shape[0], 1))], axis=1)
    hots, combs = route(picks, route_ids.shape[1])

    latents = attend(lengths, c.astype(jnp.int32).reshape(1), queries, kv_cache, new_latent, latent_dim)
    moved = lax.all_to_all(latents.reshape(16, 32, -1), YX, 0, 0, tiled=True)
    moved, down_cut = tied(moved, cut(expert_down[0], 1, (1, 2, 3)))
    got = swap_core(moved[:, 16:].reshape(256, -1))
    rows = zgather(head_values(moved.reshape(512, -1), got, value_proj))
    rows, down_cut = tied(rows, down_cut)
    down_a = fetch(only(down_cut, 1, 3))
    other = plane_dot(out_proj_kernel, zs, rows, out_proj, 1)
    parts = plane_scatter(plane_dot(out_proj_kernel, zs, rows, out_proj, 0), other)
    parts, down_a, down_cut = tied(parts, down_a, only(down_cut, 2))
    first, spread = first_sum(parts, residual)
    own = lax.all_to_all(spread, YX, 0, 0, tiled=True).reshape(256, -1)
    other = swap_core(own)
    width = dense_gate.shape[1]

    def activate(summed):
        scale = lax.rsqrt((summed[:, 2 * width] + summed[:, 2 * width + 1]) / D + EPS)[:, None]
        gate_act = summed[:, :width] * scale
        return (jax.nn.silu(gate_act) * (summed[:, width : 2 * width] * scale)).astype(BF)

    blocks_own = dense_in(zs, own, gain_first, dense_gate, dense_up, "dense_in_own")
    other, blocks_own = lax.optimization_barrier((other, blocks_own))
    blocks_other = dense_in(zs, other, gain_first, dense_gate, dense_up, "dense_in_other")
    hidden_own = activate(zscatter(blocks_own))
    summed, hidden_own = lax.optimization_barrier((zscatter(blocks_other), hidden_own))
    hidden_other = activate(summed)
    hidden_own, hidden_other = zgather(hidden_own), zgather(hidden_other)
    mine = plane_dot(dense_out_kernel, zs, hidden_own, dense_down, 0)
    mine, hidden_other = lax.optimization_barrier((mine, hidden_other))
    hidden_other, down_cut = tied(hidden_other, down_cut)
    down_b = fetch(down_cut)
    parts = plane_scatter(mine, plane_dot(dense_out_kernel, zs, hidden_other, dense_down, 1))
    parts, down_b = tied(parts, down_b)
    second, scaled = second_sum(parts, first, gain_second)

    scaled = jnp.concatenate([scaled, swap_core(scaled)], axis=0)
    far = zsend(scaled, 2)
    spread = lambda rows: lax.all_to_all(rows.reshape(16, 8, -1), YX, 0, 0, tiled=True).reshape(128, -1)
    near = spread(pack(scaled, hots, quarter))
    near, far = lax.optimization_barrier((near, far))
    ahead, behind = zsend(near, NZ - 1), zsend(near, 1)
    far = spread(pack(far, hots, quarter))
    expert_hidden = expert_in(zs, [near, ahead, far, behind], expert_gate[0], expert_up[0])
    result = expert_out(zs, zgather(expert_hidden), expert_down[0], [down_a[1], down_b[2], down_a[3]])
    returned = lax.all_to_all(result.reshape(16, 8, -1), YX, 0, 0, tiled=True).reshape(128, -1)
    total, theirs = combine(returned, combs, second)
    return (total + swap_core(theirs)).astype(BF)


def solution(mesh):
    grid = Mesh(mesh.devices.reshape(4, 4, 2, 4), ("y", "x", "c", "z"))
    ep = ("y", "x", "c")
    both = ("y", "x", "c", "z")
    return jax.shard_map(
        shards,
        mesh=grid,
        in_specs=(
            P(both, None, None),
            P(both, None, None),
            P(both, None),
            P(both),
            P(ep, "z"),
            P("z"),
            P("z"),
            P(ep, None, None),
            P(ep, "z"),
            P("z", ep),
            P("z", ep),
            P(ep, "z"),
            P(ep, None),
            P(ep, None),
            P(ep, None, "z"),
            P(ep, None, "z"),
            P(ep, "z", None),
        ),
        out_specs=P(ep, "z"),
        check_vma=False,
    )
```

time: 230 us -> 219 us (0.952)
  blocking collectives: 69 us -> 46.1 us
  starting transfers between devices: 52.1 us -> 58.8 us
  waiting for transfers between devices: 73.6 us -> 77.4 us
  local copies, waits for them, and re-layouts: 4.39 us -> 7.75 us
  Pallas kernels: 27.7 us -> 24.5 us
    all_to_all x1, blocking collectives: 36.8 us -> 15.2 us  [shards(): lax.all_to_all(rows.reshape(16, 8, -1), YX, 0, 0, tiled=True)]
    all_to_all x1 -> x2, starting transfers between devices: 6.84 us -> 11.2 us  [the longest x1 7.59 us: shards(): moved = lax.all_to_all(latents.reshape(16, 32, -1), YX, 0, 0, tiled=True)]
    unnamed x28 -> x30, local copies, waits for them, and re-layouts: 0.15 us -> 4.21 us
    pallas_call x4, Pallas kernels: 6.94 us -> 3.33 us  [plane_dot(): pl.pallas_call(lambda *refs: kernel(*refs, rel=rel), grid_spec=pltpu.Pref...]
    all_to_all x1 -> x2, waiting for transfers between devices: 10.7 us -> 14 us  [the longest x1 7.04 us: shards(): moved = lax.all_to_all(latents.reshape(16, 32, -1), YX, 0, 0, tiled=True)]
    ppermute x18 -> x24, waiting for transfers between devices: 55.7 us -> 58.3 us  [zsend(): return lax.ppermute(values, 'z', [(i, (i + shift) % NZ) for i in range(NZ)])]
    convert_element_type x1 -> x4, other arithmetic: 0.15 us -> 2.49 us  [the longest x2 2.26 us: plane_scatter(): mine = (mine + swap_core(other).astype(F32)).astype(BF)]
    ppermute x18 -> x24, starting transfers between devices: 24.5 us -> 24.1 us  [zsend(): return lax.ppermute(values, 'z', [(i, (i + shift) % NZ) for i in range(NZ)])]
  transfers between devices with their start and end apart: 28 -> 35, of which waited for: 22 -> 24; matrix products, arithmetic and copies ran while one was open for 2% -> 3% of each run, Pallas kernels for 2% -> 3%
where the time goes in v4:
time: 219 us
  waiting for transfers between devices  77.4 us (35%)
  starting transfers between devices  58.8 us (27%)
  blocking collectives  46.1 us (21%)
  Pallas kernels  24.5 us (11%)
  local copies, waits for them, and re-layouts  7.75 us (4%)
  other arithmetic  3.75 us (2%)
    ppermute x24, waiting for transfers between devices, zsend(): return lax.ppermute(values, 'z', [(i, (i + shift) % NZ) for i in range(NZ)])  58.3 us
    ppermute x24, starting transfers between devices, zsend(): return lax.ppermute(values, 'z', [(i, (i + shift) % NZ) for i in range(NZ)])  24.1 us
    all_to_all x1, blocking collectives, shards(): own = lax.all_to_all(spread, YX, 0, 0, tiled=True).reshape(256, -1)  17.8 us
    ppermute x7, starting transfers between devices, swap_core(): return lax.ppermute(values, 'c', [(0, 1), (1, 0)])  15.2 us
    all_to_all x1, blocking collectives, shards(): lax.all_to_all(rows.reshape(16, 8, -1), YX, 0, 0, tiled=True)  15.2 us
    all_to_all x1, blocking collectives, shards(): lax.all_to_all(result.reshape(16, 8, -1), YX, 0, 0, tiled=True)  13.1 us
    all_to_all x2, starting transfers between devices, plane_scatter(): return lax.all_to_all(mine.reshape(16, 16, -1), YX, 0, 0, tiled=True)  8.2 us
    all_to_all x1, starting transfers between devices, shards(): moved = lax.all_to_all(latents.reshape(16, 32, -1), YX, 0, 0, tiled=True)  7.59 us
  transfers between devices with their start and end apart: 35, of which 24 were waited for; matrix products, arithmetic and copies ran while one was open for 3% of the time, Pallas kernels for 3%

profile of v4, /device:TPU:1, one launch (start us, length us, event | category | flops | bytes accessed | tf_op | source)
XLA Modules:
  0.0 218.6 jit_solution(8396350210450373888)
XLA Ops:
  0.0 6.1 %attend.1 = bf16[512,512]{1,0:T(8,128)(2,1)} custom-call(s32[4]{0:T(128)} %len_ref.1, s32[1]{0:T(128)} %bitcast.1.c_ref, bf16[4,576,128]{2,1,0:T(8,128)(2,1)} %bitcast.50, bf16[4,576,512]{2,1,0:T(8,128)(2,1)} %bitcast.48, bf16[4,576]{1,0:T(4,128)(2,1)} %new_ref.1), custom_call_target="tpu_custom_call" | custom-call | flops 603979776 | bytes 2359296 | tf_op jit(solution)/shard_map/attend/pallas_call | solution.py:98
  6.1 7.6 %all-to-all-start = ((bf16[16,32,512]{2,1,0:T(8,128)(2,1)}), bf16[16,32,512]{2,1,0:T(8,128)(2,1)S(1)}, u32[]{:S(2)}, u32[]{:S(2)}) async-start(bf16[16,32,512]{2,1,0:T(8,128)(2,1)} %bitcast.49), calls=%async_computation | async-start | bytes 1048576 | tf_op jit(solution)/shard_map/all_to_all | solution.py:560
  13.7 3.4 %dynamic-slice_bitcast_fusion = (bf16[256,1792]{1,0:T(8,128)(2,1)}, bf16[256,1792]{1,0:T(8,128)(2,1)}, bf16[256,1792]{1,0:T(8,128)(2,1)}) fusion(bf16[1,256,7168]{2,1,0:T(8,128)(2,1)} %param.33, s32[]{:T(128)S(6)} %select_n.11, s32[]{:T(128)S(6)} %select_n.10, s32[]{:T(128)S(6)} %select_n.9), kind=kLoop, calls=%fused_computation.2 | loop fusion | bytes 5505036 | tf_op jit(solution)/shard_map/dynamic_slice | solution.py:539
  17.1 7.0 %all-to-all-done = bf16[16,32,512]{2,1,0:T(8,128)(2,1)S(1)} async-done(((bf16[16,32,512]{2,1,0:T(8,128)(2,1)}), bf16[16,32,512]{2,1,0:T(8,128)(2,1)S(1)}, u32[]{:S(2)}, u32[]{:S(2)}) %all-to-all-start) | async-done | bytes 524320 | tf_op jit(solution)/shard_map/all_to_all | solution.py:560
  28.6 3.8 %collective-permute-start.1 = (bf16[128,512]{1,0:T(8,128)(2,1)S(1)}, bf16[128,512]{1,0:T(8,128)(2,1)S(1)}, u32[]{:S(2)}, u32[]{:S(2)}) collective-permute-start(bf16[128,512]{1,0:T(8,128)(2,1)S(1)} %head_values.1.refs_1_), channel_id=1, source_target_pairs={{0,3},{1,0},{2,1},{3,2},{4,7},{5,4},{6,5},{7,6},{8,11},{9,8},{10,9... | collective-permute-start | bytes 393224 | tf_op jit(solution)/shard_map/ppermute | solution.py:19
  33.1 4.9 %collective-permute-done.1.refs_2_ = bf16[128,512]{1,0:T(8,128)(2,1)S(1)} collective-permute-done((bf16[128,512]{1,0:T(8,128)(2,1)S(1)}, bf16[128,512]{1,0:T(8,128)(2,1)S(1)}, u32[]{:S(2)}, u32[]{:S(2)}) %collective-permute-start.1) | collective-permute-done | bytes 131104 | tf_op jit(solution)/shard_map/ppermute | solution.py:19
  38.4 3.2 %collective-permute-done.3.refs_4_ = bf16[128,512]{1,0:T(8,128)(2,1)S(1)} collective-permute-done((bf16[128,512]{1,0:T(8,128)(2,1)S(1)}, bf16[128,512]{1,0:T(8,128)(2,1)S(1)}, u32[]{:S(2)}, u32[]{:S(2)}) %collective-permute-start.3) | collective-permute-done | bytes 131104 | tf_op jit(solution)/shard_map/ppermute | solution.py:19
  47.1 4.4 %all-to-all-start.1 = ((bf16[16,16,1792]{2,1,0:T(8,128)(2,1)}), bf16[16,16,1792]{2,1,0:T(8,128)(2,1)}, u32[]{:S(2)}, u32[]{:S(2)}) async-start(bf16[16,16,1792]{2,1,0:T(8,128)(2,1)} %bitcast.10), calls=%async_computation.1 | async-start | bytes 1835008 | tf_op jit(solution)/shard_map/all_to_all | solution.py:40
  51.6 14.1 %collective-permute-done.5.refs_5_ = bf16[256,1792]{1,0:T(8,128)(2,1)} collective-permute-done((bf16[256,1792]{1,0:T(8,128)(2,1)}, bf16[256,1792]{1,0:T(8,128)(2,1)}, u32[]{:S(2)}, u32[]{:S(2)}) %collective-permute-start.5) | collective-permute-done | bytes 917536 | tf_op jit(solution)/shard_map/ppermute | solution.py:19
  68.5 17.8 %all_to_all.35 = bf16[16,16,1792]{2,1,0:T(8,128)(2,1)S(1)} all-to-all(bf16[16,16,1792]{2,1,0:T(8,128)(2,1)S(1)} %get-tuple-element.69), channel_id=1, replica_groups=mesh['y'=4,'x'=4,'c'=2,'z'=4] {'y','x'}, dimensions={0} | all-to-all | bytes 1835008 | tf_op jit(solution)/shard_map/all_to_all | solution.py:570
  98.4 2.9 %collective-permute-done.11 = bf16[64,896]{1,0:T(8,128)(2,1)S(1)} collective-permute-done((bf16[64,896]{1,0:T(8,128)(2,1)S(1)}, bf16[64,896]{1,0:T(8,128)(2,1)S(1)}, u32[]{:S(2)}, u32[]{:S(2)}) %collective-permute-start.11) | collective-permute-done | bytes 114720 | tf_op jit(solution)/shard_map/ppermute | solution.py:19
  111.7 3.1 %collective-permute-done.18.refs_3_ = bf16[64,384]{1,0:T(8,128)(2,1)S(1)} collective-permute-done((bf16[64,384]{1,0:T(8,128)(2,1)S(1)}, bf16[64,384]{1,0:T(8,128)(2,1)S(1)}, u32[]{:S(2)}, u32[]{:S(2)}) %collective-permute-start.18) | collective-permute-done | bytes 49184 | tf_op jit(solution)/shard_map/ppermute | solution.py:19
  115.5 3.9 %collective-permute-start.20 = (bf16[256,1792]{1,0:T(8,128)(2,1)S(1)}, bf16[256,1792]{1,0:T(8,128)(2,1)S(1)}, u32[]{:S(2)}, u32[]{:S(2)}) collective-permute-start(bf16[256,1792]{1,0:T(8,128)(2,1)S(1)} %dense_out_other.1), channel_id=1, source_target_pairs={{0,4},{4,0},{1,5},{5,1},{2,6},{6,2},{3,7},{7,3},{8,12},{12,8},{9,1... | collective-permute-start | bytes 2752520 | tf_op jit(solution)/shard_map/ppermute | solution.py:23
  122.7 3.8 %all-to-all-start.3 = ((bf16[16,16,1792]{2,1,0:T(8,128)(2,1)}), bf16[16,16,1792]{2,1,0:T(8,128)(2,1)S(1)}, u32[]{:S(2)}, u32[]{:S(2)}) async-start(bf16[16,16,1792]{2,1,0:T(8,128)(2,1)} %bitcast.12), calls=%async_computation.3 | async-start | bytes 1835008 | tf_op jit(solution)/shard_map/all_to_all | solution.py:40
  128.4 14.4 %collective-permute-done.21.refs_6_ = bf16[256,1792]{1,0:T(8,128)(2,1)S(1)} collective-permute-done((bf16[256,1792]{1,0:T(8,128)(2,1)S(1)}, bf16[256,1792]{1,0:T(8,128)(2,1)S(1)}, u32[]{:S(2)}, u32[]{:S(2)}) %collective-permute-start.21) | collective-permute-done | bytes 917536 | tf_op jit(solution)/shard_map/ppermute | solution.py:19
  146.1 3.6 %all-to-all-start.4 = ((bf16[16,8,2816]{2,1,0:T(8,128)(2,1)}), bf16[16,8,2816]{2,1,0:T(8,128)(2,1)S(1)}, u32[]{:S(2)}, u32[]{:S(2)}) async-start(bf16[16,8,2816]{2,1,0:T(8,128)(2,1)} %bitcast.13), calls=%async_computation.4 | async-start | bytes 1441792 | tf_op jit(solution)/shard_map/all_to_all | solution.py:596
  150.9 4.9 %collective-permute-done.24.refs_0_ = bf16[32,1920]{1,0:T(8,128)(2,1)S(1)} collective-permute-done((bf16[32,1920]{1,0:T(8,128)(2,1)S(1)}, bf16[32,1920]{1,0:T(8,128)(2,1)S(1)}, u32[]{:S(2)}, u32[]{:S(2)}) %collective-permute-start.24) | collective-permute-done | bytes 122912 | tf_op jit(solution)/shard_map/ppermute | solution.py:19
  155.9 6.9 %all-to-all-done.4 = bf16[16,8,2816]{2,1,0:T(8,128)(2,1)S(1)} async-done(((bf16[16,8,2816]{2,1,0:T(8,128)(2,1)}), bf16[16,8,2816]{2,1,0:T(8,128)(2,1)S(1)}, u32[]{:S(2)}, u32[]{:S(2)}) %all-to-all-start.4) | async-done | bytes 720928 | tf_op jit(solution)/shard_map/all_to_all | solution.py:596
  164.7 15.2 %all_to_all.36 = bf16[16,8,2816]{2,1,0:T(8,128)(2,1)S(1)} all-to-all(bf16[16,8,2816]{2,1,0:T(8,128)(2,1)S(1)} %bitcast.45), channel_id=1, replica_groups=mesh['y'=4,'x'=4,'c'=2,'z'=4] {'y','x'}, dimensions={0} | all-to-all | bytes 1441792 | tf_op jit(solution)/shard_map/all_to_all | solution.py:596
  184.4 3.6 %expert_in.1.refs_0_ = bf16[192,256]{1,0:T(8,128)(2,1)S(1)} custom-call(s32[1]{0:T(128)} %bitcast.refs_0_.z_ref, bf16[128,2816]{1,0:T(8,128)(2,1)S(1)} %bitcast.35, bf16[128,2816]{1,0:T(8,128)(2,1)S(1)} %collective-permute-done.25.refs_1_.refs_5_.refs_9_, bf16[128,2816]{1,0:T(8,128)(2,1)S(1)} %bitcast.38, ...), custom_call_target="tpu_custom_call" | custom-call | flops 1409286144 | bytes 7340032 | tf_op jit(solution)/shard_map/expert_in/pallas_call | solution.py:404
  191.6 2.8 %collective-permute-done.28.refs_2_ = bf16[192,256]{1,0:T(8,128)(2,1)S(1)} collective-permute-done((bf16[192,256]{1,0:T(8,128)(2,1)S(1)}, bf16[192,256]{1,0:T(8,128)(2,1)S(1)}, u32[]{:S(2)}, u32[]{:S(2)}) %collective-permute-start.28) | collective-permute-done | bytes 98336 | tf_op jit(solution)/shard_map/ppermute | solution.py:19
  195.4 2.9 %expert_out.1 = bf16[128,2688]{1,0:T(8,128)(2,1)S(1)} custom-call(s32[1]{0:T(128)} %bitcast.refs_0_.z_ref, bf16[192,256]{1,0:T(8,128)(2,1)S(1)} %expert_in.1.refs_0_, bf16[192,256]{1,0:T(8,128)(2,1)S(1)} %collective-permute-done.27.refs_1_, bf16[192,256]{1,0:T(8,128)(2,1)S(1)} %collective-permute-done.28.refs_2_, ...), custom_call_target="tpu_custom_call" | custom-call | flops 939524096 | bytes 3670016 | tf_op jit(solution)/shard_map/expert_out/pallas_call | solution.py:453
  198.3 13.1 %all_to_all.37 = bf16[16,8,2688]{2,1,0:T(8,128)(2,1)S(1)} all-to-all(bf16[16,8,2688]{2,1,0:T(8,128)(2,1)S(1)} %bitcast.47), channel_id=1, replica_groups=mesh['y'=4,'x'=4,'c'=2,'z'=4] {'y','x'}, dimensions={0} | all-to-all | bytes 1376256 | tf_op jit(solution)/shard_map/all_to_all | solution.py:603
  211.9 5.2 %collective-permute-start.30 = (f32[16,1792]{1,0:T(8,128)S(1)}, f32[16,1792]{1,0:T(8,128)S(1)}, u32[]{:S(2)}, u32[]{:S(2)}) collective-permute-start(f32[16,1792]{1,0:T(8,128)S(1)} %get-tuple-element.108), channel_id=1, source_target_pairs={{0,4},{4,0},{1,5},{5,1},{2,6},{6,2},{3,7},{7,3},{8,12},{12,8},{9,1... | collective-permute-start | bytes 344072 | tf_op jit(solution)/shard_map/ppermute | solution.py:23
  (113 shorter events, 59.5 us)
Async XLA Ops:
  6.1 18.1 %all-to-all-start = ((bf16[16,32,512]{2,1,0:T(8,128)(2,1)}), bf16[16,32,512]{2,1,0:T(8,128)(2,1)S(1)}, u32[]{:S(2)}, u32[]{:S(2)}) async-start(bf16[16,32,512]{2,1,0:T(8,128)(2,1)} %bitcast.49), calls=%async_computation | async-start | bytes 1048576 | tf_op jit(solution)/shard_map/all_to_all | solution.py:560
  28.6 9.4 %collective-permute-start.1 = (bf16[128,512]{1,0:T(8,128)(2,1)S(1)}, bf16[128,512]{1,0:T(8,128)(2,1)S(1)}, u32[]{:S(2)}, u32[]{:S(2)}) collective-permute-start(bf16[128,512]{1,0:T(8,128)(2,1)S(1)} %head_values.1.refs_1_), channel_id=1, source_target_pairs={{0,3},{1,0},{2,1},{3,2},{4,7},{5,4},{6,5},{7,6},{8,11},{9,8},{10,9... | collective-permute-start | bytes 393224 | tf_op jit(solution)/shard_map/ppermute | solution.py:19
  32.4 6.0 %collective-permute-start.2 = (bf16[128,512]{1,0:T(8,128)(2,1)S(1)}, bf16[128,512]{1,0:T(8,128)(2,1)S(1)}, u32[]{:S(2)}, u32[]{:S(2)}) collective-permute-start(bf16[128,512]{1,0:T(8,128)(2,1)S(1)} %head_values.1.refs_1_), channel_id=1, source_target_pairs={{0,2},{1,3},{2,0},{3,1},{4,6},{5,7},{6,4},{7,5},{8,10},{9,11},{10,... | collective-permute-start | bytes 393224 | tf_op jit(solution)/shard_map/ppermute | solution.py:19
  32.4 9.1 %collective-permute-start.3 = (bf16[128,512]{1,0:T(8,128)(2,1)S(1)}, bf16[128,512]{1,0:T(8,128)(2,1)S(1)}, u32[]{:S(2)}, u32[]{:S(2)}) collective-permute-start(bf16[128,512]{1,0:T(8,128)(2,1)S(1)} %head_values.1.refs_1_), channel_id=1, source_target_pairs={{0,1},{1,2},{2,3},{3,0},{4,5},{5,6},{6,7},{7,4},{8,9},{9,10},{10,1... | collective-permute-start | bytes 393224 | tf_op jit(solution)/shard_map/ppermute | solution.py:19
  43.5 22.2 %collective-permute-start.5 = (bf16[256,1792]{1,0:T(8,128)(2,1)}, bf16[256,1792]{1,0:T(8,128)(2,1)}, u32[]{:S(2)}, u32[]{:S(2)}) collective-permute-start(bf16[256,1792]{1,0:T(8,128)(2,1)} %get-tuple-element.65), channel_id=1, source_target_pairs={{0,3},{1,0},{2,1},{3,2},{4,7},{5,4},{6,5},{7,6},{8,11},{9,8},{10,9... | collective-permute-start | bytes 2752520 | tf_op jit(solution)/shard_map/ppermute | solution.py:19
  44.1 23.1 %collective-permute-start.6 = (bf16[256,1792]{1,0:T(8,128)(2,1)}, bf16[256,1792]{1,0:T(8,128)(2,1)}, u32[]{:S(2)}, u32[]{:S(2)}) collective-permute-start(bf16[256,1792]{1,0:T(8,128)(2,1)} %get-tuple-element.66), channel_id=1, source_target_pairs={{0,1},{1,2},{2,3},{3,0},{4,5},{5,6},{6,7},{7,4},{8,9},{9,10},{10,1... | collective-permute-start | bytes 2752520 | tf_op jit(solution)/shard_map/ppermute | solution.py:19
  47.1 20.1 %all-to-all-start.1 = ((bf16[16,16,1792]{2,1,0:T(8,128)(2,1)}), bf16[16,16,1792]{2,1,0:T(8,128)(2,1)}, u32[]{:S(2)}, u32[]{:S(2)}) async-start(bf16[16,16,1792]{2,1,0:T(8,128)(2,1)} %bitcast.10), calls=%async_computation.1 | async-start | bytes 1835008 | tf_op jit(solution)/shard_map/all_to_all | solution.py:40
  90.4 8.0 %collective-permute-start.13 = (bf16[64,896]{1,0:T(8,128)(2,1)S(1)}, bf16[64,896]{1,0:T(8,128)(2,1)S(1)}, u32[]{:S(2)}, u32[]{:S(2)}) collective-permute-start(bf16[64,896]{1,0:T(8,128)(2,1)S(1)} %get-tuple-element.82), channel_id=1, source_target_pairs={{0,3},{1,0},{2,1},{3,2},{4,7},{5,4},{6,5},{7,6},{8,11},{9,8},{10,9... | collective-permute-start | bytes 344072 | tf_op jit(solution)/shard_map/ppermute | solution.py:19
  92.2 6.2 %collective-permute-start.12 = (bf16[64,896]{1,0:T(8,128)(2,1)S(1)}, bf16[64,896]{1,0:T(8,128)(2,1)S(1)}, u32[]{:S(2)}, u32[]{:S(2)}) collective-permute-start(bf16[64,896]{1,0:T(8,128)(2,1)S(1)} %get-tuple-element.81), channel_id=1, source_target_pairs={{0,2},{1,3},{2,0},{3,1},{4,6},{5,7},{6,4},{7,5},{8,10},{9,11},{10,... | collective-permute-start | bytes 344072 | tf_op jit(solution)/shard_map/ppermute | solution.py:19
  92.5 8.8 %collective-permute-start.11 = (bf16[64,896]{1,0:T(8,128)(2,1)S(1)}, bf16[64,896]{1,0:T(8,128)(2,1)S(1)}, u32[]{:S(2)}, u32[]{:S(2)}) collective-permute-start(bf16[64,896]{1,0:T(8,128)(2,1)S(1)} %get-tuple-element.80), channel_id=1, source_target_pairs={{0,1},{1,2},{2,3},{3,0},{4,5},{5,6},{6,7},{7,4},{8,9},{9,10},{10,1... | collective-permute-start | bytes 344072 | tf_op jit(solution)/shard_map/ppermute | solution.py:19
  94.4 7.2 %collective-permute-start.10 = (bf16[64,896]{1,0:T(8,128)(2,1)S(1)}, bf16[64,896]{1,0:T(8,128)(2,1)S(1)}, u32[]{:S(2)}, u32[]{:S(2)}) collective-permute-start(bf16[64,896]{1,0:T(8,128)(2,1)S(1)} %get-tuple-element.78), channel_id=1, source_target_pairs={{0,3},{1,0},{2,1},{3,2},{4,7},{5,4},{6,5},{7,6},{8,11},{9,8},{10,9... | collective-permute-start | bytes 344072 | tf_op jit(solution)/shard_map/ppermute | solution.py:19
  96.9 5.4 %collective-permute-start.9 = (bf16[64,896]{1,0:T(8,128)(2,1)S(1)}, bf16[64,896]{1,0:T(8,128)(2,1)S(1)}, u32[]{:S(2)}, u32[]{:S(2)}) collective-permute-start(bf16[64,896]{1,0:T(8,128)(2,1)S(1)} %get-tuple-element.77), channel_id=1, source_target_pairs={{0,2},{1,3},{2,0},{3,1},{4,6},{5,7},{6,4},{7,5},{8,10},{9,11},{10,... | collective-permute-start | bytes 344072 | tf_op jit(solution)/shard_map/ppermute | solution.py:19
  98.4 6.0 %collective-permute-start.8 = (bf16[64,896]{1,0:T(8,128)(2,1)S(1)}, bf16[64,896]{1,0:T(8,128)(2,1)S(1)}, u32[]{:S(2)}, u32[]{:S(2)}) collective-permute-start(bf16[64,896]{1,0:T(8,128)(2,1)S(1)} %get-tuple-element.76), channel_id=1, source_target_pairs={{0,1},{1,2},{2,3},{3,0},{4,5},{5,6},{6,7},{7,4},{8,9},{9,10},{10,1... | collective-permute-start | bytes 344072 | tf_op jit(solution)/shard_map/ppermute | solution.py:19
  104.5 5.6 %collective-permute-start.14 = (bf16[64,384]{1,0:T(8,128)(2,1)S(1)}, bf16[64,384]{1,0:T(8,128)(2,1)S(1)}, u32[]{:S(2)}, u32[]{:S(2)}) collective-permute-start(bf16[64,384]{1,0:T(8,128)(2,1)S(1)} %fusion.1.refs_1_), channel_id=1, source_target_pairs={{0,3},{1,0},{2,1},{3,2},{4,7},{5,4},{6,5},{7,6},{8,11},{9,8},{10,9... | collective-permute-start | bytes 147464 | tf_op jit(solution)/shard_map/ppermute | solution.py:19
  104.8 6.0 %collective-permute-start.15 = (bf16[64,384]{1,0:T(8,128)(2,1)S(1)}, bf16[64,384]{1,0:T(8,128)(2,1)S(1)}, u32[]{:S(2)}, u32[]{:S(2)}) collective-permute-start(bf16[64,384]{1,0:T(8,128)(2,1)S(1)} %fusion.1.refs_1_), channel_id=1, source_target_pairs={{0,2},{1,3},{2,0},{3,1},{4,6},{5,7},{6,4},{7,5},{8,10},{9,11},{10,... | collective-permute-start | bytes 147464 | tf_op jit(solution)/shard_map/ppermute | solution.py:19
  115.5 6.0 %collective-permute-start.20 = (bf16[256,1792]{1,0:T(8,128)(2,1)S(1)}, bf16[256,1792]{1,0:T(8,128)(2,1)S(1)}, u32[]{:S(2)}, u32[]{:S(2)}) collective-permute-start(bf16[256,1792]{1,0:T(8,128)(2,1)S(1)} %dense_out_other.1), channel_id=1, source_target_pairs={{0,4},{4,0},{1,5},{5,1},{2,6},{6,2},{3,7},{7,3},{8,12},{12,8},{9,1... | collective-permute-start | bytes 2752520 | tf_op jit(solution)/shard_map/ppermute | solution.py:23
  119.4 23.4 %collective-permute-start.21 = (bf16[256,1792]{1,0:T(8,128)(2,1)S(1)}, bf16[256,1792]{1,0:T(8,128)(2,1)S(1)}, u32[]{:S(2)}, u32[]{:S(2)}) collective-permute-start(bf16[256,1792]{1,0:T(8,128)(2,1)S(1)} %copy-done.9), channel_id=1, source_target_pairs={{0,2},{1,3},{2,0},{3,1},{4,6},{5,7},{6,4},{7,5},{8,10},{9,11},{10,... | collective-permute-start | bytes 2752520 | tf_op jit(solution)/shard_map/ppermute | solution.py:19
  122.7 20.2 %all-to-all-start.3 = ((bf16[16,16,1792]{2,1,0:T(8,128)(2,1)}), bf16[16,16,1792]{2,1,0:T(8,128)(2,1)S(1)}, u32[]{:S(2)}, u32[]{:S(2)}) async-start(bf16[16,16,1792]{2,1,0:T(8,128)(2,1)} %bitcast.12), calls=%async_computation.3 | async-start | bytes 1835008 | tf_op jit(solution)/shard_map/all_to_all | solution.py:40
  146.1 16.7 %all-to-all-start.4 = ((bf16[16,8,2816]{2,1,0:T(8,128)(2,1)}), bf16[16,8,2816]{2,1,0:T(8,128)(2,1)S(1)}, u32[]{:S(2)}, u32[]{:S(2)}) async-start(bf16[16,8,2816]{2,1,0:T(8,128)(2,1)} %bitcast.13), calls=%async_computation.4 | async-start | bytes 1441792 | tf_op jit(solution)/shard_map/all_to_all | solution.py:596
  149.7 6.1 %collective-permute-start.24 = (bf16[32,1920]{1,0:T(8,128)(2,1)S(1)}, bf16[32,1920]{1,0:T(8,128)(2,1)S(1)}, u32[]{:S(2)}, u32[]{:S(2)}) collective-permute-start(bf16[32,1920]{1,0:T(8,128)(2,1)S(1)} %constant_dynamic-update-slice_fusion.refs_0_), channel_id=1, source_target_pairs={{0,2},{1,3},{2,0},{3,1},{4,6},{5,7},{6,4},{7,5},{8,10},{9,11},{10,... | collective-permute-start | bytes 368648 | tf_op jit(solution)/shard_map/ppermute | solution.py:19
  162.8 17.1 %collective-permute-start.25 = (bf16[128,2816]{1,0:T(8,128)(2,1)S(1)}, bf16[128,2816]{1,0:T(8,128)(2,1)S(1)}, u32[]{:S(2)}, u32[]{:S(2)}) collective-permute-start(bf16[128,2816]{1,0:T(8,128)(2,1)S(1)} %bitcast.33), channel_id=1, source_target_pairs={{0,3},{1,0},{2,1},{3,2},{4,7},{5,4},{6,5},{7,6},{8,11},{9,8},{10,9... | collective-permute-start | bytes 2162696 | tf_op jit(solution)/shard_map/ppermute | solution.py:19
  163.3 17.1 %collective-permute-start.26 = (bf16[128,2816]{1,0:T(8,128)(2,1)S(1)}, bf16[128,2816]{1,0:T(8,128)(2,1)S(1)}, u32[]{:S(2)}, u32[]{:S(2)}) collective-permute-start(bf16[128,2816]{1,0:T(8,128)(2,1)S(1)} %bitcast.34), channel_id=1, source_target_pairs={{0,1},{1,2},{2,3},{3,0},{4,5},{5,6},{6,7},{7,4},{8,9},{9,10},{10,1... | collective-permute-start | bytes 2162696 | tf_op jit(solution)/shard_map/ppermute | solution.py:19
  189.7 5.7 %collective-permute-start.29 = (bf16[192,256]{1,0:T(8,128)(2,1)S(1)}, bf16[192,256]{1,0:T(8,128)(2,1)S(1)}, u32[]{:S(2)}, u32[]{:S(2)}) collective-permute-start(bf16[192,256]{1,0:T(8,128)(2,1)S(1)} %expert_in.1.refs_0_), channel_id=1, source_target_pairs={{0,1},{1,2},{2,3},{3,0},{4,5},{5,6},{6,7},{7,4},{8,9},{9,10},{10,1... | collective-permute-start | bytes 294920 | tf_op jit(solution)/shard_map/ppermute | solution.py:19
  211.9 6.1 %collective-permute-start.30 = (f32[16,1792]{1,0:T(8,128)S(1)}, f32[16,1792]{1,0:T(8,128)S(1)}, u32[]{:S(2)}, u32[]{:S(2)}) collective-permute-start(f32[16,1792]{1,0:T(8,128)S(1)} %get-tuple-element.108), channel_id=1, source_target_pairs={{0,4},{4,0},{1,5},{5,1},{2,6},{6,2},{3,7},{7,3},{8,12},{12,8},{9,1... | collective-permute-start | bytes 344072 | tf_op jit(solution)/shard_map/ppermute | solution.py:23
  (25 other events, 259.8 us)

commit v5 on v4

--- a/solution.py
+++ b/solution.py
@@ -35,9 +35,8 @@
     return total
 
 
-def plane_scatter(mine, other):
-    mine = (mine + swap_core(other).astype(F32)).astype(BF)
-    return lax.all_to_all(mine.reshape(16, 16, -1), YX, 0, 0, tiled=True)
+def plane_scatter(rows):
+    return lax.all_to_all(rows.reshape(16, 16, -1), YX, 0, 0, tiled=True)
 
 
 def onehot(hit):
@@ -115,29 +114,28 @@
     )(lengths, c, queries.transpose(0, 2, 1), kv_cache.transpose(0, 2, 1), new_latent)
 
 
-def heads_kernel(x, got, values, out):
-    width = values.shape[2]
-    for hh in range(values.shape[0]):
-        row, col = grid_of((out.shape[0], x.shape[0]))
-        pick = onehot(((row & 4) == 0) & (col == (row >> 3) * 32 + (row & 3) * 4 + hh))
-        latent = jnp.dot(pick, x[...], preferred_element_type=F32)
-        row, col = grid_of((out.shape[0], got.shape[0]))
-        pick = onehot(((row & 4) != 0) & (col == (row >> 3) * 16 + (row & 3) * 4 + hh))
-        latent = latent + jnp.dot(pick, got[...], preferred_element_type=F32)
-        latent = jnp.dot(latent.astype(BF), values[hh], preferred_element_type=F32)
-        out[:, hh * width : (hh + 1) * width] = latent.astype(BF)
-
-
-def head_values(x, got, values):
-    count, lat, width = values.shape
-    rows = x.shape[0] // count
+def heads_kernel(x, own, got, out):
+    rows = x.shape[0]
+    row, col = grid_of((rows, rows))
+    head, chip, r = row >> 6, (row >> 2) & 15, row & 3
+    latent = exact(onehot(col == chip * 32 + (head >> 2) * 16 + r * 4 + (head & 3)), x[...])
+    part, width = out.shape[0], own.shape[2]
+    for head in range(2 * own.shape[0]):
+        values = (own, got)[head // own.shape[0]]
+        value = jnp.dot(latent[head * part : (head + 1) * part], values[head % own.shape[0]], preferred_element_type=F32)
+        out[:, head * width : (head + 1) * width] = value.astype(BF)
+
+
+def head_values(x, own, got):
+    count, lat, width = own.shape
+    rows = x.shape[0] // count // 2
     return pl.pallas_call(
         heads_kernel,
-        out_shape=jax.ShapeDtypeStruct((rows, count * width), BF),
+        out_shape=jax.ShapeDtypeStruct((rows, 2 * count * width), BF),
         compiler_params=pltpu.CompilerParams(vmem_limit_bytes=16 * 1024 * 1024),
-        cost_estimate=pl.CostEstimate(flops=2 * rows * count * lat * (width + x.shape[0]), bytes_accessed=2 * count * lat * width, transcendentals=0),
+        cost_estimate=pl.CostEstimate(flops=2 * x.shape[0] * lat * (width + x.shape[0]), bytes_accessed=4 * count * lat * width, transcendentals=0),
         name="head_values",
-    )(x, got, values)
+    )(x, own, got)
 
 
 def first_kernel(parts, residual, first, wide):
@@ -154,7 +152,7 @@
         first_kernel,
         out_shape=[jax.ShapeDtypeStruct(residual.shape, F32), jax.ShapeDtypeStruct(parts.shape, BF)],
         compiler_params=pltpu.CompilerParams(vmem_limit_bytes=16 * 1024 * 1024),
-        cost_estimate=pl.CostEstimate(flops=parts.size, bytes_accessed=24 * parts.size, transcendentals=0),
+        cost_estimate=pl.CostEstimate(flops=parts.size, bytes_accessed=200 * parts.size, transcendentals=0),
         name="first_sum",
     )(parts, residual)
 
@@ -181,7 +179,7 @@
         compiler_params=pltpu.CompilerParams(vmem_limit_bytes=16 * 1024 * 1024),
         cost_estimate=pl.CostEstimate(flops=parts.size, bytes_accessed=2 * parts.size, transcendentals=0),
         name="second_sum",
-    )(parts, first, gain.reshape(1, -1))
+    )(parts, first, gain)
 
 
 def route_kernel(picks, hots, combs, *, top):
@@ -293,7 +291,7 @@
     return jnp.where(lane < 4, jnp.where((lane & 1) == 0, hi, total - hi), 0.0).astype(BF)
 
 
-def dense_in_kernel(z_ref, x, gain, gate, up, o0, o1, o2, o3, acc, squares, tail):
+def dense_in_kernel(z_ref, x, gain, gate, gate_got, up, up_got, o0, o1, o2, o3, acc, squares, tail):
     step = pl.program_id(0)
     width = gate.shape[1]
 
@@ -304,8 +302,8 @@
 
     value = x[...].astype(F32)
     normed = (value * gain[...].astype(F32)).astype(BF)
-    acc[:, :width] += jnp.dot(normed, gate[...], preferred_element_type=F32)
-    acc[:, width:] += jnp.dot(normed, up[...], preferred_element_type=F32)
+    for j, weight in enumerate((gate, gate_got, up, up_got)):
+        acc[:, j * width : (j + 1) * width] += jnp.dot(normed, weight[...], preferred_element_type=F32)
     square = value * value
     for j in range(square.shape[1] // 128):
         squares[...] += square[:, j * 128 : (j + 1) * 128]
@@ -317,16 +315,15 @@
         part = acc.shape[0] // NZ
         for k, out in enumerate((o0, o1, o2, o3)):
             at = pl.ds(pl.multiple_of(lax.rem(z + k, NZ) * part, part), part)
-            out[:, : 2 * width] = acc[at, :].astype(BF)
-            out[:, 2 * width :] = tail[at, :]
-
-
-def dense_in(z, x, gain, gate, up, name):
-    depth, width = gate.shape
+            out[:, : 4 * width] = acc[at, :].astype(BF)
+            out[:, 4 * width :] = tail[at, :]
+
+
+def dense_in(z, x, gain, weights):
+    depth, width = weights[0].shape
     step = depth // 2
     rows = x.shape[0]
-    weight = pl.BlockSpec((step, width), lambda i, z: (i, 0))
-    lanes = 2 * width + 128
+    lanes = 4 * width + 128
     return pl.pallas_call(
         dense_in_kernel,
         grid_spec=pltpu.PrefetchScalarGridSpec(
@@ -335,21 +332,20 @@
             in_specs=[
                 pl.BlockSpec((rows, step), lambda i, z: (0, i)),
                 pl.BlockSpec((1, step), lambda i, z: (0, i)),
-                weight,
-                weight,
-            ],
+            ]
+            + [pl.BlockSpec((step, width), lambda i, z: (i, 0))] * 4,
             out_specs=[pl.BlockSpec((rows // NZ, lanes), lambda i, z: (0, 0))] * NZ,
             scratch_shapes=[
-                pltpu.VMEM((rows, 2 * width), F32),
+                pltpu.VMEM((rows, 4 * width), F32),
                 pltpu.VMEM((rows, 128), F32),
                 pltpu.VMEM((rows, 128), BF),
             ],
         ),
         out_shape=[jax.ShapeDtypeStruct((rows // NZ, lanes), BF)] * NZ,
         compiler_params=params(),
-        cost_estimate=pl.CostEstimate(flops=4 * rows * depth * width, bytes_accessed=4 * depth * (rows + width), transcendentals=0),
-        name=name,
-    )(z, x, gain.reshape(1, -1), gate, up)
+        cost_estimate=pl.CostEstimate(flops=8 * rows * depth * width, bytes_accessed=2 * depth * (rows + 4 * width), transcendentals=0),
+        name="dense_in",
+    )(z, x, gain, *weights)
 
 
 def silu(value):
@@ -468,9 +464,14 @@
     )(z, *hidden, down, *got)
 
 
-def dense_out_kernel(z_ref, h0, h1, h2, h3, weight, *refs, rel):
-    out, held = refs
-
+def two_dots(rows, own, got, out):
+    depth = own.shape[0]
+    total = jnp.dot(rows[:, :depth], own[...], preferred_element_type=F32)
+    total = total + jnp.dot(rows[:, depth:], got[...], preferred_element_type=F32)
+    out[...] = total.astype(BF)
+
+
+def dense_out_kernel(z_ref, h0, h1, h2, h3, own, got, out, held):
     @pl.when(pl.program_id(0) == 0)
     def _():
         z = z_ref[0]
@@ -478,50 +479,43 @@
             at = pl.multiple_of(lax.rem(z + k, NZ) * 64, 64)
             held[pl.ds(at, 64), :] = ref[...]
 
-    total = jnp.dot(held[...], weight[...], preferred_element_type=F32)
-    out[...] = total.astype(out.dtype)
-
-
-def out_proj_kernel(z_ref, h0, h1, h2, h3, weight, *refs, rel):
-    out, held = refs
-
+    two_dots(held, own, got, out)
+
+
+def out_proj_kernel(z_ref, h0, h1, h2, h3, own, got, out, held):
     @pl.when(pl.program_id(0) == 0)
     def _():
         z = z_ref[0]
-        rows, cols = held.shape[0], h0.shape[0]
-        row = lax.broadcasted_iota(jnp.int32, (rows, cols), 0)
-        col = lax.broadcasted_iota(jnp.int32, (rows, cols), 1)
-        match = col == (row >> 4) * 8 + rel * 4 + (row & 3)
+        row, col = grid_of((held.shape[0], h0.shape[0]))
+        match = col == (row >> 4) * 4 + (row & 3)
         total = None
         for k, ref in enumerate((h0, h1, h2, h3)):
             hit = match & (((row >> 2) & 3) == lax.rem(z + k, NZ))
-            term = jnp.dot(jnp.where(hit, 1.0, 0.0).astype(BF), ref[...], preferred_element_type=F32)
+            term = jnp.dot(onehot(hit), ref[...], preferred_element_type=F32)
             total = term if total is None else total + term
         held[...] = total.astype(BF)
 
-    total = jnp.dot(held[...], weight[...], preferred_element_type=F32)
-    out[...] = total.astype(out.dtype)
-
-
-def plane_dot(kernel, z, blocks, weight, rel):
-    depth, columns = weight.shape
-    step = columns
-    block_rows = blocks[0].shape[0]
-    return pl.pallas_call(
-        lambda *refs: kernel(*refs, rel=rel),
+    two_dots(held, own, got, out)
+
+
+def plane_dot(kernel, z, blocks, own, got, name):
+    depth, columns = own.shape
+    step = columns // 2
+    weight = pl.BlockSpec((depth, step), lambda i, z: (0, i))
+    return pl.pallas_call(
+        kernel,
         grid_spec=pltpu.PrefetchScalarGridSpec(
             num_scalar_prefetch=1,
             grid=(columns // step,),
-            in_specs=[pl.BlockSpec((block_rows, depth), lambda i, z: (0, 0))] * NZ
-            + [pl.BlockSpec((depth, step), lambda i, z: (0, i))],
+            in_specs=[pl.BlockSpec(blocks[0].shape, lambda i, z: (0, 0))] * NZ + [weight, weight],
             out_specs=pl.BlockSpec((256, step), lambda i, z: (0, i)),
-            scratch_shapes=[pltpu.VMEM((256, depth), BF)],
+            scratch_shapes=[pltpu.VMEM((256, 2 * depth), BF)],
         ),
-        out_shape=jax.ShapeDtypeStruct((256, columns), BF if rel else F32),
+        out_shape=jax.ShapeDtypeStruct((256, columns), BF),
         compiler_params=params(),
-        cost_estimate=pl.CostEstimate(flops=512 * depth * columns, bytes_accessed=2 * depth * columns, transcendentals=0),
-        name=("dense_out" if kernel is dense_out_kernel else "out_proj") + ("_other" if rel else "_own"),
-    )(z, *blocks, weight)
+        cost_estimate=pl.CostEstimate(flops=1024 * depth * columns, bytes_accessed=4 * depth * columns, transcendentals=0),
+        name=name,
+    )(z, *blocks, own, got)
 
 
 def shards(
@@ -555,41 +549,39 @@
     picks = jnp.concatenate([picks, swap_core(picks)], axis=0)
     picks = jnp.concatenate([picks, jnp.broadcast_to(c.astype(F32), (picks.shape[0], 1))], axis=1)
     hots, combs = route(picks, route_ids.shape[1])
+    gain_a, gain_b = gain_first.reshape(1, -1), gain_second.reshape(1, -1)
 
     latents = attend(lengths, c.astype(jnp.int32).reshape(1), queries, kv_cache, new_latent, latent_dim)
     moved = lax.all_to_all(latents.reshape(16, 32, -1), YX, 0, 0, tiled=True)
+    moved, value_got = lax.optimization_barrier((moved, swap_core(value_proj)))
+    moved, gain_a, gain_b, hots, combs = lax.optimization_barrier((moved, gain_a, gain_b, hots, combs))
     moved, down_cut = tied(moved, cut(expert_down[0], 1, (1, 2, 3)))
-    got = swap_core(moved[:, 16:].reshape(256, -1))
-    rows = zgather(head_values(moved.reshape(512, -1), got, value_proj))
+    moved, mine = lax.optimization_barrier((moved, out_proj))
+    out_got = swap_core(mine)
+    rows = zgather(head_values(moved.reshape(512, -1), value_proj, value_got))
+    rows, out_got, *mine = lax.optimization_barrier((rows, out_got, dense_gate, dense_up, dense_down))
+    dense_got = [swap_core(weight) for weight in mine]
     rows, down_cut = tied(rows, down_cut)
     down_a = fetch(only(down_cut, 1, 3))
-    other = plane_dot(out_proj_kernel, zs, rows, out_proj, 1)
-    parts = plane_scatter(plane_dot(out_proj_kernel, zs, rows, out_proj, 0), other)
+    parts = plane_scatter(plane_dot(out_proj_kernel, zs, rows, out_proj, out_got, "out_proj"))
     parts, down_a, down_cut = tied(parts, down_a, only(down_cut, 2))
+    parts, *dense_got = lax.optimization_barrier((parts, *dense_got))
     first, spread = first_sum(parts, residual)
     own = lax.all_to_all(spread, YX, 0, 0, tiled=True).reshape(256, -1)
-    other = swap_core(own)
-    width = dense_gate.shape[1]
+    width = 2 * dense_gate.shape[1]
 
     def activate(summed):
         scale = lax.rsqrt((summed[:, 2 * width] + summed[:, 2 * width + 1]) / D + EPS)[:, None]
         gate_act = summed[:, :width] * scale
         return (jax.nn.silu(gate_act) * (summed[:, width : 2 * width] * scale)).astype(BF)
 
-    blocks_own = dense_in(zs, own, gain_first, dense_gate, dense_up, "dense_in_own")
-    other, blocks_own = lax.optimization_barrier((other, blocks_own))
-    blocks_other = dense_in(zs, other, gain_first, dense_gate, dense_up, "dense_in_other")
-    hidden_own = activate(zscatter(blocks_own))
-    summed, hidden_own = lax.optimization_barrier((zscatter(blocks_other), hidden_own))
-    hidden_other = activate(summed)
-    hidden_own, hidden_other = zgather(hidden_own), zgather(hidden_other)
-    mine = plane_dot(dense_out_kernel, zs, hidden_own, dense_down, 0)
-    mine, hidden_other = lax.optimization_barrier((mine, hidden_other))
-    hidden_other, down_cut = tied(hidden_other, down_cut)
+    blocks = dense_in(zs, own, gain_a, [dense_gate, dense_got[0], dense_up, dense_got[1]])
+    hidden = zgather(activate(zscatter(blocks)))
+    hidden, down_cut = tied(hidden, down_cut)
     down_b = fetch(down_cut)
-    parts = plane_scatter(mine, plane_dot(dense_out_kernel, zs, hidden_other, dense_down, 1))
+    parts = plane_scatter(plane_dot(dense_out_kernel, zs, hidden, dense_down, dense_got[2], "dense_out"))
     parts, down_b = tied(parts, down_b)
-    second, scaled = second_sum(parts, first, gain_second)
+    second, scaled = second_sum(parts, first, gain_b)
 
     scaled = jnp.concatenate([scaled, swap_core(scaled)], axis=0)
     far = zsend(scaled, 2)

time: 219 us -> 207 us (0.945)
  blocking collectives: 46.1 us -> 81.1 us
  waiting for transfers between devices: 77.4 us -> 46.1 us
  starting transfers between devices: 58.8 us -> 45.1 us
  other arithmetic: 3.75 us -> 1.22 us
  local copies, waits for them, and re-layouts: 7.75 us -> 10.1 us
    all_to_all x0 -> x2, blocking collectives: none -> 34.2 us  [plane_scatter(): return lax.all_to_all(rows.reshape(16, 16, -1), YX, 0, 0, tiled=True)]
    ppermute x24 -> x18, waiting for transfers between devices: 58.3 us -> 32.8 us  [zsend(): return lax.ppermute(values, 'z', [(i, (i + shift) % NZ) for i in range(NZ)])]
    all_to_all x2 -> x0, starting transfers between devices: 8.2 us -> none  [plane_scatter(): return lax.all_to_all(mine.reshape(16, 16, -1), YX, 0, 0, tiled=True)]
    ppermute x7 -> x8, starting transfers between devices: 15.2 us -> 11.6 us  [swap_core(): return lax.ppermute(values, 'c', [(0, 1), (1, 0)])]
    ppermute x7 -> x8, waiting for transfers between devices: 5.17 us -> 1.87 us  [swap_core(): return lax.ppermute(values, 'c', [(0, 1), (1, 0)])]
    all_to_all x1, waiting for transfers between devices: 7.04 us -> 4.47 us  [shards(): moved = lax.all_to_all(latents.reshape(16, 32, -1), YX, 0, 0, tiled=True)]
    unnamed x30 -> x42, local copies, waits for them, and re-layouts: 4.21 us -> 6.56 us
    convert_element_type x2 -> x0, other arithmetic: 2.26 us -> none  [plane_scatter(): mine = (mine + swap_core(other).astype(F32)).astype(BF)]
  transfers between devices with their start and end apart: 35 -> 28, of which waited for: 24 -> 16; matrix products, arithmetic and copies ran while one was open for 3% -> 2% of each run, Pallas kernels for 3% -> 3%
where the time goes in v5:
time: 207 us; the launch traced here: 206 us
  blocking collectives  81.1 us (39%)
  waiting for transfers between devices  46.1 us (22%)
  starting transfers between devices  45.1 us (22%)
  Pallas kernels  22.4 us (11%)
  local copies, waits for them, and re-layouts  10.1 us (5%)
    all_to_all x2, blocking collectives, plane_scatter(): return lax.all_to_all(rows.reshape(16, 16, -1), YX, 0, 0, tiled=True)  34.2 us
    ppermute x18, waiting for transfers between devices, zsend(): return lax.ppermute(values, 'z', [(i, (i + shift) % NZ) for i in range(NZ)])  32.8 us
    ppermute x18, starting transfers between devices, zsend(): return lax.ppermute(values, 'z', [(i, (i + shift) % NZ) for i in range(NZ)])  21.9 us
    all_to_all x1, blocking collectives, shards(): own = lax.all_to_all(spread, YX, 0, 0, tiled=True).reshape(256, -1)  17.1 us
    all_to_all x1, blocking collectives, shards(): lax.all_to_all(rows.reshape(16, 8, -1), YX, 0, 0, tiled=True)  15.3 us
    all_to_all x1, blocking collectives, shards(): lax.all_to_all(result.reshape(16, 8, -1), YX, 0, 0, tiled=True)  14.5 us
    ppermute x8, starting transfers between devices, swap_core(): return lax.ppermute(values, 'c', [(0, 1), (1, 0)])  11.6 us
    all_to_all x1, starting transfers between devices, shards(): moved = lax.all_to_all(latents.reshape(16, 32, -1), YX, 0, 0, tiled=True)  7.6 us
  transfers between devices with their start and end apart: 28, of which 16 were waited for; matrix products, arithmetic and copies ran while one was open for 2% of the time, Pallas kernels for 3%

profile of v5, /device:TPU:1, one launch (start us, length us, event | category | flops | bytes accessed | tf_op | source)
XLA Modules:
  0.0 206.2 jit_solution(7691294113305438351)
XLA Ops:
  0.0 6.2 %attend.1 = bf16[512,512]{1,0:T(8,128)(2,1)} custom-call(s32[4]{0:T(128)} %len_ref.1, s32[1]{0:T(128)} %bitcast.1.c_ref, bf16[4,576,128]{2,1,0:T(8,128)(2,1)} %bitcast.50, bf16[4,576,512]{2,1,0:T(8,128)(2,1)} %bitcast.48, bf16[4,576]{1,0:T(4,128)(2,1)} %new_ref.1), custom_call_target="tpu_custom_call" | custom-call | flops 603979776 | bytes 2359296 | tf_op jit(solution)/shard_map/attend/pallas_call | solution.py:97
  6.2 7.6 %all-to-all-start = ((bf16[16,32,512]{2,1,0:T(8,128)(2,1)}), bf16[16,32,512]{2,1,0:T(8,128)(2,1)S(1)}, u32[]{:S(2)}, u32[]{:S(2)}) async-start(bf16[16,32,512]{2,1,0:T(8,128)(2,1)} %bitcast.49), calls=%async_computation | async-start | bytes 1048576 | tf_op jit(solution)/shard_map/all_to_all | solution.py:555
  15.2 3.4 %dynamic-slice_bitcast_fusion = (bf16[256,1792]{1,0:T(8,128)(2,1)}, bf16[256,1792]{1,0:T(8,128)(2,1)}, bf16[256,1792]{1,0:T(8,128)(2,1)}) fusion(bf16[1,256,7168]{2,1,0:T(8,128)(2,1)} %param.33, s32[]{:T(128)S(6)} %select_n.11, s32[]{:T(128)S(6)} %select_n.10, s32[]{:T(128)S(6)} %select_n.9), kind=kLoop, calls=%fused_computation | loop fusion | bytes 5505036 | tf_op jit(solution)/shard_map/dynamic_slice | solution.py:533
  19.9 4.5 %all-to-all-done = bf16[16,32,512]{2,1,0:T(8,128)(2,1)S(1)} async-done(((bf16[16,32,512]{2,1,0:T(8,128)(2,1)}), bf16[16,32,512]{2,1,0:T(8,128)(2,1)S(1)}, u32[]{:S(2)}, u32[]{:S(2)}) %all-to-all-start) | async-done | bytes 524320 | tf_op jit(solution)/shard_map/all_to_all | solution.py:555
  28.6 3.3 %collective-permute-start.3 = (bf16[64,1024]{1,0:T(8,128)(2,1)S(1)}, bf16[64,1024]{1,0:T(8,128)(2,1)S(1)}, u32[]{:S(2)}, u32[]{:S(2)}) collective-permute-start(bf16[64,1024]{1,0:T(8,128)(2,1)S(1)} %head_values.1.h0), channel_id=1, source_target_pairs={{0,2},{1,3},{2,0},{3,1},{4,6},{5,7},{6,4},{7,5},{8,10},{9,11},{10,... | collective-permute-start | bytes 393224 | tf_op jit(solution)/shard_map/ppermute | solution.py:19
  34.6 3.8 %collective-permute-done.3.h2 = bf16[64,1024]{1,0:T(8,128)(2,1)S(1)} collective-permute-done((bf16[64,1024]{1,0:T(8,128)(2,1)S(1)}, bf16[64,1024]{1,0:T(8,128)(2,1)S(1)}, u32[]{:S(2)}, u32[]{:S(2)}) %collective-permute-start.3) | collective-permute-done | bytes 131104 | tf_op jit(solution)/shard_map/ppermute | solution.py:19
  44.1 17.9 %all_to_all.35.parts = bf16[16,16,1792]{2,1,0:T(8,128)(2,1)S(1)} all-to-all(bf16[16,16,1792]{2,1,0:T(8,128)(2,1)S(1)} %bitcast.43), channel_id=1, replica_groups=mesh['y'=4,'x'=4,'c'=2,'z'=4] {'y','x'}, dimensions={0} | all-to-all | bytes 1835008 | tf_op jit(solution)/shard_map/all_to_all | solution.py:39
  62.0 2.7 %collective-permute-done.7.refs_7_ = bf16[256,1792]{1,0:T(8,128)(2,1)S(1)} collective-permute-done((bf16[256,1792]{1,0:T(8,128)(2,1)}, bf16[256,1792]{1,0:T(8,128)(2,1)S(1)}, u32[]{:S(2)}, u32[]{:S(2)}) %collective-permute-start.7) | collective-permute-done | bytes 917536 | tf_op jit(solution)/shard_map/ppermute | solution.py:19
  65.7 17.1 %all_to_all.36 = bf16[16,16,1792]{2,1,0:T(8,128)(2,1)S(1)} all-to-all(bf16[16,16,1792]{2,1,0:T(8,128)(2,1)S(1)} %get-tuple-element.90), channel_id=1, replica_groups=mesh['y'=4,'x'=4,'c'=2,'z'=4] {'y','x'}, dimensions={0} | all-to-all | bytes 1835008 | tf_op jit(solution)/shard_map/all_to_all | solution.py:570
  82.8 2.8 %dense_in.1 = (bf16[64,1664]{1,0:T(8,128)(2,1)S(1)}, bf16[64,1664]{1,0:T(8,128)(2,1)S(1)}, bf16[64,1664]{1,0:T(8,128)(2,1)S(1)}, bf16[64,1664]{1,0:T(8,128)(2,1)S(1)}) custom-call(s32[1]{0:T(128)} %bitcast.z_ref, bf16[256,1792]{1,0:T(8,128)(2,1)S(1)} %bitcast.42, bf16[1,1792]{1,0:T(2,128)(2,1)S(1)} %reshape.51.gain, bf16[1792,384]{1,0:T(8,128)(2,1)S(1)} %copy-done.4, ...), custom_call_target="tpu_custom_call" | custom-call | flops 1409286144 | bytes 6422528 | tf_op jit(solution)/shard_map/dense_in/pallas_call | solution.py:327
  88.4 6.2 %collective-permute-done.11 = bf16[64,1664]{1,0:T(8,128)(2,1)S(1)} collective-permute-done((bf16[64,1664]{1,0:T(8,128)(2,1)S(1)}, bf16[64,1664]{1,0:T(8,128)(2,1)S(1)}, u32[]{:S(2)}, u32[]{:S(2)}) %collective-permute-start.11) | collective-permute-done | bytes 213024 | tf_op jit(solution)/shard_map/ppermute | solution.py:19
  98.2 4.0 %collective-permute-start.15 = (bf16[64,768]{1,0:T(8,128)(2,1)S(1)}, bf16[64,768]{1,0:T(8,128)(2,1)S(1)}, u32[]{:S(2)}, u32[]{:S(2)}) collective-permute-start(bf16[64,768]{1,0:T(8,128)(2,1)S(1)} %fusion.1.h0), channel_id=1, source_target_pairs={{0,2},{1,3},{2,0},{3,1},{4,6},{5,7},{6,4},{7,5},{8,10},{9,11},{10,... | collective-permute-start | bytes 294920 | tf_op jit(solution)/shard_map/ppermute | solution.py:19
  109.0 16.3 %all_to_all.37.parts = bf16[16,16,1792]{2,1,0:T(8,128)(2,1)S(1)} all-to-all(bf16[16,16,1792]{2,1,0:T(8,128)(2,1)S(1)} %bitcast.41), channel_id=1, replica_groups=mesh['y'=4,'x'=4,'c'=2,'z'=4] {'y','x'}, dimensions={0} | all-to-all | bytes 1835008 | tf_op jit(solution)/shard_map/all_to_all | solution.py:39
  125.3 2.6 %collective-permute-done.17.refs_6_ = bf16[256,1792]{1,0:T(8,128)(2,1)S(1)} collective-permute-done((bf16[256,1792]{1,0:T(8,128)(2,1)S(1)}, bf16[256,1792]{1,0:T(8,128)(2,1)S(1)}, u32[]{:S(2)}, u32[]{:S(2)}) %collective-permute-start.17) | collective-permute-done | bytes 917536 | tf_op jit(solution)/shard_map/ppermute | solution.py:19
  128.9 3.0 %collective-permute-start.18 = (bf16[16,1920]{1,0:T(8,128)(2,1)S(1)}, bf16[16,1920]{1,0:T(8,128)(2,1)S(1)}, u32[]{:S(2)}, u32[]{:S(2)}) collective-permute-start(bf16[16,1920]{1,0:T(8,128)(2,1)S(1)} %get-tuple-element.108), channel_id=1, source_target_pairs={{0,4},{4,0},{1,5},{5,1},{2,6},{6,2},{3,7},{7,3},{8,12},{12,8},{9,1... | collective-permute-start | bytes 184328 | tf_op jit(solution)/shard_map/ppermute | solution.py:23
  134.0 4.0 %all-to-all-start.4 = ((bf16[16,8,2816]{2,1,0:T(8,128)(2,1)}), bf16[16,8,2816]{2,1,0:T(8,128)(2,1)S(1)}, u32[]{:S(2)}, u32[]{:S(2)}) async-start(bf16[16,8,2816]{2,1,0:T(8,128)(2,1)} %bitcast.12), calls=%async_computation.4 | async-start | bytes 1441792 | tf_op jit(solution)/shard_map/all_to_all | solution.py:588
  138.7 5.1 %collective-permute-done.19.refs_0_ = bf16[32,1920]{1,0:T(8,128)(2,1)S(1)} collective-permute-done((bf16[32,1920]{1,0:T(8,128)(2,1)S(1)}, bf16[32,1920]{1,0:T(8,128)(2,1)S(1)}, u32[]{:S(2)}, u32[]{:S(2)}) %collective-permute-start.19) | collective-permute-done | bytes 122912 | tf_op jit(solution)/shard_map/ppermute | solution.py:19
  143.8 7.0 %all-to-all-done.4 = bf16[16,8,2816]{2,1,0:T(8,128)(2,1)S(1)} async-done(((bf16[16,8,2816]{2,1,0:T(8,128)(2,1)}), bf16[16,8,2816]{2,1,0:T(8,128)(2,1)S(1)}, u32[]{:S(2)}, u32[]{:S(2)}) %all-to-all-start.4) | async-done | bytes 720928 | tf_op jit(solution)/shard_map/all_to_all | solution.py:588
  150.9 2.7 %collective-permute-start.20 = (bf16[128,2816]{1,0:T(8,128)(2,1)S(1)}, bf16[128,2816]{1,0:T(8,128)(2,1)S(1)}, u32[]{:S(2)}, u32[]{:S(2)}) collective-permute-start(bf16[128,2816]{1,0:T(8,128)(2,1)S(1)} %bitcast.33), channel_id=1, source_target_pairs={{0,3},{1,0},{2,1},{3,2},{4,7},{5,4},{6,5},{7,6},{8,11},{9,8},{10,9... | collective-permute-start | bytes 2162696 | tf_op jit(solution)/shard_map/ppermute | solution.py:19
  153.9 15.3 %all_to_all.38 = bf16[16,8,2816]{2,1,0:T(8,128)(2,1)S(1)} all-to-all(bf16[16,8,2816]{2,1,0:T(8,128)(2,1)S(1)} %bitcast.44), channel_id=1, replica_groups=mesh['y'=4,'x'=4,'c'=2,'z'=4] {'y','x'}, dimensions={0} | all-to-all | bytes 1441792 | tf_op jit(solution)/shard_map/all_to_all | solution.py:588
  173.3 3.6 %expert_in.1.refs_0_ = bf16[192,256]{1,0:T(8,128)(2,1)S(1)} custom-call(s32[1]{0:T(128)} %bitcast.z_ref, bf16[128,2816]{1,0:T(8,128)(2,1)S(1)} %bitcast.34, bf16[128,2816]{1,0:T(8,128)(2,1)S(1)} %collective-permute-done.20.refs_1_.refs_5_.refs_9_, bf16[128,2816]{1,0:T(8,128)(2,1)S(1)} %bitcast.37, ...), custom_call_target="tpu_custom_call" | custom-call | flops 1409286144 | bytes 7340032 | tf_op jit(solution)/shard_map/expert_in/pallas_call | solution.py:400
  179.7 3.1 %collective-permute-done.24.refs_3_ = bf16[192,256]{1,0:T(8,128)(2,1)S(1)} collective-permute-done((bf16[192,256]{1,0:T(8,128)(2,1)S(1)}, bf16[192,256]{1,0:T(8,128)(2,1)S(1)}, u32[]{:S(2)}, u32[]{:S(2)}) %collective-permute-start.24) | collective-permute-done | bytes 98336 | tf_op jit(solution)/shard_map/ppermute | solution.py:19
  185.4 14.5 %all_to_all.39 = bf16[16,8,2688]{2,1,0:T(8,128)(2,1)S(1)} all-to-all(bf16[16,8,2688]{2,1,0:T(8,128)(2,1)S(1)} %bitcast.46), channel_id=1, replica_groups=mesh['y'=4,'x'=4,'c'=2,'z'=4] {'y','x'}, dimensions={0} | all-to-all | bytes 1376256 | tf_op jit(solution)/shard_map/all_to_all | solution.py:595
  200.4 4.3 %collective-permute-start.25 = (f32[16,1792]{1,0:T(8,128)S(1)}, f32[16,1792]{1,0:T(8,128)S(1)}, u32[]{:S(2)}, u32[]{:S(2)}) collective-permute-start(f32[16,1792]{1,0:T(8,128)S(1)} %get-tuple-element.118), channel_id=1, source_target_pairs={{0,4},{4,0},{1,5},{5,1},{2,6},{6,2},{3,7},{7,3},{8,12},{12,8},{9,1... | collective-permute-start | bytes 344072 | tf_op jit(solution)/shard_map/ppermute | solution.py:23
  (104 shorter events, 45.1 us)
Async XLA Ops:
  6.2 18.1 %all-to-all-start = ((bf16[16,32,512]{2,1,0:T(8,128)(2,1)}), bf16[16,32,512]{2,1,0:T(8,128)(2,1)S(1)}, u32[]{:S(2)}, u32[]{:S(2)}) async-start(bf16[16,32,512]{2,1,0:T(8,128)(2,1)} %bitcast.49), calls=%async_computation | async-start | bytes 1048576 | tf_op jit(solution)/shard_map/all_to_all | solution.py:555
  13.8 10.5 %collective-permute-start = (bf16[4,512,128]{2,1,0:T(8,128)(2,1)S(1)}, bf16[4,512,128]{2,1,0:T(8,128)(2,1)S(1)}, u32[]{:S(2)}, u32[]{:S(2)}) collective-permute-start(bf16[4,512,128]{2,1,0:T(8,128)(2,1)S(1)} %copy-done.11), channel_id=1, source_target_pairs={{0,4},{4,0},{1,5},{5,1},{2,6},{6,2},{3,7},{7,3},{8,12},{12,8},{9,1... | collective-permute-start | bytes 1572872 | tf_op jit(solution)/shard_map/ppermute | solution.py:23
  24.3 14.1 %collective-permute-start.5 = (bf16[512,1792]{1,0:T(8,128)(2,1)S(1)}, bf16[512,1792]{1,0:T(8,128)(2,1)S(1)}, u32[]{:S(2)}, u32[]{:S(2)}) collective-permute-start(bf16[512,1792]{1,0:T(8,128)(2,1)S(1)} %copy-done.3), channel_id=1, source_target_pairs={{0,4},{4,0},{1,5},{5,1},{2,6},{6,2},{3,7},{7,3},{8,12},{12,8},{9,1... | collective-permute-start | bytes 5505032 | tf_op jit(solution)/shard_map/ppermute | solution.py:23
  26.9 7.7 %collective-permute-start.4 = (bf16[64,1024]{1,0:T(8,128)(2,1)S(1)}, bf16[64,1024]{1,0:T(8,128)(2,1)S(1)}, u32[]{:S(2)}, u32[]{:S(2)}) collective-permute-start(bf16[64,1024]{1,0:T(8,128)(2,1)S(1)} %head_values.1.h0), channel_id=1, source_target_pairs={{0,1},{1,2},{2,3},{3,0},{4,5},{5,6},{6,7},{7,4},{8,9},{9,10},{10,1... | collective-permute-start | bytes 393224 | tf_op jit(solution)/shard_map/ppermute | solution.py:19
  28.6 9.8 %collective-permute-start.3 = (bf16[64,1024]{1,0:T(8,128)(2,1)S(1)}, bf16[64,1024]{1,0:T(8,128)(2,1)S(1)}, u32[]{:S(2)}, u32[]{:S(2)}) collective-permute-start(bf16[64,1024]{1,0:T(8,128)(2,1)S(1)} %head_values.1.h0), channel_id=1, source_target_pairs={{0,2},{1,3},{2,0},{3,1},{4,6},{5,7},{6,4},{7,5},{8,10},{9,11},{10,... | collective-permute-start | bytes 393224 | tf_op jit(solution)/shard_map/ppermute | solution.py:19
  31.9 6.5 %collective-permute-start.2 = (bf16[64,1024]{1,0:T(8,128)(2,1)S(1)}, bf16[64,1024]{1,0:T(8,128)(2,1)S(1)}, u32[]{:S(2)}, u32[]{:S(2)}) collective-permute-start(bf16[64,1024]{1,0:T(8,128)(2,1)S(1)} %head_values.1.h0), channel_id=1, source_target_pairs={{0,3},{1,0},{2,1},{3,2},{4,7},{5,4},{6,5},{7,6},{8,11},{9,8},{10,9... | collective-permute-start | bytes 393224 | tf_op jit(solution)/shard_map/ppermute | solution.py:19
  38.4 27.2 %collective-permute-start.8 = (bf16[1792,384]{1,0:T(8,128)(2,1)}, bf16[1792,384]{1,0:T(8,128)(2,1)S(1)}, u32[]{:S(2)}, u32[]{:S(2)}) collective-permute-start(bf16[1792,384]{1,0:T(8,128)(2,1)} %gate.1), channel_id=1, source_target_pairs={{0,4},{4,0},{1,5},{5,1},{2,6},{6,2},{3,7},{7,3},{8,12},{12,8},{9,1... | collective-permute-start | bytes 4128776 | tf_op jit(solution)/shard_map/ppermute | solution.py:23
  39.2 26.4 %collective-permute-start.9 = (bf16[1792,384]{1,0:T(8,128)(2,1)}, bf16[1792,384]{1,0:T(8,128)(2,1)S(1)}, u32[]{:S(2)}, u32[]{:S(2)}) collective-permute-start(bf16[1792,384]{1,0:T(8,128)(2,1)} %up.1), channel_id=1, source_target_pairs={{0,4},{4,0},{1,5},{5,1},{2,6},{6,2},{3,7},{7,3},{8,12},{12,8},{9,1... | collective-permute-start | bytes 4128776 | tf_op jit(solution)/shard_map/ppermute | solution.py:23
  39.3 26.3 %collective-permute-start.10 = (bf16[384,1792]{1,0:T(8,128)(2,1)}, bf16[384,1792]{1,0:T(8,128)(2,1)S(1)}, u32[]{:S(2)}, u32[]{:S(2)}) collective-permute-start(bf16[384,1792]{1,0:T(8,128)(2,1)} %own.5), channel_id=1, source_target_pairs={{0,4},{4,0},{1,5},{5,1},{2,6},{6,2},{3,7},{7,3},{8,12},{12,8},{9,1... | collective-permute-start | bytes 4128776 | tf_op jit(solution)/shard_map/ppermute | solution.py:23
  39.7 22.3 %collective-permute-start.6 = (bf16[256,1792]{1,0:T(8,128)(2,1)}, bf16[256,1792]{1,0:T(8,128)(2,1)S(1)}, u32[]{:S(2)}, u32[]{:S(2)}) collective-permute-start(bf16[256,1792]{1,0:T(8,128)(2,1)} %get-tuple-element.82), channel_id=1, source_target_pairs={{0,3},{1,0},{2,1},{3,2},{4,7},{5,4},{6,5},{7,6},{8,11},{9,8},{10,9... | collective-permute-start | bytes 2752520 | tf_op jit(solution)/shard_map/ppermute | solution.py:19
  41.6 23.1 %collective-permute-start.7 = (bf16[256,1792]{1,0:T(8,128)(2,1)}, bf16[256,1792]{1,0:T(8,128)(2,1)S(1)}, u32[]{:S(2)}, u32[]{:S(2)}) collective-permute-start(bf16[256,1792]{1,0:T(8,128)(2,1)} %get-tuple-element.83), channel_id=1, source_target_pairs={{0,1},{1,2},{2,3},{3,0},{4,5},{5,6},{6,7},{7,4},{8,9},{9,10},{10,1... | collective-permute-start | bytes 2752520 | tf_op jit(solution)/shard_map/ppermute | solution.py:19
  85.6 9.0 %collective-permute-start.11 = (bf16[64,1664]{1,0:T(8,128)(2,1)S(1)}, bf16[64,1664]{1,0:T(8,128)(2,1)S(1)}, u32[]{:S(2)}, u32[]{:S(2)}) collective-permute-start(bf16[64,1664]{1,0:T(8,128)(2,1)S(1)} %get-tuple-element.95), channel_id=1, source_target_pairs={{0,1},{1,2},{2,3},{3,0},{4,5},{5,6},{6,7},{7,4},{8,9},{9,10},{10,1... | collective-permute-start | bytes 638984 | tf_op jit(solution)/shard_map/ppermute | solution.py:19
  85.7 8.9 %collective-permute-start.12 = (bf16[64,1664]{1,0:T(8,128)(2,1)S(1)}, bf16[64,1664]{1,0:T(8,128)(2,1)S(1)}, u32[]{:S(2)}, u32[]{:S(2)}) collective-permute-start(bf16[64,1664]{1,0:T(8,128)(2,1)S(1)} %get-tuple-element.96), channel_id=1, source_target_pairs={{0,2},{1,3},{2,0},{3,1},{4,6},{5,7},{6,4},{7,5},{8,10},{9,11},{10,... | collective-permute-start | bytes 638984 | tf_op jit(solution)/shard_map/ppermute | solution.py:19
  87.3 9.7 %collective-permute-start.13 = (bf16[64,1664]{1,0:T(8,128)(2,1)S(1)}, bf16[64,1664]{1,0:T(8,128)(2,1)S(1)}, u32[]{:S(2)}, u32[]{:S(2)}) collective-permute-start(bf16[64,1664]{1,0:T(8,128)(2,1)S(1)} %get-tuple-element.97), channel_id=1, source_target_pairs={{0,3},{1,0},{2,1},{3,2},{4,7},{5,4},{6,5},{7,6},{8,11},{9,8},{10,9... | collective-permute-start | bytes 638984 | tf_op jit(solution)/shard_map/ppermute | solution.py:19
  97.5 5.6 %collective-permute-start.16 = (bf16[64,768]{1,0:T(8,128)(2,1)S(1)}, bf16[64,768]{1,0:T(8,128)(2,1)S(1)}, u32[]{:S(2)}, u32[]{:S(2)}) collective-permute-start(bf16[64,768]{1,0:T(8,128)(2,1)S(1)} %fusion.1.h0), channel_id=1, source_target_pairs={{0,1},{1,2},{2,3},{3,0},{4,5},{5,6},{6,7},{7,4},{8,9},{9,10},{10,1... | collective-permute-start | bytes 294920 | tf_op jit(solution)/shard_map/ppermute | solution.py:19
  98.2 7.4 %collective-permute-start.15 = (bf16[64,768]{1,0:T(8,128)(2,1)S(1)}, bf16[64,768]{1,0:T(8,128)(2,1)S(1)}, u32[]{:S(2)}, u32[]{:S(2)}) collective-permute-start(bf16[64,768]{1,0:T(8,128)(2,1)S(1)} %fusion.1.h0), channel_id=1, source_target_pairs={{0,2},{1,3},{2,0},{3,1},{4,6},{5,7},{6,4},{7,5},{8,10},{9,11},{10,... | collective-permute-start | bytes 294920 | tf_op jit(solution)/shard_map/ppermute | solution.py:19
  106.7 21.3 %collective-permute-start.17 = (bf16[256,1792]{1,0:T(8,128)(2,1)S(1)}, bf16[256,1792]{1,0:T(8,128)(2,1)S(1)}, u32[]{:S(2)}, u32[]{:S(2)}) collective-permute-start(bf16[256,1792]{1,0:T(8,128)(2,1)S(1)} %copy-done.15), channel_id=1, source_target_pairs={{0,2},{1,3},{2,0},{3,1},{4,6},{5,7},{6,4},{7,5},{8,10},{9,11},{10,... | collective-permute-start | bytes 2752520 | tf_op jit(solution)/shard_map/ppermute | solution.py:19
  134.0 16.8 %all-to-all-start.4 = ((bf16[16,8,2816]{2,1,0:T(8,128)(2,1)}), bf16[16,8,2816]{2,1,0:T(8,128)(2,1)S(1)}, u32[]{:S(2)}, u32[]{:S(2)}) async-start(bf16[16,8,2816]{2,1,0:T(8,128)(2,1)} %bitcast.12), calls=%async_computation.4 | async-start | bytes 1441792 | tf_op jit(solution)/shard_map/all_to_all | solution.py:588
  138.0 5.8 %collective-permute-start.19 = (bf16[32,1920]{1,0:T(8,128)(2,1)S(1)}, bf16[32,1920]{1,0:T(8,128)(2,1)S(1)}, u32[]{:S(2)}, u32[]{:S(2)}) collective-permute-start(bf16[32,1920]{1,0:T(8,128)(2,1)S(1)} %constant_dynamic-update-slice_fusion.refs_0_), channel_id=1, source_target_pairs={{0,2},{1,3},{2,0},{3,1},{4,6},{5,7},{6,4},{7,5},{8,10},{9,11},{10,... | collective-permute-start | bytes 368648 | tf_op jit(solution)/shard_map/ppermute | solution.py:19
  150.8 18.3 %collective-permute-start.21 = (bf16[128,2816]{1,0:T(8,128)(2,1)S(1)}, bf16[128,2816]{1,0:T(8,128)(2,1)S(1)}, u32[]{:S(2)}, u32[]{:S(2)}) collective-permute-start(bf16[128,2816]{1,0:T(8,128)(2,1)S(1)} %bitcast.32), channel_id=1, source_target_pairs={{0,1},{1,2},{2,3},{3,0},{4,5},{5,6},{6,7},{7,4},{8,9},{9,10},{10,1... | collective-permute-start | bytes 2162696 | tf_op jit(solution)/shard_map/ppermute | solution.py:19
  150.9 18.3 %collective-permute-start.20 = (bf16[128,2816]{1,0:T(8,128)(2,1)S(1)}, bf16[128,2816]{1,0:T(8,128)(2,1)S(1)}, u32[]{:S(2)}, u32[]{:S(2)}) collective-permute-start(bf16[128,2816]{1,0:T(8,128)(2,1)S(1)} %bitcast.33), channel_id=1, source_target_pairs={{0,3},{1,0},{2,1},{3,2},{4,7},{5,4},{6,5},{7,6},{8,11},{9,8},{10,9... | collective-permute-start | bytes 2162696 | tf_op jit(solution)/shard_map/ppermute | solution.py:19
  176.9 5.8 %collective-permute-start.24 = (bf16[192,256]{1,0:T(8,128)(2,1)S(1)}, bf16[192,256]{1,0:T(8,128)(2,1)S(1)}, u32[]{:S(2)}, u32[]{:S(2)}) collective-permute-start(bf16[192,256]{1,0:T(8,128)(2,1)S(1)} %expert_in.1.refs_0_), channel_id=1, source_target_pairs={{0,1},{1,2},{2,3},{3,0},{4,5},{5,6},{6,7},{7,4},{8,9},{9,10},{10,1... | collective-permute-start | bytes 294920 | tf_op jit(solution)/shard_map/ppermute | solution.py:19
  177.0 5.7 %collective-permute-start.23 = (bf16[192,256]{1,0:T(8,128)(2,1)S(1)}, bf16[192,256]{1,0:T(8,128)(2,1)S(1)}, u32[]{:S(2)}, u32[]{:S(2)}) collective-permute-start(bf16[192,256]{1,0:T(8,128)(2,1)S(1)} %expert_in.1.refs_0_), channel_id=1, source_target_pairs={{0,2},{1,3},{2,0},{3,1},{4,6},{5,7},{6,4},{7,5},{8,10},{9,11},{10,... | collective-permute-start | bytes 294920 | tf_op jit(solution)/shard_map/ppermute | solution.py:19
  200.4 5.2 %collective-permute-start.25 = (f32[16,1792]{1,0:T(8,128)S(1)}, f32[16,1792]{1,0:T(8,128)S(1)}, u32[]{:S(2)}, u32[]{:S(2)}) collective-permute-start(f32[16,1792]{1,0:T(8,128)S(1)} %get-tuple-element.118), channel_id=1, source_target_pairs={{0,4},{4,0},{1,5},{5,1},{2,6},{6,2},{3,7},{7,3},{8,12},{12,8},{9,1... | collective-permute-start | bytes 344072 | tf_op jit(solution)/shard_map/ppermute | solution.py:23
  (24 other events, 237.7 us)

commit v6 on v5

--- a/solution.py
+++ b/solution.py
@@ -583,10 +583,14 @@
     parts, down_b = tied(parts, down_b)
     second, scaled = second_sum(parts, first, gain_b)
 
+    across = lambda rows, flip: lax.ppermute(
+        rows, ("c", "z"), [(c0 * NZ + z0, (c0 ^ flip) * NZ + (z0 + 2) % NZ) for c0 in range(2) for z0 in range(NZ)]
+    )
+    far = jnp.concatenate([across(scaled, 0), across(scaled, 1)], axis=0)
     scaled = jnp.concatenate([scaled, swap_core(scaled)], axis=0)
-    far = zsend(scaled, 2)
     spread = lambda rows: lax.all_to_all(rows.reshape(16, 8, -1), YX, 0, 0, tiled=True).reshape(128, -1)
-    near = spread(pack(scaled, hots, quarter))
+    near, far = lax.optimization_barrier((pack(scaled, hots, quarter), far))
+    near = spread(near)
     near, far = lax.optimization_barrier((near, far))
     ahead, behind = zsend(near, NZ - 1), zsend(near, 1)
     far = spread(pack(far, hots, quarter))

time: 207 us -> 204 us (0.986)
  blocking collectives: 81.1 us -> 95.5 us
  waiting for transfers between devices: 46.1 us -> 35.2 us
  local copies, waits for them, and re-layouts: 10.1 us -> 4.35 us
    all_to_all x1 -> x2, blocking collectives: 15.3 us -> 30.4 us  [shards(): lax.all_to_all(rows.reshape(16, 8, -1), YX, 0, 0, tiled=True)]
    all_to_all x1 -> x0, waiting for transfers between devices: 7.02 us -> none  [shards(): lax.all_to_all(rows.reshape(16, 8, -1), YX, 0, 0, tiled=True)]
    unnamed x42 -> x33, local copies, waits for them, and re-layouts: 6.56 us -> 0.81 us
    ppermute x18 -> x17, waiting for transfers between devices: 32.8 us -> 27.2 us  [zsend(): return lax.ppermute(values, 'z', [(i, (i + shift) % NZ) for i in range(NZ)])]
    all_to_all x1 -> x0, starting transfers between devices: 3.96 us -> none  [shards(): lax.all_to_all(rows.reshape(16, 8, -1), YX, 0, 0, tiled=True)]
    ppermute x0 -> x2, starting transfers between devices: none -> 2.95 us  [shards(): lax.ppermute(rows, ('c', 'z'), [(c0 * NZ + z0, (c0 ^ flip) * NZ + (z0 + 2...]
    ppermute x0 -> x2, waiting for transfers between devices: none -> 2.51 us  [shards(): lax.ppermute(rows, ('c', 'z'), [(c0 * NZ + z0, (c0 ^ flip) * NZ + (z0 + 2...]
    ppermute x18 -> x17, starting transfers between devices: 21.9 us -> 21.6 us  [zsend(): return lax.ppermute(values, 'z', [(i, (i + shift) % NZ) for i in range(NZ)])]
where the time goes in v6:
time: 204 us
  blocking collectives  95.5 us (47%)
  starting transfers between devices  45.7 us (22%)
  waiting for transfers between devices  35.2 us (17%)
  Pallas kernels  21.5 us (11%)
  local copies, waits for them, and re-layouts  4.35 us (2%)
    all_to_all x2, blocking collectives, plane_scatter(): return lax.all_to_all(rows.reshape(16, 16, -1), YX, 0, 0, tiled=True)  34.5 us
    all_to_all x2, blocking collectives, shards(): lax.all_to_all(rows.reshape(16, 8, -1), YX, 0, 0, tiled=True)  30.4 us
    ppermute x17, waiting for transfers between devices, zsend(): return lax.ppermute(values, 'z', [(i, (i + shift) % NZ) for i in range(NZ)])  27.2 us
    ppermute x17, starting transfers between devices, zsend(): return lax.ppermute(values, 'z', [(i, (i + shift) % NZ) for i in range(NZ)])  21.6 us
    all_to_all x1, blocking collectives, shards(): own = lax.all_to_all(spread, YX, 0, 0, tiled=True).reshape(256, -1)  17.1 us
    all_to_all x1, blocking collectives, shards(): lax.all_to_all(result.reshape(16, 8, -1), YX, 0, 0, tiled=True)  13.5 us
    ppermute x8, starting transfers between devices, swap_core(): return lax.ppermute(values, 'c', [(0, 1), (1, 0)])  13.5 us
    all_to_all x1, starting transfers between devices, shards(): moved = lax.all_to_all(latents.reshape(16, 32, -1), YX, 0, 0, tiled=True)  7.6 us
  transfers between devices with their start and end apart: 28, of which 16 were waited for; matrix products, arithmetic and copies ran while one was open for 2% of the time, Pallas kernels for 3%

profile of v6, /device:TPU:1, one launch (start us, length us, event | category | flops | bytes accessed | tf_op | source)
XLA Modules:
  0.0 203.8 jit_solution(4674985571988898931)
XLA Ops:
  0.0 6.2 %attend.1 = bf16[512,512]{1,0:T(8,128)(2,1)} custom-call(s32[4]{0:T(128)} %len_ref.1, s32[1]{0:T(128)} %bitcast.1.c_ref, bf16[4,576,128]{2,1,0:T(8,128)(2,1)} %bitcast.51, bf16[4,576,512]{2,1,0:T(8,128)(2,1)} %bitcast.49, bf16[4,576]{1,0:T(4,128)(2,1)} %new_ref.1), custom_call_target="tpu_custom_call" | custom-call | flops 603979776 | bytes 2359296 | tf_op jit(solution)/shard_map/attend/pallas_call | solution.py:97
  6.2 7.6 %all-to-all-start = ((bf16[16,32,512]{2,1,0:T(8,128)(2,1)}), bf16[16,32,512]{2,1,0:T(8,128)(2,1)S(1)}, u32[]{:S(2)}, u32[]{:S(2)}) async-start(bf16[16,32,512]{2,1,0:T(8,128)(2,1)} %bitcast.50), calls=%async_computation | async-start | bytes 1048576 | tf_op jit(solution)/shard_map/all_to_all | solution.py:555
  15.2 3.4 %dynamic-slice_bitcast_fusion = (bf16[256,1792]{1,0:T(8,128)(2,1)}, bf16[256,1792]{1,0:T(8,128)(2,1)}, bf16[256,1792]{1,0:T(8,128)(2,1)}) fusion(bf16[1,256,7168]{2,1,0:T(8,128)(2,1)} %param.33, s32[]{:T(128)S(6)} %select_n.11, s32[]{:T(128)S(6)} %select_n.10, s32[]{:T(128)S(6)} %select_n.9), kind=kLoop, calls=%fused_computation | loop fusion | bytes 5505036 | tf_op jit(solution)/shard_map/dynamic_slice | solution.py:533
  19.9 4.5 %all-to-all-done = bf16[16,32,512]{2,1,0:T(8,128)(2,1)S(1)} async-done(((bf16[16,32,512]{2,1,0:T(8,128)(2,1)}), bf16[16,32,512]{2,1,0:T(8,128)(2,1)S(1)}, u32[]{:S(2)}, u32[]{:S(2)}) %all-to-all-start) | async-done | bytes 524320 | tf_op jit(solution)/shard_map/all_to_all | solution.py:555
  28.6 3.3 %collective-permute-start.3 = (bf16[64,1024]{1,0:T(8,128)(2,1)S(1)}, bf16[64,1024]{1,0:T(8,128)(2,1)S(1)}, u32[]{:S(2)}, u32[]{:S(2)}) collective-permute-start(bf16[64,1024]{1,0:T(8,128)(2,1)S(1)} %head_values.1.h0), channel_id=1, source_target_pairs={{0,2},{1,3},{2,0},{3,1},{4,6},{5,7},{6,4},{7,5},{8,10},{9,11},{10,... | collective-permute-start | bytes 393224 | tf_op jit(solution)/shard_map/ppermute | solution.py:19
  34.6 3.8 %collective-permute-done.3.h2 = bf16[64,1024]{1,0:T(8,128)(2,1)S(1)} collective-permute-done((bf16[64,1024]{1,0:T(8,128)(2,1)S(1)}, bf16[64,1024]{1,0:T(8,128)(2,1)S(1)}, u32[]{:S(2)}, u32[]{:S(2)}) %collective-permute-start.3) | collective-permute-done | bytes 131104 | tf_op jit(solution)/shard_map/ppermute | solution.py:19
  41.6 2.5 %out_proj.1 = bf16[256,1792]{1,0:T(8,128)(2,1)S(1)} custom-call(s32[1]{0:T(128)} %bitcast.z_ref, bf16[64,1024]{1,0:T(8,128)(2,1)S(1)} %head_values.1.h0, bf16[64,1024]{1,0:T(8,128)(2,1)S(1)} %collective-permute-done.2.h1, bf16[64,1024]{1,0:T(8,128)(2,1)S(1)} %collective-permute-done.3.h2, bf16[64,1024]{1,0:T(8,128)(2,1)S(1)} %collective-permute-done.4.h3, ...), custom_call_target="tpu_custom_call" | custom-call | flops 939524096 | bytes 3670016 | tf_op jit(solution)/shard_map/out_proj/pallas_call | solution.py:505
  44.1 17.9 %all_to_all.35.parts = bf16[16,16,1792]{2,1,0:T(8,128)(2,1)S(1)} all-to-all(bf16[16,16,1792]{2,1,0:T(8,128)(2,1)S(1)} %bitcast.43), channel_id=1, replica_groups=mesh['y'=4,'x'=4,'c'=2,'z'=4] {'y','x'}, dimensions={0} | all-to-all | bytes 1835008 | tf_op jit(solution)/shard_map/all_to_all | solution.py:39
  62.0 2.7 %collective-permute-done.7.refs_7_ = bf16[256,1792]{1,0:T(8,128)(2,1)S(1)} collective-permute-done((bf16[256,1792]{1,0:T(8,128)(2,1)}, bf16[256,1792]{1,0:T(8,128)(2,1)S(1)}, u32[]{:S(2)}, u32[]{:S(2)}) %collective-permute-start.7) | collective-permute-done | bytes 917536 | tf_op jit(solution)/shard_map/ppermute | solution.py:19
  64.8 17.1 %all_to_all.36 = bf16[16,16,1792]{2,1,0:T(8,128)(2,1)S(1)} all-to-all(bf16[16,16,1792]{2,1,0:T(8,128)(2,1)S(1)} %get-tuple-element.92), channel_id=1, replica_groups=mesh['y'=4,'x'=4,'c'=2,'z'=4] {'y','x'}, dimensions={0} | all-to-all | bytes 1835008 | tf_op jit(solution)/shard_map/all_to_all | solution.py:570
  81.9 2.8 %dense_in.1 = (bf16[64,1664]{1,0:T(8,128)(2,1)S(1)}, bf16[64,1664]{1,0:T(8,128)(2,1)S(1)}, bf16[64,1664]{1,0:T(8,128)(2,1)S(1)}, bf16[64,1664]{1,0:T(8,128)(2,1)S(1)}) custom-call(s32[1]{0:T(128)} %bitcast.z_ref, bf16[256,1792]{1,0:T(8,128)(2,1)S(1)} %bitcast.42, bf16[1,1792]{1,0:T(2,128)(2,1)S(1)} %reshape.51.gain, bf16[1792,384]{1,0:T(8,128)(2,1)S(1)} %copy-done.4, ...), custom_call_target="tpu_custom_call" | custom-call | flops 1409286144 | bytes 6422528 | tf_op jit(solution)/shard_map/dense_in/pallas_call | solution.py:327
  87.5 6.2 %collective-permute-done.11 = bf16[64,1664]{1,0:T(8,128)(2,1)S(1)} collective-permute-done((bf16[64,1664]{1,0:T(8,128)(2,1)S(1)}, bf16[64,1664]{1,0:T(8,128)(2,1)S(1)}, u32[]{:S(2)}, u32[]{:S(2)}) %collective-permute-start.11) | collective-permute-done | bytes 213024 | tf_op jit(solution)/shard_map/ppermute | solution.py:19
  93.7 2.4 %collective-permute-done.13 = bf16[64,1664]{1,0:T(8,128)(2,1)S(1)} collective-permute-done((bf16[64,1664]{1,0:T(8,128)(2,1)S(1)}, bf16[64,1664]{1,0:T(8,128)(2,1)S(1)}, u32[]{:S(2)}, u32[]{:S(2)}) %collective-permute-start.13) | collective-permute-done | bytes 213024 | tf_op jit(solution)/shard_map/ppermute | solution.py:19
  97.3 4.0 %collective-permute-start.15 = (bf16[64,768]{1,0:T(8,128)(2,1)S(1)}, bf16[64,768]{1,0:T(8,128)(2,1)S(1)}, u32[]{:S(2)}, u32[]{:S(2)}) collective-permute-start(bf16[64,768]{1,0:T(8,128)(2,1)S(1)} %fusion.1.h0), channel_id=1, source_target_pairs={{0,2},{1,3},{2,0},{3,1},{4,6},{5,7},{6,4},{7,5},{8,10},{9,11},{10,... | collective-permute-start | bytes 294920 | tf_op jit(solution)/shard_map/ppermute | solution.py:19
  102.2 2.6 %collective-permute-done.15.h2 = bf16[64,768]{1,0:T(8,128)(2,1)S(1)} collective-permute-done((bf16[64,768]{1,0:T(8,128)(2,1)S(1)}, bf16[64,768]{1,0:T(8,128)(2,1)S(1)}, u32[]{:S(2)}, u32[]{:S(2)}) %collective-permute-start.15) | collective-permute-done | bytes 98336 | tf_op jit(solution)/shard_map/ppermute | solution.py:19
  108.1 16.6 %all_to_all.37.parts = bf16[16,16,1792]{2,1,0:T(8,128)(2,1)S(1)} all-to-all(bf16[16,16,1792]{2,1,0:T(8,128)(2,1)S(1)} %bitcast.41), channel_id=1, replica_groups=mesh['y'=4,'x'=4,'c'=2,'z'=4] {'y','x'}, dimensions={0} | all-to-all | bytes 1835008 | tf_op jit(solution)/shard_map/all_to_all | solution.py:39
  127.2 3.0 %collective-permute-start.18 = (bf16[16,1920]{1,0:T(8,128)(2,1)S(1)}, bf16[16,1920]{1,0:T(8,128)(2,1)S(1)}, u32[]{:S(2)}, u32[]{:S(2)}) collective-permute-start(bf16[16,1920]{1,0:T(8,128)(2,1)S(1)} %get-tuple-element.110), channel_id=1, source_target_pairs={{0,4},{4,0},{1,5},{5,1},{2,6},{6,2},{3,7},{7,3},{8,12},{12,8},{9,1... | collective-permute-start | bytes 184328 | tf_op jit(solution)/shard_map/ppermute | solution.py:23
  136.1 16.6 %all_to_all.38 = bf16[16,8,2816]{2,1,0:T(8,128)(2,1)S(1)} all-to-all(bf16[16,8,2816]{2,1,0:T(8,128)(2,1)S(1)} %bitcast.44), channel_id=1, replica_groups=mesh['y'=4,'x'=4,'c'=2,'z'=4] {'y','x'}, dimensions={0} | all-to-all | bytes 1441792 | tf_op jit(solution)/shard_map/all_to_all | solution.py:591
  152.7 2.7 %collective-permute-start.21 = (bf16[128,2816]{1,0:T(8,128)(2,1)S(1)}, bf16[128,2816]{1,0:T(8,128)(2,1)S(1)}, u32[]{:S(2)}, u32[]{:S(2)}) collective-permute-start(bf16[128,2816]{1,0:T(8,128)(2,1)S(1)} %bitcast.33), channel_id=1, source_target_pairs={{0,3},{1,0},{2,1},{3,2},{4,7},{5,4},{6,5},{7,6},{8,11},{9,8},{10,9... | collective-permute-start | bytes 2162696 | tf_op jit(solution)/shard_map/ppermute | solution.py:19
  155.8 13.8 %all_to_all.39 = bf16[16,8,2816]{2,1,0:T(8,128)(2,1)S(1)} all-to-all(bf16[16,8,2816]{2,1,0:T(8,128)(2,1)S(1)} %bitcast.45), channel_id=1, replica_groups=mesh['y'=4,'x'=4,'c'=2,'z'=4] {'y','x'}, dimensions={0} | all-to-all | bytes 1441792 | tf_op jit(solution)/shard_map/all_to_all | solution.py:591
  169.6 3.7 %expert_in.1.refs_0_ = bf16[192,256]{1,0:T(8,128)(2,1)S(1)} custom-call(s32[1]{0:T(128)} %bitcast.z_ref, bf16[128,2816]{1,0:T(8,128)(2,1)S(1)} %bitcast.34, bf16[128,2816]{1,0:T(8,128)(2,1)S(1)} %collective-permute-done.21.refs_1_.refs_5_.refs_9_, bf16[128,2816]{1,0:T(8,128)(2,1)S(1)} %bitcast.37, ...), custom_call_target="tpu_custom_call" | custom-call | flops 1409286144 | bytes 7340032 | tf_op jit(solution)/shard_map/expert_in/pallas_call | solution.py:400
  173.4 3.1 %collective-permute-start.24 = (bf16[192,256]{1,0:T(8,128)(2,1)S(1)}, bf16[192,256]{1,0:T(8,128)(2,1)S(1)}, u32[]{:S(2)}, u32[]{:S(2)}) collective-permute-start(bf16[192,256]{1,0:T(8,128)(2,1)S(1)} %expert_in.1.refs_0_), channel_id=1, source_target_pairs={{0,2},{1,3},{2,0},{3,1},{4,6},{5,7},{6,4},{7,5},{8,10},{9,11},{10,... | collective-permute-start | bytes 294920 | tf_op jit(solution)/shard_map/ppermute | solution.py:19
  182.1 13.5 %all_to_all.40 = bf16[16,8,2688]{2,1,0:T(8,128)(2,1)S(1)} all-to-all(bf16[16,8,2688]{2,1,0:T(8,128)(2,1)S(1)} %bitcast.47), channel_id=1, replica_groups=mesh['y'=4,'x'=4,'c'=2,'z'=4] {'y','x'}, dimensions={0} | all-to-all | bytes 1376256 | tf_op jit(solution)/shard_map/all_to_all | solution.py:599
  196.0 6.2 %collective-permute-start.26 = (f32[16,1792]{1,0:T(8,128)S(1)}, f32[16,1792]{1,0:T(8,128)S(1)}, u32[]{:S(2)}, u32[]{:S(2)}) collective-permute-start(f32[16,1792]{1,0:T(8,128)S(1)} %get-tuple-element.122), channel_id=1, source_target_pairs={{0,4},{4,0},{1,5},{5,1},{2,6},{6,2},{3,7},{7,3},{8,12},{12,8},{9,1... | collective-permute-start | bytes 344072 | tf_op jit(solution)/shard_map/ppermute | solution.py:23
  (97 shorter events, 37.3 us)
Async XLA Ops:
  6.2 18.1 %all-to-all-start = ((bf16[16,32,512]{2,1,0:T(8,128)(2,1)}), bf16[16,32,512]{2,1,0:T(8,128)(2,1)S(1)}, u32[]{:S(2)}, u32[]{:S(2)}) async-start(bf16[16,32,512]{2,1,0:T(8,128)(2,1)} %bitcast.50), calls=%async_computation | async-start | bytes 1048576 | tf_op jit(solution)/shard_map/all_to_all | solution.py:555
  13.8 10.5 %collective-permute-start = (bf16[4,512,128]{2,1,0:T(8,128)(2,1)S(1)}, bf16[4,512,128]{2,1,0:T(8,128)(2,1)S(1)}, u32[]{:S(2)}, u32[]{:S(2)}) collective-permute-start(bf16[4,512,128]{2,1,0:T(8,128)(2,1)S(1)} %copy-done.7), channel_id=1, source_target_pairs={{0,4},{4,0},{1,5},{5,1},{2,6},{6,2},{3,7},{7,3},{8,12},{12,8},{9,1... | collective-permute-start | bytes 1572872 | tf_op jit(solution)/shard_map/ppermute | solution.py:23
  24.3 14.1 %collective-permute-start.5 = (bf16[512,1792]{1,0:T(8,128)(2,1)S(1)}, bf16[512,1792]{1,0:T(8,128)(2,1)S(1)}, u32[]{:S(2)}, u32[]{:S(2)}) collective-permute-start(bf16[512,1792]{1,0:T(8,128)(2,1)S(1)} %copy-done.3), channel_id=1, source_target_pairs={{0,4},{4,0},{1,5},{5,1},{2,6},{6,2},{3,7},{7,3},{8,12},{12,8},{9,1... | collective-permute-start | bytes 5505032 | tf_op jit(solution)/shard_map/ppermute | solution.py:23
  26.9 7.7 %collective-permute-start.4 = (bf16[64,1024]{1,0:T(8,128)(2,1)S(1)}, bf16[64,1024]{1,0:T(8,128)(2,1)S(1)}, u32[]{:S(2)}, u32[]{:S(2)}) collective-permute-start(bf16[64,1024]{1,0:T(8,128)(2,1)S(1)} %head_values.1.h0), channel_id=1, source_target_pairs={{0,1},{1,2},{2,3},{3,0},{4,5},{5,6},{6,7},{7,4},{8,9},{9,10},{10,1... | collective-permute-start | bytes 393224 | tf_op jit(solution)/shard_map/ppermute | solution.py:19
  28.6 9.8 %collective-permute-start.3 = (bf16[64,1024]{1,0:T(8,128)(2,1)S(1)}, bf16[64,1024]{1,0:T(8,128)(2,1)S(1)}, u32[]{:S(2)}, u32[]{:S(2)}) collective-permute-start(bf16[64,1024]{1,0:T(8,128)(2,1)S(1)} %head_values.1.h0), channel_id=1, source_target_pairs={{0,2},{1,3},{2,0},{3,1},{4,6},{5,7},{6,4},{7,5},{8,10},{9,11},{10,... | collective-permute-start | bytes 393224 | tf_op jit(solution)/shard_map/ppermute | solution.py:19
  31.9 6.5 %collective-permute-start.2 = (bf16[64,1024]{1,0:T(8,128)(2,1)S(1)}, bf16[64,1024]{1,0:T(8,128)(2,1)S(1)}, u32[]{:S(2)}, u32[]{:S(2)}) collective-permute-start(bf16[64,1024]{1,0:T(8,128)(2,1)S(1)} %head_values.1.h0), channel_id=1, source_target_pairs={{0,3},{1,0},{2,1},{3,2},{4,7},{5,4},{6,5},{7,6},{8,11},{9,8},{10,9... | collective-permute-start | bytes 393224 | tf_op jit(solution)/shard_map/ppermute | solution.py:19
  38.4 26.3 %collective-permute-start.8 = (bf16[1792,384]{1,0:T(8,128)(2,1)}, bf16[1792,384]{1,0:T(8,128)(2,1)S(1)}, u32[]{:S(2)}, u32[]{:S(2)}) collective-permute-start(bf16[1792,384]{1,0:T(8,128)(2,1)} %gate.1), channel_id=1, source_target_pairs={{0,4},{4,0},{1,5},{5,1},{2,6},{6,2},{3,7},{7,3},{8,12},{12,8},{9,1... | collective-permute-start | bytes 4128776 | tf_op jit(solution)/shard_map/ppermute | solution.py:23
  39.2 25.5 %collective-permute-start.9 = (bf16[1792,384]{1,0:T(8,128)(2,1)}, bf16[1792,384]{1,0:T(8,128)(2,1)S(1)}, u32[]{:S(2)}, u32[]{:S(2)}) collective-permute-start(bf16[1792,384]{1,0:T(8,128)(2,1)} %up.1), channel_id=1, source_target_pairs={{0,4},{4,0},{1,5},{5,1},{2,6},{6,2},{3,7},{7,3},{8,12},{12,8},{9,1... | collective-permute-start | bytes 4128776 | tf_op jit(solution)/shard_map/ppermute | solution.py:23
  39.3 25.4 %collective-permute-start.10 = (bf16[384,1792]{1,0:T(8,128)(2,1)}, bf16[384,1792]{1,0:T(8,128)(2,1)S(1)}, u32[]{:S(2)}, u32[]{:S(2)}) collective-permute-start(bf16[384,1792]{1,0:T(8,128)(2,1)} %own.5), channel_id=1, source_target_pairs={{0,4},{4,0},{1,5},{5,1},{2,6},{6,2},{3,7},{7,3},{8,12},{12,8},{9,1... | collective-permute-start | bytes 4128776 | tf_op jit(solution)/shard_map/ppermute | solution.py:23
  39.7 22.3 %collective-permute-start.6 = (bf16[256,1792]{1,0:T(8,128)(2,1)}, bf16[256,1792]{1,0:T(8,128)(2,1)S(1)}, u32[]{:S(2)}, u32[]{:S(2)}) collective-permute-start(bf16[256,1792]{1,0:T(8,128)(2,1)} %get-tuple-element.84), channel_id=1, source_target_pairs={{0,3},{1,0},{2,1},{3,2},{4,7},{5,4},{6,5},{7,6},{8,11},{9,8},{10,9... | collective-permute-start | bytes 2752520 | tf_op jit(solution)/shard_map/ppermute | solution.py:19
  41.6 23.1 %collective-permute-start.7 = (bf16[256,1792]{1,0:T(8,128)(2,1)}, bf16[256,1792]{1,0:T(8,128)(2,1)S(1)}, u32[]{:S(2)}, u32[]{:S(2)}) collective-permute-start(bf16[256,1792]{1,0:T(8,128)(2,1)} %get-tuple-element.85), channel_id=1, source_target_pairs={{0,1},{1,2},{2,3},{3,0},{4,5},{5,6},{6,7},{7,4},{8,9},{9,10},{10,1... | collective-permute-start | bytes 2752520 | tf_op jit(solution)/shard_map/ppermute | solution.py:19
  84.7 9.0 %collective-permute-start.11 = (bf16[64,1664]{1,0:T(8,128)(2,1)S(1)}, bf16[64,1664]{1,0:T(8,128)(2,1)S(1)}, u32[]{:S(2)}, u32[]{:S(2)}) collective-permute-start(bf16[64,1664]{1,0:T(8,128)(2,1)S(1)} %get-tuple-element.97), channel_id=1, source_target_pairs={{0,1},{1,2},{2,3},{3,0},{4,5},{5,6},{6,7},{7,4},{8,9},{9,10},{10,1... | collective-permute-start | bytes 638984 | tf_op jit(solution)/shard_map/ppermute | solution.py:19
  84.8 8.9 %collective-permute-start.12 = (bf16[64,1664]{1,0:T(8,128)(2,1)S(1)}, bf16[64,1664]{1,0:T(8,128)(2,1)S(1)}, u32[]{:S(2)}, u32[]{:S(2)}) collective-permute-start(bf16[64,1664]{1,0:T(8,128)(2,1)S(1)} %get-tuple-element.98), channel_id=1, source_target_pairs={{0,2},{1,3},{2,0},{3,1},{4,6},{5,7},{6,4},{7,5},{8,10},{9,11},{10,... | collective-permute-start | bytes 638984 | tf_op jit(solution)/shard_map/ppermute | solution.py:19
  86.4 9.7 %collective-permute-start.13 = (bf16[64,1664]{1,0:T(8,128)(2,1)S(1)}, bf16[64,1664]{1,0:T(8,128)(2,1)S(1)}, u32[]{:S(2)}, u32[]{:S(2)}) collective-permute-start(bf16[64,1664]{1,0:T(8,128)(2,1)S(1)} %get-tuple-element.99), channel_id=1, source_target_pairs={{0,3},{1,0},{2,1},{3,2},{4,7},{5,4},{6,5},{7,6},{8,11},{9,8},{10,9... | collective-permute-start | bytes 638984 | tf_op jit(solution)/shard_map/ppermute | solution.py:19
  96.5 5.6 %collective-permute-start.16 = (bf16[64,768]{1,0:T(8,128)(2,1)S(1)}, bf16[64,768]{1,0:T(8,128)(2,1)S(1)}, u32[]{:S(2)}, u32[]{:S(2)}) collective-permute-start(bf16[64,768]{1,0:T(8,128)(2,1)S(1)} %fusion.1.h0), channel_id=1, source_target_pairs={{0,1},{1,2},{2,3},{3,0},{4,5},{5,6},{6,7},{7,4},{8,9},{9,10},{10,1... | collective-permute-start | bytes 294920 | tf_op jit(solution)/shard_map/ppermute | solution.py:19
  97.3 7.4 %collective-permute-start.15 = (bf16[64,768]{1,0:T(8,128)(2,1)S(1)}, bf16[64,768]{1,0:T(8,128)(2,1)S(1)}, u32[]{:S(2)}, u32[]{:S(2)}) collective-permute-start(bf16[64,768]{1,0:T(8,128)(2,1)S(1)} %fusion.1.h0), channel_id=1, source_target_pairs={{0,2},{1,3},{2,0},{3,1},{4,6},{5,7},{6,4},{7,5},{8,10},{9,11},{10,... | collective-permute-start | bytes 294920 | tf_op jit(solution)/shard_map/ppermute | solution.py:19
  105.7 21.3 %collective-permute-start.17 = (bf16[256,1792]{1,0:T(8,128)(2,1)S(1)}, bf16[256,1792]{1,0:T(8,128)(2,1)S(1)}, u32[]{:S(2)}, u32[]{:S(2)}) collective-permute-start(bf16[256,1792]{1,0:T(8,128)(2,1)S(1)} %copy-done.11), channel_id=1, source_target_pairs={{0,2},{1,3},{2,0},{3,1},{4,6},{5,7},{6,4},{7,5},{8,10},{9,11},{10,... | collective-permute-start | bytes 2752520 | tf_op jit(solution)/shard_map/ppermute | solution.py:19
  127.2 5.9 %collective-permute-start.18 = (bf16[16,1920]{1,0:T(8,128)(2,1)S(1)}, bf16[16,1920]{1,0:T(8,128)(2,1)S(1)}, u32[]{:S(2)}, u32[]{:S(2)}) collective-permute-start(bf16[16,1920]{1,0:T(8,128)(2,1)S(1)} %get-tuple-element.110), channel_id=1, source_target_pairs={{0,4},{4,0},{1,5},{5,1},{2,6},{6,2},{3,7},{7,3},{8,12},{12,8},{9,1... | collective-permute-start | bytes 184328 | tf_op jit(solution)/shard_map/ppermute | solution.py:23
  130.2 5.3 %collective-permute-start.20 = (bf16[16,1920]{1,0:T(8,128)(2,1)S(1)}, bf16[16,1920]{1,0:T(8,128)(2,1)S(1)}, u32[]{:S(2)}, u32[]{:S(2)}) collective-permute-start(bf16[16,1920]{1,0:T(8,128)(2,1)S(1)} %get-tuple-element.110), channel_id=1, source_target_pairs={{0,6},{1,7},{2,4},{3,5},{4,2},{5,3},{6,0},{7,1},{8,14},{9,15},{10,... | collective-permute-start | bytes 184328 | tf_op jit(solution)/shard_map/ppermute | solution.py:586
  152.7 16.9 %collective-permute-start.22 = (bf16[128,2816]{1,0:T(8,128)(2,1)S(1)}, bf16[128,2816]{1,0:T(8,128)(2,1)S(1)}, u32[]{:S(2)}, u32[]{:S(2)}) collective-permute-start(bf16[128,2816]{1,0:T(8,128)(2,1)S(1)} %bitcast.32), channel_id=1, source_target_pairs={{0,1},{1,2},{2,3},{3,0},{4,5},{5,6},{6,7},{7,4},{8,9},{9,10},{10,1... | collective-permute-start | bytes 2162696 | tf_op jit(solution)/shard_map/ppermute | solution.py:19
  152.7 16.9 %collective-permute-start.21 = (bf16[128,2816]{1,0:T(8,128)(2,1)S(1)}, bf16[128,2816]{1,0:T(8,128)(2,1)S(1)}, u32[]{:S(2)}, u32[]{:S(2)}) collective-permute-start(bf16[128,2816]{1,0:T(8,128)(2,1)S(1)} %bitcast.33), channel_id=1, source_target_pairs={{0,3},{1,0},{2,1},{3,2},{4,7},{5,4},{6,5},{7,6},{8,11},{9,8},{10,9... | collective-permute-start | bytes 2162696 | tf_op jit(solution)/shard_map/ppermute | solution.py:19
  173.3 4.7 %collective-permute-start.25 = (bf16[192,256]{1,0:T(8,128)(2,1)S(1)}, bf16[192,256]{1,0:T(8,128)(2,1)S(1)}, u32[]{:S(2)}, u32[]{:S(2)}) collective-permute-start(bf16[192,256]{1,0:T(8,128)(2,1)S(1)} %expert_in.1.refs_0_), channel_id=1, source_target_pairs={{0,1},{1,2},{2,3},{3,0},{4,5},{5,6},{6,7},{7,4},{8,9},{9,10},{10,1... | collective-permute-start | bytes 294920 | tf_op jit(solution)/shard_map/ppermute | solution.py:19
  173.4 6.2 %collective-permute-start.24 = (bf16[192,256]{1,0:T(8,128)(2,1)S(1)}, bf16[192,256]{1,0:T(8,128)(2,1)S(1)}, u32[]{:S(2)}, u32[]{:S(2)}) collective-permute-start(bf16[192,256]{1,0:T(8,128)(2,1)S(1)} %expert_in.1.refs_0_), channel_id=1, source_target_pairs={{0,2},{1,3},{2,0},{3,1},{4,6},{5,7},{6,4},{7,5},{8,10},{9,11},{10,... | collective-permute-start | bytes 294920 | tf_op jit(solution)/shard_map/ppermute | solution.py:19
  196.0 7.1 %collective-permute-start.26 = (f32[16,1792]{1,0:T(8,128)S(1)}, f32[16,1792]{1,0:T(8,128)S(1)}, u32[]{:S(2)}, u32[]{:S(2)}) collective-permute-start(f32[16,1792]{1,0:T(8,128)S(1)} %get-tuple-element.122), channel_id=1, source_target_pairs={{0,4},{4,0},{1,5},{5,1},{2,6},{6,2},{3,7},{7,3},{8,12},{12,8},{9,1... | collective-permute-start | bytes 344072 | tf_op jit(solution)/shard_map/ppermute | solution.py:23
  (20 other events, 303.3 us)

commit v7 on v6

--- a/solution.py
+++ b/solution.py
@@ -321,7 +321,7 @@
 
 def dense_in(z, x, gain, weights):
     depth, width = weights[0].shape
-    step = depth // 2
+    step = depth
     rows = x.shape[0]
     lanes = 4 * width + 128
     return pl.pallas_call(
@@ -342,7 +342,7 @@
             ],
         ),
         out_shape=[jax.ShapeDtypeStruct((rows // NZ, lanes), BF)] * NZ,
-        compiler_params=params(),
+        compiler_params=params(28),
         cost_estimate=pl.CostEstimate(flops=8 * rows * depth * width, bytes_accessed=2 * depth * (rows + 4 * width), transcendentals=0),
         name="dense_in",
     )(z, x, gain, *weights)
@@ -353,64 +353,52 @@
 
 
 def expert_in_kernel(z_ref, *refs):
-    heads, tails, sums, gates, ups = (refs[4 * j : 4 * j + 4] for j in range(5))
-    out, gate_acc, up_acc = refs[20:]
-    step = pl.program_id(0)
-
-    @pl.when(step == 0)
-    def _():
-        gate_acc[...] = jnp.zeros_like(gate_acc)
-        up_acc[...] = jnp.zeros_like(up_acc)
-
-    rows = heads[0].shape[0]
+    xs, gates, ups, out = refs[:4], refs[4:8], refs[8:12], refs[12]
+    rows = xs[0].shape[0]
+    depth = gates[0].shape[0]
+    half = depth // 2
     row, col = grid_of((rows // 2, rows))
-    pick = onehot(col == 2 * row + step)
+    picks = [onehot(col == 2 * row + i) for i in range(2)]
+    lane = lax.broadcasted_iota(jnp.int32, (1, 128), 1)
+    gate, up, total = None, None, None
     for m in range(NZ):
-        x = jnp.concatenate([heads[m][...], exact(pick, tails[m][...])], axis=0)
-        gate_acc[...] += jnp.dot(x, gates[m][...], preferred_element_type=F32)
-        up_acc[...] += jnp.dot(x, ups[m][...], preferred_element_type=F32)
-
-    @pl.when(step == pl.num_programs(0) - 1)
-    def _():
-        lane = lax.broadcasted_iota(jnp.int32, (1, 128), 1)
-        total = None
-        for ref in sums:
-            square = jnp.concatenate(
-                [
-                    jnp.where(lane < 2, ref[...].astype(F32), 0.0),
-                    jnp.where((lane >= 2) & (lane < 4), jnp.dot(pick, ref[...], preferred_element_type=F32), 0.0),
-                ],
-                axis=0,
-            )
-            total = square if total is None else total + square
-        scale = lax.rsqrt(jnp.sum(total, axis=1, keepdims=True) / D + EPS)
-        out[...] = (silu(gate_acc[...] * scale) * (up_acc[...] * scale)).astype(BF)
+        head, rest = xs[m][:, :depth], xs[m][:, depth:]
+        even, odd = exact(picks[0], rest), exact(picks[1], rest[:, :half])
+        x = jnp.concatenate([head, jnp.concatenate([even[:, :half], odd], axis=1)], axis=0)
+        square = jnp.concatenate(
+            [
+                jnp.where(lane < 2, rest[:, half:].astype(F32), 0.0),
+                jnp.where((lane >= 2) & (lane < 4), even[:, half:].astype(F32), 0.0),
+            ],
+            axis=0,
+        )
+        one = jnp.dot(x, gates[m][...], preferred_element_type=F32)
+        two = jnp.dot(x, ups[m][...], preferred_element_type=F32)
+        gate = one if gate is None else gate + one
+        up = two if up is None else up + two
+        total = square if total is None else total + square
+    scale = lax.rsqrt(jnp.sum(total, axis=1, keepdims=True) / D + EPS)
+    out[...] = (silu(gate * scale) * (up * scale)).astype(BF)
 
 
 def expert_in(z, xs, gate, up):
     depth, width = gate.shape
-    steps = 2
-    step = depth // NZ // steps
-    rows = xs[0].shape[0]
-    heads = [pl.BlockSpec((rows, step), lambda i, z: (0, i))] * NZ
-    tails = [pl.BlockSpec((rows, step), lambda i, z: (0, 2))] * NZ
-    sums = [pl.BlockSpec((rows, 128), lambda i, z: (0, 3 * step // 128))] * NZ
-    ws = [pl.BlockSpec((step, width), lambda i, z, m=m: (lax.rem(z[0] + m, NZ) * steps + i, 0)) for m in range(NZ)]
+    rows, lanes = xs[0].shape
+    ws = [pl.BlockSpec((depth // NZ, width), lambda i, z, m=m: (lax.rem(z[0] + m, NZ), 0)) for m in range(NZ)]
     total = rows * 3 // 2
     return pl.pallas_call(
         expert_in_kernel,
         grid_spec=pltpu.PrefetchScalarGridSpec(
             num_scalar_prefetch=1,
-            grid=(steps,),
-            in_specs=heads + tails + sums + ws + ws,
+            grid=(1,),
+            in_specs=[pl.BlockSpec((rows, lanes), lambda i, z: (0, 0))] * NZ + ws + ws,
             out_specs=pl.BlockSpec((total, width), lambda i, z: (0, 0)),
-            scratch_shapes=[pltpu.VMEM((total, width), F32)] * 2,
         ),
         out_shape=jax.ShapeDtypeStruct((total, width), BF),
-        compiler_params=params(),
+        compiler_params=params(28),
         cost_estimate=pl.CostEstimate(flops=4 * total * depth * width, bytes_accessed=4 * depth * width, transcendentals=0),
         name="expert_in",
-    )(z, *xs, *xs, *xs, *[gate] * 4, *[up] * 4)
+    )(z, *xs, *[gate] * 4, *[up] * 4)
 
 
 def expert_out_kernel(z_ref, *refs):
@@ -500,7 +488,7 @@
 
 def plane_dot(kernel, z, blocks, own, got, name):
     depth, columns = own.shape
-    step = columns // 2
+    step = columns
     weight = pl.BlockSpec((depth, step), lambda i, z: (0, i))
     return pl.pallas_call(
         kernel,

time: 204 us -> 202 us (level)
  Pallas kernels: 21.5 us -> 18.1 us
  transfers between devices with their start and end apart: 28 -> 28, of which waited for: 16 -> 18; matrix products, arithmetic and copies ran while one was open for 2% -> 2% of each run, Pallas kernels for 3% -> 2%
where the time goes in v7:
time: 202 us
  blocking collectives  95.1 us (47%)
  starting transfers between devices  45.9 us (23%)
  waiting for transfers between devices  36.8 us (18%)
  Pallas kernels  18.1 us (9%)
  local copies, waits for them, and re-layouts  4.35 us (2%)
    all_to_all x2, blocking collectives, plane_scatter(): return lax.all_to_all(rows.reshape(16, 16, -1), YX, 0, 0, tiled=True)  34.5 us
    all_to_all x2, blocking collectives, shards(): lax.all_to_all(rows.reshape(16, 8, -1), YX, 0, 0, tiled=True)  30 us
    ppermute x17, waiting for transfers between devices, zsend(): return lax.ppermute(values, 'z', [(i, (i + shift) % NZ) for i in range(NZ)])  28.4 us
    ppermute x17, starting transfers between devices, zsend(): return lax.ppermute(values, 'z', [(i, (i + shift) % NZ) for i in range(NZ)])  21.8 us
    all_to_all x1, blocking collectives, shards(): own = lax.all_to_all(spread, YX, 0, 0, tiled=True).reshape(256, -1)  17.1 us
    all_to_all x1, blocking collectives, shards(): lax.all_to_all(result.reshape(16, 8, -1), YX, 0, 0, tiled=True)  13.5 us
    ppermute x8, starting transfers between devices, swap_core(): return lax.ppermute(values, 'c', [(0, 1), (1, 0)])  13.5 us
    all_to_all x1, starting transfers between devices, shards(): moved = lax.all_to_all(latents.reshape(16, 32, -1), YX, 0, 0, tiled=True)  7.6 us
  transfers between devices with their start and end apart: 28, of which 18 were waited for; matrix products, arithmetic and copies ran while one was open for 2% of the time, Pallas kernels for 2%

profile of v7, /device:TPU:1, one launch (start us, length us, event | category | flops | bytes accessed | tf_op | source)
XLA Modules:
  0.0 201.8 jit_solution(9532679749252355889)
XLA Ops:
  0.0 6.2 %attend.1 = bf16[512,512]{1,0:T(8,128)(2,1)} custom-call(s32[4]{0:T(128)} %len_ref.1, s32[1]{0:T(128)} %bitcast.1.c_ref, bf16[4,576,128]{2,1,0:T(8,128)(2,1)} %bitcast.47, bf16[4,576,512]{2,1,0:T(8,128)(2,1)} %bitcast.45, bf16[4,576]{1,0:T(4,128)(2,1)} %new_ref.1), custom_call_target="tpu_custom_call" | custom-call | flops 603979776 | bytes 2359296 | tf_op jit(solution)/shard_map/attend/pallas_call | solution.py:97
  6.2 7.6 %all-to-all-start = ((bf16[16,32,512]{2,1,0:T(8,128)(2,1)}), bf16[16,32,512]{2,1,0:T(8,128)(2,1)S(1)}, u32[]{:S(2)}, u32[]{:S(2)}) async-start(bf16[16,32,512]{2,1,0:T(8,128)(2,1)} %bitcast.46), calls=%async_computation | async-start | bytes 1048576 | tf_op jit(solution)/shard_map/all_to_all | solution.py:543
  15.2 3.4 %dynamic-slice_bitcast_fusion = (bf16[256,1792]{1,0:T(8,128)(2,1)}, bf16[256,1792]{1,0:T(8,128)(2,1)}, bf16[256,1792]{1,0:T(8,128)(2,1)}) fusion(bf16[1,256,7168]{2,1,0:T(8,128)(2,1)} %param.33, s32[]{:T(128)S(6)} %select_n.11, s32[]{:T(128)S(6)} %select_n.10, s32[]{:T(128)S(6)} %select_n.9), kind=kLoop, calls=%fused_computation | loop fusion | bytes 5505036 | tf_op jit(solution)/shard_map/dynamic_slice | solution.py:521
  19.9 4.5 %all-to-all-done = bf16[16,32,512]{2,1,0:T(8,128)(2,1)S(1)} async-done(((bf16[16,32,512]{2,1,0:T(8,128)(2,1)}), bf16[16,32,512]{2,1,0:T(8,128)(2,1)S(1)}, u32[]{:S(2)}, u32[]{:S(2)}) %all-to-all-start) | async-done | bytes 524320 | tf_op jit(solution)/shard_map/all_to_all | solution.py:543
  28.6 3.3 %collective-permute-start.3 = (bf16[64,1024]{1,0:T(8,128)(2,1)S(1)}, bf16[64,1024]{1,0:T(8,128)(2,1)S(1)}, u32[]{:S(2)}, u32[]{:S(2)}) collective-permute-start(bf16[64,1024]{1,0:T(8,128)(2,1)S(1)} %head_values.1.h0), channel_id=1, source_target_pairs={{0,2},{1,3},{2,0},{3,1},{4,6},{5,7},{6,4},{7,5},{8,10},{9,11},{10,... | collective-permute-start | bytes 393224 | tf_op jit(solution)/shard_map/ppermute | solution.py:19
  34.6 3.8 %collective-permute-done.3.h2 = bf16[64,1024]{1,0:T(8,128)(2,1)S(1)} collective-permute-done((bf16[64,1024]{1,0:T(8,128)(2,1)S(1)}, bf16[64,1024]{1,0:T(8,128)(2,1)S(1)}, u32[]{:S(2)}, u32[]{:S(2)}) %collective-permute-start.3) | collective-permute-done | bytes 131104 | tf_op jit(solution)/shard_map/ppermute | solution.py:19
  43.5 17.9 %all_to_all.35.parts = bf16[16,16,1792]{2,1,0:T(8,128)(2,1)S(1)} all-to-all(bf16[16,16,1792]{2,1,0:T(8,128)(2,1)S(1)} %bitcast.35), channel_id=1, replica_groups=mesh['y'=4,'x'=4,'c'=2,'z'=4] {'y','x'}, dimensions={0} | all-to-all | bytes 1835008 | tf_op jit(solution)/shard_map/all_to_all | solution.py:39
  61.8 2.8 %collective-permute-done.7.refs_7_ = bf16[256,1792]{1,0:T(8,128)(2,1)S(1)} collective-permute-done((bf16[256,1792]{1,0:T(8,128)(2,1)}, bf16[256,1792]{1,0:T(8,128)(2,1)S(1)}, u32[]{:S(2)}, u32[]{:S(2)}) %collective-permute-start.7) | collective-permute-done | bytes 917536 | tf_op jit(solution)/shard_map/ppermute | solution.py:19
  64.8 17.1 %all_to_all.36 = bf16[16,16,1792]{2,1,0:T(8,128)(2,1)S(1)} all-to-all(bf16[16,16,1792]{2,1,0:T(8,128)(2,1)S(1)} %get-tuple-element.92), channel_id=1, replica_groups=mesh['y'=4,'x'=4,'c'=2,'z'=4] {'y','x'}, dimensions={0} | all-to-all | bytes 1835008 | tf_op jit(solution)/shard_map/all_to_all | solution.py:558
  86.9 4.5 %collective-permute-done.11 = bf16[64,1664]{1,0:T(8,128)(2,1)S(1)} collective-permute-done((bf16[64,1664]{1,0:T(8,128)(2,1)S(1)}, bf16[64,1664]{1,0:T(8,128)(2,1)S(1)}, u32[]{:S(2)}, u32[]{:S(2)}) %collective-permute-start.11) | collective-permute-done | bytes 213024 | tf_op jit(solution)/shard_map/ppermute | solution.py:19
  91.4 2.5 %collective-permute-done.12 = bf16[64,1664]{1,0:T(8,128)(2,1)S(1)} collective-permute-done((bf16[64,1664]{1,0:T(8,128)(2,1)S(1)}, bf16[64,1664]{1,0:T(8,128)(2,1)S(1)}, u32[]{:S(2)}, u32[]{:S(2)}) %collective-permute-start.12) | collective-permute-done | bytes 213024 | tf_op jit(solution)/shard_map/ppermute | solution.py:19
  97.0 4.0 %collective-permute-start.15 = (bf16[64,768]{1,0:T(8,128)(2,1)S(1)}, bf16[64,768]{1,0:T(8,128)(2,1)S(1)}, u32[]{:S(2)}, u32[]{:S(2)}) collective-permute-start(bf16[64,768]{1,0:T(8,128)(2,1)S(1)} %fusion.1.h0), channel_id=1, source_target_pairs={{0,2},{1,3},{2,0},{3,1},{4,6},{5,7},{6,4},{7,5},{8,10},{9,11},{10,... | collective-permute-start | bytes 294920 | tf_op jit(solution)/shard_map/ppermute | solution.py:19
  101.9 2.6 %collective-permute-done.15.h2 = bf16[64,768]{1,0:T(8,128)(2,1)S(1)} collective-permute-done((bf16[64,768]{1,0:T(8,128)(2,1)S(1)}, bf16[64,768]{1,0:T(8,128)(2,1)S(1)}, u32[]{:S(2)}, u32[]{:S(2)}) %collective-permute-start.15) | collective-permute-done | bytes 98336 | tf_op jit(solution)/shard_map/ppermute | solution.py:19
  107.2 16.6 %all_to_all.37.parts = bf16[16,16,1792]{2,1,0:T(8,128)(2,1)S(1)} all-to-all(bf16[16,16,1792]{2,1,0:T(8,128)(2,1)S(1)} %bitcast.33), channel_id=1, replica_groups=mesh['y'=4,'x'=4,'c'=2,'z'=4] {'y','x'}, dimensions={0} | all-to-all | bytes 1835008 | tf_op jit(solution)/shard_map/all_to_all | solution.py:39
  123.8 2.9 %collective-permute-done.17.refs_6_ = bf16[256,1792]{1,0:T(8,128)(2,1)S(1)} collective-permute-done((bf16[256,1792]{1,0:T(8,128)(2,1)S(1)}, bf16[256,1792]{1,0:T(8,128)(2,1)S(1)}, u32[]{:S(2)}, u32[]{:S(2)}) %collective-permute-start.17) | collective-permute-done | bytes 917536 | tf_op jit(solution)/shard_map/ppermute | solution.py:19
  126.9 3.0 %collective-permute-start.18 = (bf16[16,1920]{1,0:T(8,128)(2,1)S(1)}, bf16[16,1920]{1,0:T(8,128)(2,1)S(1)}, u32[]{:S(2)}, u32[]{:S(2)}) collective-permute-start(bf16[16,1920]{1,0:T(8,128)(2,1)S(1)} %get-tuple-element.110), channel_id=1, source_target_pairs={{0,4},{4,0},{1,5},{5,1},{2,6},{6,2},{3,7},{7,3},{8,12},{12,8},{9,1... | collective-permute-start | bytes 184328 | tf_op jit(solution)/shard_map/ppermute | solution.py:23
  130.6 2.3 %collective-permute-start.19 = (bf16[16,1920]{1,0:T(8,128)(2,1)S(1)}, bf16[16,1920]{1,0:T(8,128)(2,1)S(1)}, u32[]{:S(2)}, u32[]{:S(2)}) collective-permute-start(bf16[16,1920]{1,0:T(8,128)(2,1)S(1)} %get-tuple-element.110), channel_id=1, source_target_pairs={{0,2},{1,3},{2,0},{3,1},{4,6},{5,7},{6,4},{7,5},{8,10},{9,11},{10,... | collective-permute-start | bytes 184328 | tf_op jit(solution)/shard_map/ppermute | solution.py:574
  133.3 2.4 %collective-permute-done.20 = bf16[16,1920]{1,0:T(8,128)(2,1)S(1)} collective-permute-done((bf16[16,1920]{1,0:T(8,128)(2,1)S(1)}, bf16[16,1920]{1,0:T(8,128)(2,1)S(1)}, u32[]{:S(2)}, u32[]{:S(2)}) %collective-permute-start.20) | collective-permute-done | bytes 61472 | tf_op jit(solution)/shard_map/ppermute | solution.py:574
  136.2 16.2 %all_to_all.38 = bf16[16,8,2816]{2,1,0:T(8,128)(2,1)S(1)} all-to-all(bf16[16,8,2816]{2,1,0:T(8,128)(2,1)S(1)} %bitcast.36), channel_id=1, replica_groups=mesh['y'=4,'x'=4,'c'=2,'z'=4] {'y','x'}, dimensions={0} | all-to-all | bytes 1441792 | tf_op jit(solution)/shard_map/all_to_all | solution.py:579
  152.4 2.7 %collective-permute-start.21 = (bf16[128,2816]{1,0:T(8,128)(2,1)S(1)}, bf16[128,2816]{1,0:T(8,128)(2,1)S(1)}, u32[]{:S(2)}, u32[]{:S(2)}) collective-permute-start(bf16[128,2816]{1,0:T(8,128)(2,1)S(1)} %bitcast.39), channel_id=1, source_target_pairs={{0,3},{1,0},{2,1},{3,2},{4,7},{5,4},{6,5},{7,6},{8,11},{9,8},{10,9... | collective-permute-start | bytes 2162696 | tf_op jit(solution)/shard_map/ppermute | solution.py:19
  155.5 13.8 %all_to_all.39 = bf16[16,8,2816]{2,1,0:T(8,128)(2,1)S(1)} all-to-all(bf16[16,8,2816]{2,1,0:T(8,128)(2,1)S(1)} %bitcast.37), channel_id=1, replica_groups=mesh['y'=4,'x'=4,'c'=2,'z'=4] {'y','x'}, dimensions={0} | all-to-all | bytes 1441792 | tf_op jit(solution)/shard_map/all_to_all | solution.py:579
  171.4 3.1 %collective-permute-start.24 = (bf16[192,256]{1,0:T(8,128)(2,1)S(1)}, bf16[192,256]{1,0:T(8,128)(2,1)S(1)}, u32[]{:S(2)}, u32[]{:S(2)}) collective-permute-start(bf16[192,256]{1,0:T(8,128)(2,1)S(1)} %expert_in.1.refs_0_), channel_id=1, source_target_pairs={{0,2},{1,3},{2,0},{3,1},{4,6},{5,7},{6,4},{7,5},{8,10},{9,11},{10,... | collective-permute-start | bytes 294920 | tf_op jit(solution)/shard_map/ppermute | solution.py:19
  180.1 13.5 %all_to_all.40 = bf16[16,8,2688]{2,1,0:T(8,128)(2,1)S(1)} all-to-all(bf16[16,8,2688]{2,1,0:T(8,128)(2,1)S(1)} %bitcast.43), channel_id=1, replica_groups=mesh['y'=4,'x'=4,'c'=2,'z'=4] {'y','x'}, dimensions={0} | all-to-all | bytes 1376256 | tf_op jit(solution)/shard_map/all_to_all | solution.py:587
  194.0 6.2 %collective-permute-start.26 = (f32[16,1792]{1,0:T(8,128)S(1)}, f32[16,1792]{1,0:T(8,128)S(1)}, u32[]{:S(2)}, u32[]{:S(2)}) collective-permute-start(f32[16,1792]{1,0:T(8,128)S(1)} %get-tuple-element.122), channel_id=1, source_target_pairs={{0,4},{4,0},{1,5},{5,1},{2,6},{6,2},{3,7},{7,3},{8,12},{12,8},{9,1... | collective-permute-start | bytes 344072 | tf_op jit(solution)/shard_map/ppermute | solution.py:23
  (97 shorter events, 38.6 us)
Async XLA Ops:
  6.2 18.1 %all-to-all-start = ((bf16[16,32,512]{2,1,0:T(8,128)(2,1)}), bf16[16,32,512]{2,1,0:T(8,128)(2,1)S(1)}, u32[]{:S(2)}, u32[]{:S(2)}) async-start(bf16[16,32,512]{2,1,0:T(8,128)(2,1)} %bitcast.46), calls=%async_computation | async-start | bytes 1048576 | tf_op jit(solution)/shard_map/all_to_all | solution.py:543
  13.8 10.5 %collective-permute-start = (bf16[4,512,128]{2,1,0:T(8,128)(2,1)S(1)}, bf16[4,512,128]{2,1,0:T(8,128)(2,1)S(1)}, u32[]{:S(2)}, u32[]{:S(2)}) collective-permute-start(bf16[4,512,128]{2,1,0:T(8,128)(2,1)S(1)} %copy-done.7), channel_id=1, source_target_pairs={{0,4},{4,0},{1,5},{5,1},{2,6},{6,2},{3,7},{7,3},{8,12},{12,8},{9,1... | collective-permute-start | bytes 1572872 | tf_op jit(solution)/shard_map/ppermute | solution.py:23
  24.3 14.1 %collective-permute-start.5 = (bf16[512,1792]{1,0:T(8,128)(2,1)S(1)}, bf16[512,1792]{1,0:T(8,128)(2,1)S(1)}, u32[]{:S(2)}, u32[]{:S(2)}) collective-permute-start(bf16[512,1792]{1,0:T(8,128)(2,1)S(1)} %copy-done.3), channel_id=1, source_target_pairs={{0,4},{4,0},{1,5},{5,1},{2,6},{6,2},{3,7},{7,3},{8,12},{12,8},{9,1... | collective-permute-start | bytes 5505032 | tf_op jit(solution)/shard_map/ppermute | solution.py:23
  26.9 7.7 %collective-permute-start.4 = (bf16[64,1024]{1,0:T(8,128)(2,1)S(1)}, bf16[64,1024]{1,0:T(8,128)(2,1)S(1)}, u32[]{:S(2)}, u32[]{:S(2)}) collective-permute-start(bf16[64,1024]{1,0:T(8,128)(2,1)S(1)} %head_values.1.h0), channel_id=1, source_target_pairs={{0,1},{1,2},{2,3},{3,0},{4,5},{5,6},{6,7},{7,4},{8,9},{9,10},{10,1... | collective-permute-start | bytes 393224 | tf_op jit(solution)/shard_map/ppermute | solution.py:19
  28.6 9.8 %collective-permute-start.3 = (bf16[64,1024]{1,0:T(8,128)(2,1)S(1)}, bf16[64,1024]{1,0:T(8,128)(2,1)S(1)}, u32[]{:S(2)}, u32[]{:S(2)}) collective-permute-start(bf16[64,1024]{1,0:T(8,128)(2,1)S(1)} %head_values.1.h0), channel_id=1, source_target_pairs={{0,2},{1,3},{2,0},{3,1},{4,6},{5,7},{6,4},{7,5},{8,10},{9,11},{10,... | collective-permute-start | bytes 393224 | tf_op jit(solution)/shard_map/ppermute | solution.py:19
  31.9 6.5 %collective-permute-start.2 = (bf16[64,1024]{1,0:T(8,128)(2,1)S(1)}, bf16[64,1024]{1,0:T(8,128)(2,1)S(1)}, u32[]{:S(2)}, u32[]{:S(2)}) collective-permute-start(bf16[64,1024]{1,0:T(8,128)(2,1)S(1)} %head_values.1.h0), channel_id=1, source_target_pairs={{0,3},{1,0},{2,1},{3,2},{4,7},{5,4},{6,5},{7,6},{8,11},{9,8},{10,9... | collective-permute-start | bytes 393224 | tf_op jit(solution)/shard_map/ppermute | solution.py:19
  38.4 26.3 %collective-permute-start.8 = (bf16[1792,384]{1,0:T(8,128)(2,1)}, bf16[1792,384]{1,0:T(8,128)(2,1)S(1)}, u32[]{:S(2)}, u32[]{:S(2)}) collective-permute-start(bf16[1792,384]{1,0:T(8,128)(2,1)} %gate.1), channel_id=1, source_target_pairs={{0,4},{4,0},{1,5},{5,1},{2,6},{6,2},{3,7},{7,3},{8,12},{12,8},{9,1... | collective-permute-start | bytes 4128776 | tf_op jit(solution)/shard_map/ppermute | solution.py:23
  39.2 25.5 %collective-permute-start.9 = (bf16[1792,384]{1,0:T(8,128)(2,1)}, bf16[1792,384]{1,0:T(8,128)(2,1)S(1)}, u32[]{:S(2)}, u32[]{:S(2)}) collective-permute-start(bf16[1792,384]{1,0:T(8,128)(2,1)} %up.1), channel_id=1, source_target_pairs={{0,4},{4,0},{1,5},{5,1},{2,6},{6,2},{3,7},{7,3},{8,12},{12,8},{9,1... | collective-permute-start | bytes 4128776 | tf_op jit(solution)/shard_map/ppermute | solution.py:23
  39.3 25.4 %collective-permute-start.10 = (bf16[384,1792]{1,0:T(8,128)(2,1)}, bf16[384,1792]{1,0:T(8,128)(2,1)S(1)}, u32[]{:S(2)}, u32[]{:S(2)}) collective-permute-start(bf16[384,1792]{1,0:T(8,128)(2,1)} %own.5), channel_id=1, source_target_pairs={{0,4},{4,0},{1,5},{5,1},{2,6},{6,2},{3,7},{7,3},{8,12},{12,8},{9,1... | collective-permute-start | bytes 4128776 | tf_op jit(solution)/shard_map/ppermute | solution.py:23
  39.7 22.1 %collective-permute-start.6 = (bf16[256,1792]{1,0:T(8,128)(2,1)}, bf16[256,1792]{1,0:T(8,128)(2,1)S(1)}, u32[]{:S(2)}, u32[]{:S(2)}) collective-permute-start(bf16[256,1792]{1,0:T(8,128)(2,1)} %get-tuple-element.84), channel_id=1, source_target_pairs={{0,3},{1,0},{2,1},{3,2},{4,7},{5,4},{6,5},{7,6},{8,11},{9,8},{10,9... | collective-permute-start | bytes 2752520 | tf_op jit(solution)/shard_map/ppermute | solution.py:19
  41.6 23.1 %collective-permute-start.7 = (bf16[256,1792]{1,0:T(8,128)(2,1)}, bf16[256,1792]{1,0:T(8,128)(2,1)S(1)}, u32[]{:S(2)}, u32[]{:S(2)}) collective-permute-start(bf16[256,1792]{1,0:T(8,128)(2,1)} %get-tuple-element.85), channel_id=1, source_target_pairs={{0,1},{1,2},{2,3},{3,0},{4,5},{5,6},{6,7},{7,4},{8,9},{9,10},{10,1... | collective-permute-start | bytes 2752520 | tf_op jit(solution)/shard_map/ppermute | solution.py:19
  84.2 7.2 %collective-permute-start.11 = (bf16[64,1664]{1,0:T(8,128)(2,1)S(1)}, bf16[64,1664]{1,0:T(8,128)(2,1)S(1)}, u32[]{:S(2)}, u32[]{:S(2)}) collective-permute-start(bf16[64,1664]{1,0:T(8,128)(2,1)S(1)} %get-tuple-element.97), channel_id=1, source_target_pairs={{0,1},{1,2},{2,3},{3,0},{4,5},{5,6},{6,7},{7,4},{8,9},{9,10},{10,1... | collective-permute-start | bytes 638984 | tf_op jit(solution)/shard_map/ppermute | solution.py:19
  84.3 9.7 %collective-permute-start.12 = (bf16[64,1664]{1,0:T(8,128)(2,1)S(1)}, bf16[64,1664]{1,0:T(8,128)(2,1)S(1)}, u32[]{:S(2)}, u32[]{:S(2)}) collective-permute-start(bf16[64,1664]{1,0:T(8,128)(2,1)S(1)} %get-tuple-element.98), channel_id=1, source_target_pairs={{0,2},{1,3},{2,0},{3,1},{4,6},{5,7},{6,4},{7,5},{8,10},{9,11},{10,... | collective-permute-start | bytes 638984 | tf_op jit(solution)/shard_map/ppermute | solution.py:19
  86.3 9.3 %collective-permute-start.13 = (bf16[64,1664]{1,0:T(8,128)(2,1)S(1)}, bf16[64,1664]{1,0:T(8,128)(2,1)S(1)}, u32[]{:S(2)}, u32[]{:S(2)}) collective-permute-start(bf16[64,1664]{1,0:T(8,128)(2,1)S(1)} %get-tuple-element.99), channel_id=1, source_target_pairs={{0,3},{1,0},{2,1},{3,2},{4,7},{5,4},{6,5},{7,6},{8,11},{9,8},{10,9... | collective-permute-start | bytes 638984 | tf_op jit(solution)/shard_map/ppermute | solution.py:19
  96.0 5.8 %collective-permute-start.16 = (bf16[64,768]{1,0:T(8,128)(2,1)S(1)}, bf16[64,768]{1,0:T(8,128)(2,1)S(1)}, u32[]{:S(2)}, u32[]{:S(2)}) collective-permute-start(bf16[64,768]{1,0:T(8,128)(2,1)S(1)} %fusion.1.h0), channel_id=1, source_target_pairs={{0,1},{1,2},{2,3},{3,0},{4,5},{5,6},{6,7},{7,4},{8,9},{9,10},{10,1... | collective-permute-start | bytes 294920 | tf_op jit(solution)/shard_map/ppermute | solution.py:19
  97.0 7.4 %collective-permute-start.15 = (bf16[64,768]{1,0:T(8,128)(2,1)S(1)}, bf16[64,768]{1,0:T(8,128)(2,1)S(1)}, u32[]{:S(2)}, u32[]{:S(2)}) collective-permute-start(bf16[64,768]{1,0:T(8,128)(2,1)S(1)} %fusion.1.h0), channel_id=1, source_target_pairs={{0,2},{1,3},{2,0},{3,1},{4,6},{5,7},{6,4},{7,5},{8,10},{9,11},{10,... | collective-permute-start | bytes 294920 | tf_op jit(solution)/shard_map/ppermute | solution.py:19
  105.4 21.3 %collective-permute-start.17 = (bf16[256,1792]{1,0:T(8,128)(2,1)S(1)}, bf16[256,1792]{1,0:T(8,128)(2,1)S(1)}, u32[]{:S(2)}, u32[]{:S(2)}) collective-permute-start(bf16[256,1792]{1,0:T(8,128)(2,1)S(1)} %copy-done.11), channel_id=1, source_target_pairs={{0,2},{1,3},{2,0},{3,1},{4,6},{5,7},{6,4},{7,5},{8,10},{9,11},{10,... | collective-permute-start | bytes 2752520 | tf_op jit(solution)/shard_map/ppermute | solution.py:19
  126.9 5.9 %collective-permute-start.18 = (bf16[16,1920]{1,0:T(8,128)(2,1)S(1)}, bf16[16,1920]{1,0:T(8,128)(2,1)S(1)}, u32[]{:S(2)}, u32[]{:S(2)}) collective-permute-start(bf16[16,1920]{1,0:T(8,128)(2,1)S(1)} %get-tuple-element.110), channel_id=1, source_target_pairs={{0,4},{4,0},{1,5},{5,1},{2,6},{6,2},{3,7},{7,3},{8,12},{12,8},{9,1... | collective-permute-start | bytes 184328 | tf_op jit(solution)/shard_map/ppermute | solution.py:23
  129.9 5.8 %collective-permute-start.20 = (bf16[16,1920]{1,0:T(8,128)(2,1)S(1)}, bf16[16,1920]{1,0:T(8,128)(2,1)S(1)}, u32[]{:S(2)}, u32[]{:S(2)}) collective-permute-start(bf16[16,1920]{1,0:T(8,128)(2,1)S(1)} %get-tuple-element.110), channel_id=1, source_target_pairs={{0,6},{1,7},{2,4},{3,5},{4,2},{5,3},{6,0},{7,1},{8,14},{9,15},{10,... | collective-permute-start | bytes 184328 | tf_op jit(solution)/shard_map/ppermute | solution.py:574
  130.6 5.6 %collective-permute-start.19 = (bf16[16,1920]{1,0:T(8,128)(2,1)S(1)}, bf16[16,1920]{1,0:T(8,128)(2,1)S(1)}, u32[]{:S(2)}, u32[]{:S(2)}) collective-permute-start(bf16[16,1920]{1,0:T(8,128)(2,1)S(1)} %get-tuple-element.110), channel_id=1, source_target_pairs={{0,2},{1,3},{2,0},{3,1},{4,6},{5,7},{6,4},{7,5},{8,10},{9,11},{10,... | collective-permute-start | bytes 184328 | tf_op jit(solution)/shard_map/ppermute | solution.py:574
  152.4 16.9 %collective-permute-start.22 = (bf16[128,2816]{1,0:T(8,128)(2,1)S(1)}, bf16[128,2816]{1,0:T(8,128)(2,1)S(1)}, u32[]{:S(2)}, u32[]{:S(2)}) collective-permute-start(bf16[128,2816]{1,0:T(8,128)(2,1)S(1)} %bitcast.38), channel_id=1, source_target_pairs={{0,1},{1,2},{2,3},{3,0},{4,5},{5,6},{6,7},{7,4},{8,9},{9,10},{10,1... | collective-permute-start | bytes 2162696 | tf_op jit(solution)/shard_map/ppermute | solution.py:19
  152.4 16.9 %collective-permute-start.21 = (bf16[128,2816]{1,0:T(8,128)(2,1)S(1)}, bf16[128,2816]{1,0:T(8,128)(2,1)S(1)}, u32[]{:S(2)}, u32[]{:S(2)}) collective-permute-start(bf16[128,2816]{1,0:T(8,128)(2,1)S(1)} %bitcast.39), channel_id=1, source_target_pairs={{0,3},{1,0},{2,1},{3,2},{4,7},{5,4},{6,5},{7,6},{8,11},{9,8},{10,9... | collective-permute-start | bytes 2162696 | tf_op jit(solution)/shard_map/ppermute | solution.py:19
  171.4 6.2 %collective-permute-start.24 = (bf16[192,256]{1,0:T(8,128)(2,1)S(1)}, bf16[192,256]{1,0:T(8,128)(2,1)S(1)}, u32[]{:S(2)}, u32[]{:S(2)}) collective-permute-start(bf16[192,256]{1,0:T(8,128)(2,1)S(1)} %expert_in.1.refs_0_), channel_id=1, source_target_pairs={{0,2},{1,3},{2,0},{3,1},{4,6},{5,7},{6,4},{7,5},{8,10},{9,11},{10,... | collective-permute-start | bytes 294920 | tf_op jit(solution)/shard_map/ppermute | solution.py:19
  194.0 7.1 %collective-permute-start.26 = (f32[16,1792]{1,0:T(8,128)S(1)}, f32[16,1792]{1,0:T(8,128)S(1)}, u32[]{:S(2)}, u32[]{:S(2)}) collective-permute-start(f32[16,1792]{1,0:T(8,128)S(1)} %get-tuple-element.122), channel_id=1, source_target_pairs={{0,4},{4,0},{1,5},{5,1},{2,6},{6,2},{3,7},{7,3},{8,12},{12,8},{9,1... | collective-permute-start | bytes 344072 | tf_op jit(solution)/shard_map/ppermute | solution.py:23
  (20 other events, 303.7 us)

commit v8 on v7

--- a/solution.py
+++ b/solution.py
@@ -414,26 +414,29 @@
             wide[k, :rows] = hidden[k][:rows]
             wide[k, rows:] = exact(order, hidden[k][rows:])
 
-    half = weights[0].shape[1]
-    for n in range(0, half, 256):
-        tile = min(256, half - n)
+    width = weights[0].shape[1]
+    half = width // 2
+    even = (lax.broadcasted_iota(jnp.int32, (rows, 128), 0) & 1) == 0
+    for n in range(0, width, 256):
         total = None
         for k in range(NZ):
-            term = jnp.dot(wide[k], weights[k][:, n : n + tile], preferred_element_type=F32)
+            term = jnp.dot(wide[k], weights[k][:, n : n + 256], preferred_element_type=F32)
             total = term if total is None else total + term
         total = total.astype(BF)
-        out[:, pl.ds(pl.multiple_of(step * half + n, 128), tile)] = total[:rows]
-        lanes = slice(2 * half + n, 2 * half + n + tile)
-        mine = (lax.broadcasted_iota(jnp.int32, (rows, tile), 0) & 1) == step
-        out[:, lanes] = jnp.where(mine, total[rows:], out[:, lanes])
+        out[:, n : n + 256] = total[:rows]
+        for i in (0, 128):
+            lane = (n + i) % half
+            part = total[rows:, i : i + 128]
+            lanes = slice(width + lane, width + lane + 128)
+            out[:, lanes] = part if n + i < half else jnp.where(even, out[:, lanes], part)
 
 
 def expert_out(z, hidden, down, got):
     rows, width = hidden[0].shape
     columns = got[0].shape[1]
-    steps = 2
-    step = columns // steps
-    whole = (rows // 12 * 8, columns + step)
+    steps = 1
+    step = columns
+    whole = (rows // 12 * 8, columns + columns // 2)
     return pl.pallas_call(
         expert_out_kernel,
         grid_spec=pltpu.PrefetchScalarGridSpec(

time: 202 us -> 201 us (level)
  no operation moved by 1% of the time
where the time goes in v8:
time: 201 us
  blocking collectives  95.1 us (47%)
  starting transfers between devices  45.9 us (23%)
  waiting for transfers between devices  36.8 us (18%)
  Pallas kernels  17.3 us (9%)
  local copies, waits for them, and re-layouts  4.35 us (2%)
    all_to_all x2, blocking collectives, plane_scatter(): return lax.all_to_all(rows.reshape(16, 16, -1), YX, 0, 0, tiled=True)  34.5 us
    all_to_all x2, blocking collectives, shards(): lax.all_to_all(rows.reshape(16, 8, -1), YX, 0, 0, tiled=True)  30 us
    ppermute x17, waiting for transfers between devices, zsend(): return lax.ppermute(values, 'z', [(i, (i + shift) % NZ) for i in range(NZ)])  28.4 us
    ppermute x17, starting transfers between devices, zsend(): return lax.ppermute(values, 'z', [(i, (i + shift) % NZ) for i in range(NZ)])  21.8 us
    all_to_all x1, blocking collectives, shards(): own = lax.all_to_all(spread, YX, 0, 0, tiled=True).reshape(256, -1)  17.1 us
    all_to_all x1, blocking collectives, shards(): lax.all_to_all(result.reshape(16, 8, -1), YX, 0, 0, tiled=True)  13.5 us
    ppermute x8, starting transfers between devices, swap_core(): return lax.ppermute(values, 'c', [(0, 1), (1, 0)])  13.5 us
    all_to_all x1, starting transfers between devices, shards(): moved = lax.all_to_all(latents.reshape(16, 32, -1), YX, 0, 0, tiled=True)  7.6 us
  transfers between devices with their start and end apart: 28, of which 18 were waited for; matrix products, arithmetic and copies ran while one was open for 2% of the time, Pallas kernels for 2%

profile of v8, /device:TPU:1, one launch (start us, length us, event | category | flops | bytes accessed | tf_op | source)
XLA Modules:
  0.0 201.0 jit_solution(13000590255394746866)
XLA Ops:
  0.0 6.2 %attend.1 = bf16[512,512]{1,0:T(8,128)(2,1)} custom-call(s32[4]{0:T(128)} %len_ref.1, s32[1]{0:T(128)} %bitcast.1.c_ref, bf16[4,576,128]{2,1,0:T(8,128)(2,1)} %bitcast.47, bf16[4,576,512]{2,1,0:T(8,128)(2,1)} %bitcast.45, bf16[4,576]{1,0:T(4,128)(2,1)} %new_ref.1), custom_call_target="tpu_custom_call" | custom-call | flops 603979776 | bytes 2359296 | tf_op jit(solution)/shard_map/attend/pallas_call | solution.py:97
  6.2 7.6 %all-to-all-start = ((bf16[16,32,512]{2,1,0:T(8,128)(2,1)}), bf16[16,32,512]{2,1,0:T(8,128)(2,1)S(1)}, u32[]{:S(2)}, u32[]{:S(2)}) async-start(bf16[16,32,512]{2,1,0:T(8,128)(2,1)} %bitcast.46), calls=%async_computation | async-start | bytes 1048576 | tf_op jit(solution)/shard_map/all_to_all | solution.py:546
  15.2 3.4 %dynamic-slice_bitcast_fusion = (bf16[256,1792]{1,0:T(8,128)(2,1)}, bf16[256,1792]{1,0:T(8,128)(2,1)}, bf16[256,1792]{1,0:T(8,128)(2,1)}) fusion(bf16[1,256,7168]{2,1,0:T(8,128)(2,1)} %param.33, s32[]{:T(128)S(6)} %select_n.11, s32[]{:T(128)S(6)} %select_n.10, s32[]{:T(128)S(6)} %select_n.9), kind=kLoop, calls=%fused_computation | loop fusion | bytes 5505036 | tf_op jit(solution)/shard_map/dynamic_slice | solution.py:524
  19.9 4.5 %all-to-all-done = bf16[16,32,512]{2,1,0:T(8,128)(2,1)S(1)} async-done(((bf16[16,32,512]{2,1,0:T(8,128)(2,1)}), bf16[16,32,512]{2,1,0:T(8,128)(2,1)S(1)}, u32[]{:S(2)}, u32[]{:S(2)}) %all-to-all-start) | async-done | bytes 524320 | tf_op jit(solution)/shard_map/all_to_all | solution.py:546
  28.6 3.3 %collective-permute-start.3 = (bf16[64,1024]{1,0:T(8,128)(2,1)S(1)}, bf16[64,1024]{1,0:T(8,128)(2,1)S(1)}, u32[]{:S(2)}, u32[]{:S(2)}) collective-permute-start(bf16[64,1024]{1,0:T(8,128)(2,1)S(1)} %head_values.1.h0), channel_id=1, source_target_pairs={{0,2},{1,3},{2,0},{3,1},{4,6},{5,7},{6,4},{7,5},{8,10},{9,11},{10,... | collective-permute-start | bytes 393224 | tf_op jit(solution)/shard_map/ppermute | solution.py:19
  34.6 3.8 %collective-permute-done.3.h2 = bf16[64,1024]{1,0:T(8,128)(2,1)S(1)} collective-permute-done((bf16[64,1024]{1,0:T(8,128)(2,1)S(1)}, bf16[64,1024]{1,0:T(8,128)(2,1)S(1)}, u32[]{:S(2)}, u32[]{:S(2)}) %collective-permute-start.3) | collective-permute-done | bytes 131104 | tf_op jit(solution)/shard_map/ppermute | solution.py:19
  43.5 17.9 %all_to_all.35.parts = bf16[16,16,1792]{2,1,0:T(8,128)(2,1)S(1)} all-to-all(bf16[16,16,1792]{2,1,0:T(8,128)(2,1)S(1)} %bitcast.35), channel_id=1, replica_groups=mesh['y'=4,'x'=4,'c'=2,'z'=4] {'y','x'}, dimensions={0} | all-to-all | bytes 1835008 | tf_op jit(solution)/shard_map/all_to_all | solution.py:39
  61.8 2.8 %collective-permute-done.7.refs_7_ = bf16[256,1792]{1,0:T(8,128)(2,1)S(1)} collective-permute-done((bf16[256,1792]{1,0:T(8,128)(2,1)}, bf16[256,1792]{1,0:T(8,128)(2,1)S(1)}, u32[]{:S(2)}, u32[]{:S(2)}) %collective-permute-start.7) | collective-permute-done | bytes 917536 | tf_op jit(solution)/shard_map/ppermute | solution.py:19
  64.8 17.1 %all_to_all.36 = bf16[16,16,1792]{2,1,0:T(8,128)(2,1)S(1)} all-to-all(bf16[16,16,1792]{2,1,0:T(8,128)(2,1)S(1)} %get-tuple-element.92), channel_id=1, replica_groups=mesh['y'=4,'x'=4,'c'=2,'z'=4] {'y','x'}, dimensions={0} | all-to-all | bytes 1835008 | tf_op jit(solution)/shard_map/all_to_all | solution.py:561
  86.9 4.5 %collective-permute-done.11 = bf16[64,1664]{1,0:T(8,128)(2,1)S(1)} collective-permute-done((bf16[64,1664]{1,0:T(8,128)(2,1)S(1)}, bf16[64,1664]{1,0:T(8,128)(2,1)S(1)}, u32[]{:S(2)}, u32[]{:S(2)}) %collective-permute-start.11) | collective-permute-done | bytes 213024 | tf_op jit(solution)/shard_map/ppermute | solution.py:19
  91.4 2.5 %collective-permute-done.12 = bf16[64,1664]{1,0:T(8,128)(2,1)S(1)} collective-permute-done((bf16[64,1664]{1,0:T(8,128)(2,1)S(1)}, bf16[64,1664]{1,0:T(8,128)(2,1)S(1)}, u32[]{:S(2)}, u32[]{:S(2)}) %collective-permute-start.12) | collective-permute-done | bytes 213024 | tf_op jit(solution)/shard_map/ppermute | solution.py:19
  97.0 4.0 %collective-permute-start.15 = (bf16[64,768]{1,0:T(8,128)(2,1)S(1)}, bf16[64,768]{1,0:T(8,128)(2,1)S(1)}, u32[]{:S(2)}, u32[]{:S(2)}) collective-permute-start(bf16[64,768]{1,0:T(8,128)(2,1)S(1)} %fusion.1.h0), channel_id=1, source_target_pairs={{0,2},{1,3},{2,0},{3,1},{4,6},{5,7},{6,4},{7,5},{8,10},{9,11},{10,... | collective-permute-start | bytes 294920 | tf_op jit(solution)/shard_map/ppermute | solution.py:19
  101.9 2.6 %collective-permute-done.15.h2 = bf16[64,768]{1,0:T(8,128)(2,1)S(1)} collective-permute-done((bf16[64,768]{1,0:T(8,128)(2,1)S(1)}, bf16[64,768]{1,0:T(8,128)(2,1)S(1)}, u32[]{:S(2)}, u32[]{:S(2)}) %collective-permute-start.15) | collective-permute-done | bytes 98336 | tf_op jit(solution)/shard_map/ppermute | solution.py:19
  107.2 16.6 %all_to_all.37.parts = bf16[16,16,1792]{2,1,0:T(8,128)(2,1)S(1)} all-to-all(bf16[16,16,1792]{2,1,0:T(8,128)(2,1)S(1)} %bitcast.33), channel_id=1, replica_groups=mesh['y'=4,'x'=4,'c'=2,'z'=4] {'y','x'}, dimensions={0} | all-to-all | bytes 1835008 | tf_op jit(solution)/shard_map/all_to_all | solution.py:39
  123.8 2.9 %collective-permute-done.17.refs_6_ = bf16[256,1792]{1,0:T(8,128)(2,1)S(1)} collective-permute-done((bf16[256,1792]{1,0:T(8,128)(2,1)S(1)}, bf16[256,1792]{1,0:T(8,128)(2,1)S(1)}, u32[]{:S(2)}, u32[]{:S(2)}) %collective-permute-start.17) | collective-permute-done | bytes 917536 | tf_op jit(solution)/shard_map/ppermute | solution.py:19
  126.9 3.0 %collective-permute-start.18 = (bf16[16,1920]{1,0:T(8,128)(2,1)S(1)}, bf16[16,1920]{1,0:T(8,128)(2,1)S(1)}, u32[]{:S(2)}, u32[]{:S(2)}) collective-permute-start(bf16[16,1920]{1,0:T(8,128)(2,1)S(1)} %get-tuple-element.110), channel_id=1, source_target_pairs={{0,4},{4,0},{1,5},{5,1},{2,6},{6,2},{3,7},{7,3},{8,12},{12,8},{9,1... | collective-permute-start | bytes 184328 | tf_op jit(solution)/shard_map/ppermute | solution.py:23
  130.6 2.3 %collective-permute-start.19 = (bf16[16,1920]{1,0:T(8,128)(2,1)S(1)}, bf16[16,1920]{1,0:T(8,128)(2,1)S(1)}, u32[]{:S(2)}, u32[]{:S(2)}) collective-permute-start(bf16[16,1920]{1,0:T(8,128)(2,1)S(1)} %get-tuple-element.110), channel_id=1, source_target_pairs={{0,2},{1,3},{2,0},{3,1},{4,6},{5,7},{6,4},{7,5},{8,10},{9,11},{10,... | collective-permute-start | bytes 184328 | tf_op jit(solution)/shard_map/ppermute | solution.py:577
  133.3 2.4 %collective-permute-done.20 = bf16[16,1920]{1,0:T(8,128)(2,1)S(1)} collective-permute-done((bf16[16,1920]{1,0:T(8,128)(2,1)S(1)}, bf16[16,1920]{1,0:T(8,128)(2,1)S(1)}, u32[]{:S(2)}, u32[]{:S(2)}) %collective-permute-start.20) | collective-permute-done | bytes 61472 | tf_op jit(solution)/shard_map/ppermute | solution.py:577
  136.2 16.2 %all_to_all.38 = bf16[16,8,2816]{2,1,0:T(8,128)(2,1)S(1)} all-to-all(bf16[16,8,2816]{2,1,0:T(8,128)(2,1)S(1)} %bitcast.36), channel_id=1, replica_groups=mesh['y'=4,'x'=4,'c'=2,'z'=4] {'y','x'}, dimensions={0} | all-to-all | bytes 1441792 | tf_op jit(solution)/shard_map/all_to_all | solution.py:582
  152.4 2.7 %collective-permute-start.21 = (bf16[128,2816]{1,0:T(8,128)(2,1)S(1)}, bf16[128,2816]{1,0:T(8,128)(2,1)S(1)}, u32[]{:S(2)}, u32[]{:S(2)}) collective-permute-start(bf16[128,2816]{1,0:T(8,128)(2,1)S(1)} %bitcast.39), channel_id=1, source_target_pairs={{0,3},{1,0},{2,1},{3,2},{4,7},{5,4},{6,5},{7,6},{8,11},{9,8},{10,9... | collective-permute-start | bytes 2162696 | tf_op jit(solution)/shard_map/ppermute | solution.py:19
  155.5 13.8 %all_to_all.39 = bf16[16,8,2816]{2,1,0:T(8,128)(2,1)S(1)} all-to-all(bf16[16,8,2816]{2,1,0:T(8,128)(2,1)S(1)} %bitcast.37), channel_id=1, replica_groups=mesh['y'=4,'x'=4,'c'=2,'z'=4] {'y','x'}, dimensions={0} | all-to-all | bytes 1441792 | tf_op jit(solution)/shard_map/all_to_all | solution.py:582
  171.4 3.1 %collective-permute-start.24 = (bf16[192,256]{1,0:T(8,128)(2,1)S(1)}, bf16[192,256]{1,0:T(8,128)(2,1)S(1)}, u32[]{:S(2)}, u32[]{:S(2)}) collective-permute-start(bf16[192,256]{1,0:T(8,128)(2,1)S(1)} %expert_in.1.refs_0_), channel_id=1, source_target_pairs={{0,2},{1,3},{2,0},{3,1},{4,6},{5,7},{6,4},{7,5},{8,10},{9,11},{10,... | collective-permute-start | bytes 294920 | tf_op jit(solution)/shard_map/ppermute | solution.py:19
  179.3 13.5 %all_to_all.40 = bf16[16,8,2688]{2,1,0:T(8,128)(2,1)S(1)} all-to-all(bf16[16,8,2688]{2,1,0:T(8,128)(2,1)S(1)} %bitcast.43), channel_id=1, replica_groups=mesh['y'=4,'x'=4,'c'=2,'z'=4] {'y','x'}, dimensions={0} | all-to-all | bytes 1376256 | tf_op jit(solution)/shard_map/all_to_all | solution.py:590
  193.2 6.2 %collective-permute-start.26 = (f32[16,1792]{1,0:T(8,128)S(1)}, f32[16,1792]{1,0:T(8,128)S(1)}, u32[]{:S(2)}, u32[]{:S(2)}) collective-permute-start(f32[16,1792]{1,0:T(8,128)S(1)} %get-tuple-element.122), channel_id=1, source_target_pairs={{0,4},{4,0},{1,5},{5,1},{2,6},{6,2},{3,7},{7,3},{8,12},{12,8},{9,1... | collective-permute-start | bytes 344072 | tf_op jit(solution)/shard_map/ppermute | solution.py:23
  (97 shorter events, 37.8 us)
Async XLA Ops:
  6.2 18.1 %all-to-all-start = ((bf16[16,32,512]{2,1,0:T(8,128)(2,1)}), bf16[16,32,512]{2,1,0:T(8,128)(2,1)S(1)}, u32[]{:S(2)}, u32[]{:S(2)}) async-start(bf16[16,32,512]{2,1,0:T(8,128)(2,1)} %bitcast.46), calls=%async_computation | async-start | bytes 1048576 | tf_op jit(solution)/shard_map/all_to_all | solution.py:546
  13.8 10.5 %collective-permute-start = (bf16[4,512,128]{2,1,0:T(8,128)(2,1)S(1)}, bf16[4,512,128]{2,1,0:T(8,128)(2,1)S(1)}, u32[]{:S(2)}, u32[]{:S(2)}) collective-permute-start(bf16[4,512,128]{2,1,0:T(8,128)(2,1)S(1)} %copy-done.7), channel_id=1, source_target_pairs={{0,4},{4,0},{1,5},{5,1},{2,6},{6,2},{3,7},{7,3},{8,12},{12,8},{9,1... | collective-permute-start | bytes 1572872 | tf_op jit(solution)/shard_map/ppermute | solution.py:23
  24.3 14.1 %collective-permute-start.5 = (bf16[512,1792]{1,0:T(8,128)(2,1)S(1)}, bf16[512,1792]{1,0:T(8,128)(2,1)S(1)}, u32[]{:S(2)}, u32[]{:S(2)}) collective-permute-start(bf16[512,1792]{1,0:T(8,128)(2,1)S(1)} %copy-done.3), channel_id=1, source_target_pairs={{0,4},{4,0},{1,5},{5,1},{2,6},{6,2},{3,7},{7,3},{8,12},{12,8},{9,1... | collective-permute-start | bytes 5505032 | tf_op jit(solution)/shard_map/ppermute | solution.py:23
  26.9 7.7 %collective-permute-start.4 = (bf16[64,1024]{1,0:T(8,128)(2,1)S(1)}, bf16[64,1024]{1,0:T(8,128)(2,1)S(1)}, u32[]{:S(2)}, u32[]{:S(2)}) collective-permute-start(bf16[64,1024]{1,0:T(8,128)(2,1)S(1)} %head_values.1.h0), channel_id=1, source_target_pairs={{0,1},{1,2},{2,3},{3,0},{4,5},{5,6},{6,7},{7,4},{8,9},{9,10},{10,1... | collective-permute-start | bytes 393224 | tf_op jit(solution)/shard_map/ppermute | solution.py:19
  28.6 9.8 %collective-permute-start.3 = (bf16[64,1024]{1,0:T(8,128)(2,1)S(1)}, bf16[64,1024]{1,0:T(8,128)(2,1)S(1)}, u32[]{:S(2)}, u32[]{:S(2)}) collective-permute-start(bf16[64,1024]{1,0:T(8,128)(2,1)S(1)} %head_values.1.h0), channel_id=1, source_target_pairs={{0,2},{1,3},{2,0},{3,1},{4,6},{5,7},{6,4},{7,5},{8,10},{9,11},{10,... | collective-permute-start | bytes 393224 | tf_op jit(solution)/shard_map/ppermute | solution.py:19
  31.9 6.5 %collective-permute-start.2 = (bf16[64,1024]{1,0:T(8,128)(2,1)S(1)}, bf16[64,1024]{1,0:T(8,128)(2,1)S(1)}, u32[]{:S(2)}, u32[]{:S(2)}) collective-permute-start(bf16[64,1024]{1,0:T(8,128)(2,1)S(1)} %head_values.1.h0), channel_id=1, source_target_pairs={{0,3},{1,0},{2,1},{3,2},{4,7},{5,4},{6,5},{7,6},{8,11},{9,8},{10,9... | collective-permute-start | bytes 393224 | tf_op jit(solution)/shard_map/ppermute | solution.py:19
  38.4 26.3 %collective-permute-start.8 = (bf16[1792,384]{1,0:T(8,128)(2,1)}, bf16[1792,384]{1,0:T(8,128)(2,1)S(1)}, u32[]{:S(2)}, u32[]{:S(2)}) collective-permute-start(bf16[1792,384]{1,0:T(8,128)(2,1)} %gate.1), channel_id=1, source_target_pairs={{0,4},{4,0},{1,5},{5,1},{2,6},{6,2},{3,7},{7,3},{8,12},{12,8},{9,1... | collective-permute-start | bytes 4128776 | tf_op jit(solution)/shard_map/ppermute | solution.py:23
  39.2 25.5 %collective-permute-start.9 = (bf16[1792,384]{1,0:T(8,128)(2,1)}, bf16[1792,384]{1,0:T(8,128)(2,1)S(1)}, u32[]{:S(2)}, u32[]{:S(2)}) collective-permute-start(bf16[1792,384]{1,0:T(8,128)(2,1)} %up.1), channel_id=1, source_target_pairs={{0,4},{4,0},{1,5},{5,1},{2,6},{6,2},{3,7},{7,3},{8,12},{12,8},{9,1... | collective-permute-start | bytes 4128776 | tf_op jit(solution)/shard_map/ppermute | solution.py:23
  39.3 25.4 %collective-permute-start.10 = (bf16[384,1792]{1,0:T(8,128)(2,1)}, bf16[384,1792]{1,0:T(8,128)(2,1)S(1)}, u32[]{:S(2)}, u32[]{:S(2)}) collective-permute-start(bf16[384,1792]{1,0:T(8,128)(2,1)} %own.5), channel_id=1, source_target_pairs={{0,4},{4,0},{1,5},{5,1},{2,6},{6,2},{3,7},{7,3},{8,12},{12,8},{9,1... | collective-permute-start | bytes 4128776 | tf_op jit(solution)/shard_map/ppermute | solution.py:23
  39.7 22.1 %collective-permute-start.6 = (bf16[256,1792]{1,0:T(8,128)(2,1)}, bf16[256,1792]{1,0:T(8,128)(2,1)S(1)}, u32[]{:S(2)}, u32[]{:S(2)}) collective-permute-start(bf16[256,1792]{1,0:T(8,128)(2,1)} %get-tuple-element.84), channel_id=1, source_target_pairs={{0,3},{1,0},{2,1},{3,2},{4,7},{5,4},{6,5},{7,6},{8,11},{9,8},{10,9... | collective-permute-start | bytes 2752520 | tf_op jit(solution)/shard_map/ppermute | solution.py:19
  41.6 23.1 %collective-permute-start.7 = (bf16[256,1792]{1,0:T(8,128)(2,1)}, bf16[256,1792]{1,0:T(8,128)(2,1)S(1)}, u32[]{:S(2)}, u32[]{:S(2)}) collective-permute-start(bf16[256,1792]{1,0:T(8,128)(2,1)} %get-tuple-element.85), channel_id=1, source_target_pairs={{0,1},{1,2},{2,3},{3,0},{4,5},{5,6},{6,7},{7,4},{8,9},{9,10},{10,1... | collective-permute-start | bytes 2752520 | tf_op jit(solution)/shard_map/ppermute | solution.py:19
  84.2 7.2 %collective-permute-start.11 = (bf16[64,1664]{1,0:T(8,128)(2,1)S(1)}, bf16[64,1664]{1,0:T(8,128)(2,1)S(1)}, u32[]{:S(2)}, u32[]{:S(2)}) collective-permute-start(bf16[64,1664]{1,0:T(8,128)(2,1)S(1)} %get-tuple-element.97), channel_id=1, source_target_pairs={{0,1},{1,2},{2,3},{3,0},{4,5},{5,6},{6,7},{7,4},{8,9},{9,10},{10,1... | collective-permute-start | bytes 638984 | tf_op jit(solution)/shard_map/ppermute | solution.py:19
  84.3 9.7 %collective-permute-start.12 = (bf16[64,1664]{1,0:T(8,128)(2,1)S(1)}, bf16[64,1664]{1,0:T(8,128)(2,1)S(1)}, u32[]{:S(2)}, u32[]{:S(2)}) collective-permute-start(bf16[64,1664]{1,0:T(8,128)(2,1)S(1)} %get-tuple-element.98), channel_id=1, source_target_pairs={{0,2},{1,3},{2,0},{3,1},{4,6},{5,7},{6,4},{7,5},{8,10},{9,11},{10,... | collective-permute-start | bytes 638984 | tf_op jit(solution)/shard_map/ppermute | solution.py:19
  86.3 9.3 %collective-permute-start.13 = (bf16[64,1664]{1,0:T(8,128)(2,1)S(1)}, bf16[64,1664]{1,0:T(8,128)(2,1)S(1)}, u32[]{:S(2)}, u32[]{:S(2)}) collective-permute-start(bf16[64,1664]{1,0:T(8,128)(2,1)S(1)} %get-tuple-element.99), channel_id=1, source_target_pairs={{0,3},{1,0},{2,1},{3,2},{4,7},{5,4},{6,5},{7,6},{8,11},{9,8},{10,9... | collective-permute-start | bytes 638984 | tf_op jit(solution)/shard_map/ppermute | solution.py:19
  96.0 5.8 %collective-permute-start.16 = (bf16[64,768]{1,0:T(8,128)(2,1)S(1)}, bf16[64,768]{1,0:T(8,128)(2,1)S(1)}, u32[]{:S(2)}, u32[]{:S(2)}) collective-permute-start(bf16[64,768]{1,0:T(8,128)(2,1)S(1)} %fusion.1.h0), channel_id=1, source_target_pairs={{0,1},{1,2},{2,3},{3,0},{4,5},{5,6},{6,7},{7,4},{8,9},{9,10},{10,1... | collective-permute-start | bytes 294920 | tf_op jit(solution)/shard_map/ppermute | solution.py:19
  97.0 7.4 %collective-permute-start.15 = (bf16[64,768]{1,0:T(8,128)(2,1)S(1)}, bf16[64,768]{1,0:T(8,128)(2,1)S(1)}, u32[]{:S(2)}, u32[]{:S(2)}) collective-permute-start(bf16[64,768]{1,0:T(8,128)(2,1)S(1)} %fusion.1.h0), channel_id=1, source_target_pairs={{0,2},{1,3},{2,0},{3,1},{4,6},{5,7},{6,4},{7,5},{8,10},{9,11},{10,... | collective-permute-start | bytes 294920 | tf_op jit(solution)/shard_map/ppermute | solution.py:19
  105.4 21.3 %collective-permute-start.17 = (bf16[256,1792]{1,0:T(8,128)(2,1)S(1)}, bf16[256,1792]{1,0:T(8,128)(2,1)S(1)}, u32[]{:S(2)}, u32[]{:S(2)}) collective-permute-start(bf16[256,1792]{1,0:T(8,128)(2,1)S(1)} %copy-done.11), channel_id=1, source_target_pairs={{0,2},{1,3},{2,0},{3,1},{4,6},{5,7},{6,4},{7,5},{8,10},{9,11},{10,... | collective-permute-start | bytes 2752520 | tf_op jit(solution)/shard_map/ppermute | solution.py:19
  126.9 5.9 %collective-permute-start.18 = (bf16[16,1920]{1,0:T(8,128)(2,1)S(1)}, bf16[16,1920]{1,0:T(8,128)(2,1)S(1)}, u32[]{:S(2)}, u32[]{:S(2)}) collective-permute-start(bf16[16,1920]{1,0:T(8,128)(2,1)S(1)} %get-tuple-element.110), channel_id=1, source_target_pairs={{0,4},{4,0},{1,5},{5,1},{2,6},{6,2},{3,7},{7,3},{8,12},{12,8},{9,1... | collective-permute-start | bytes 184328 | tf_op jit(solution)/shard_map/ppermute | solution.py:23
  129.9 5.8 %collective-permute-start.20 = (bf16[16,1920]{1,0:T(8,128)(2,1)S(1)}, bf16[16,1920]{1,0:T(8,128)(2,1)S(1)}, u32[]{:S(2)}, u32[]{:S(2)}) collective-permute-start(bf16[16,1920]{1,0:T(8,128)(2,1)S(1)} %get-tuple-element.110), channel_id=1, source_target_pairs={{0,6},{1,7},{2,4},{3,5},{4,2},{5,3},{6,0},{7,1},{8,14},{9,15},{10,... | collective-permute-start | bytes 184328 | tf_op jit(solution)/shard_map/ppermute | solution.py:577
  130.6 5.6 %collective-permute-start.19 = (bf16[16,1920]{1,0:T(8,128)(2,1)S(1)}, bf16[16,1920]{1,0:T(8,128)(2,1)S(1)}, u32[]{:S(2)}, u32[]{:S(2)}) collective-permute-start(bf16[16,1920]{1,0:T(8,128)(2,1)S(1)} %get-tuple-element.110), channel_id=1, source_target_pairs={{0,2},{1,3},{2,0},{3,1},{4,6},{5,7},{6,4},{7,5},{8,10},{9,11},{10,... | collective-permute-start | bytes 184328 | tf_op jit(solution)/shard_map/ppermute | solution.py:577
  152.4 16.9 %collective-permute-start.22 = (bf16[128,2816]{1,0:T(8,128)(2,1)S(1)}, bf16[128,2816]{1,0:T(8,128)(2,1)S(1)}, u32[]{:S(2)}, u32[]{:S(2)}) collective-permute-start(bf16[128,2816]{1,0:T(8,128)(2,1)S(1)} %bitcast.38), channel_id=1, source_target_pairs={{0,1},{1,2},{2,3},{3,0},{4,5},{5,6},{6,7},{7,4},{8,9},{9,10},{10,1... | collective-permute-start | bytes 2162696 | tf_op jit(solution)/shard_map/ppermute | solution.py:19
  152.4 16.9 %collective-permute-start.21 = (bf16[128,2816]{1,0:T(8,128)(2,1)S(1)}, bf16[128,2816]{1,0:T(8,128)(2,1)S(1)}, u32[]{:S(2)}, u32[]{:S(2)}) collective-permute-start(bf16[128,2816]{1,0:T(8,128)(2,1)S(1)} %bitcast.39), channel_id=1, source_target_pairs={{0,3},{1,0},{2,1},{3,2},{4,7},{5,4},{6,5},{7,6},{8,11},{9,8},{10,9... | collective-permute-start | bytes 2162696 | tf_op jit(solution)/shard_map/ppermute | solution.py:19
  171.4 6.2 %collective-permute-start.24 = (bf16[192,256]{1,0:T(8,128)(2,1)S(1)}, bf16[192,256]{1,0:T(8,128)(2,1)S(1)}, u32[]{:S(2)}, u32[]{:S(2)}) collective-permute-start(bf16[192,256]{1,0:T(8,128)(2,1)S(1)} %expert_in.1.refs_0_), channel_id=1, source_target_pairs={{0,2},{1,3},{2,0},{3,1},{4,6},{5,7},{6,4},{7,5},{8,10},{9,11},{10,... | collective-permute-start | bytes 294920 | tf_op jit(solution)/shard_map/ppermute | solution.py:19
  193.2 7.1 %collective-permute-start.26 = (f32[16,1792]{1,0:T(8,128)S(1)}, f32[16,1792]{1,0:T(8,128)S(1)}, u32[]{:S(2)}, u32[]{:S(2)}) collective-permute-start(f32[16,1792]{1,0:T(8,128)S(1)} %get-tuple-element.122), channel_id=1, source_target_pairs={{0,4},{4,0},{1,5},{5,1},{2,6},{6,2},{3,7},{7,3},{8,12},{12,8},{9,1... | collective-permute-start | bytes 344072 | tf_op jit(solution)/shard_map/ppermute | solution.py:23
  (20 other events, 302.9 us)
